TPU v7x, 32 devices: a whole 2x2x4 slice. The times are simulated.
32 devices in a mesh: group: 2 (over x), ep: 16 (over z, y, core).
Axes of the slice: x: 2, y: 2, z: 4, core: 2. Of those that a mesh axis runs over, the one named last changes fastest.
Arguments:
- hidden: bfloat16 [4096, 2048], P(('group', 'ep')), parts along dimension 0, may hold values from -6 to 6
- norm_gain: float32 [2048], replicated, may hold values from 0.25 to 4
- routes: int32 [4096, 8], P(('group', 'ep')), parts along dimension 0, may hold values from 0 to 15, all different within a row; in each aligned block of 128 rows (0 to 127, 128 to 255, ...) at most 80 rows name the same one
- route_weight: float32 [4096, 8], P(('group', 'ep')), parts along dimension 0, may hold values from 0.05 to 1
- w_gate: bfloat16 [16, 2048, 768], P('ep'), may hold values from -0.125 to 0.125
- w_up: bfloat16 [16, 2048, 768], P('ep'), may hold values from -0.125 to 0.125
- w_down: bfloat16 [16, 768, 2048], P('ep'), may hold values from -0.21875 to 0.21875
Outputs:
- mixed: bfloat16 [4096, 2048], P(('group', 'ep')), parts along dimension 0
There are 2 independent parts, one for each index of `group`. A program takes and returns all parts, laid end to end along the dimension named above; an argument that names none is the same for every part. Nothing has to cross between parts.
Inputs may be any that keep to these rules, and one draw needn't show every extreme that they name: `routes`: each row names 8 different experts. Among the rows of one device no expert is named more than 80 times, a bound that some block reaches.
All inputs are finite; a program needn't handle non-finite values.
Results may differ from a plain program's by a relative error of at most 0.0085.
Values may be sent and summed in bfloat16 or wider, within the bound.
No kernel may reach another device: no remote copies, remote signals or barrier semaphores. Data moves between devices by JAX's collectives and lax.ppermute only.
A program may use at most 128 MiB of HBM per device.

v0:
```python
import jax
import jax.numpy as jnp
from jax import lax
from jax.sharding import PartitionSpec as P


def body(hidden, norm_gain, routes, route_weight, w_gate, w_up, w_down):
    count = lax.axis_size("ep")
    tok = hidden.shape[0]
    width = hidden.shape[1]
    picks = routes.shape[1]
    experts = count * w_gate.shape[0]
    slots = tok * picks * 5 // (4 * experts)
    xf = hidden.astype(jnp.float32)
    normed = (xf * lax.rsqrt(jnp.mean(xf * xf, axis=-1, keepdims=True) + 1e-06) * norm_gain).astype(
        jnp.bfloat16
    )
    share = route_weight / jnp.sum(route_weight, axis=1, keepdims=True)
    flat = routes.reshape(-1)
    onehot = (flat[:, None] == jnp.arange(experts, dtype=jnp.int32)[None, :]).astype(jnp.int32)
    ranked = jnp.cumsum(onehot, axis=0) - onehot
    slot = jnp.sum(ranked * onehot, axis=1)
    token_of = jnp.arange(tok * picks, dtype=jnp.int32) // picks
    outgoing = jnp.zeros((experts, slots, width), jnp.bfloat16).at[flat, slot].set(normed[token_of])
    arrived = lax.all_to_all(outgoing, "ep", split_axis=0, concat_axis=0, tiled=True)
    rows = arrived.reshape(-1, width)
    gate = jnp.dot(rows, w_gate[0], preferred_element_type=jnp.float32)
    upper = jnp.dot(rows, w_up[0], preferred_element_type=jnp.float32)
    units = (jax.nn.silu(gate) * upper).astype(jnp.bfloat16)
    result = jnp.dot(units, w_down[0], preferred_element_type=jnp.float32).astype(jnp.bfloat16)
    coming_back = lax.all_to_all(
        result.reshape(arrived.shape), "ep", split_axis=0, concat_axis=0, tiled=True
    )
    picked = coming_back[flat, slot]
    picked = picked.reshape(tok, picks, width).astype(jnp.float32)
    mixed = jnp.einsum("tk,tkd->td", share, picked)
    return mixed.astype(jnp.bfloat16)


def solution(mesh):
    in_specs = (
        P(("group", "ep"), None),
        P(),
        P(("group", "ep"), None),
        P(("group", "ep"), None),
        P("ep", None, None),
        P("ep", None, None),
        P("ep", None, None),
    )
    out_specs = P(("group", "ep"), None)
    return jax.shard_map(body, mesh=mesh, in_specs=in_specs, out_specs=out_specs, check_vma=False)
```

profile of v0, /device:TPU:18, one launch (start us, length us, event | category | flops | bytes accessed | tf_op | source)
XLA Modules:
  0.0 321.9 jit_solution(12659669588335324400)
XLA Ops:
  0.0 0.0 copy-start
  0.0 0.9 copy.10
  0.9 0.1 eq.29
  1.0 0.1 eq.25
  1.1 0.1 reshape.123
  1.3 4.5 %reduce-window.6 = s32[16,8,128]{2,1,0:T(8,128)S(1)} reduce-window(s32[16,8,128]{2,1,0:T(8,128)S(1)} %fusion.16, s32[]{:T(128)} %constant.31.clone.1), window={size=1x1x128 pad=0_0x0_0x127_0}, to_apply=%region_1.0 | reduce-window | flops 2080768 | bytes 131076 | tf_op jit(solution)/shard_map/reduce-window
  5.8 0.1 slice.12
  5.8 0.1 copy.13
  6.0 0.1 copy.14
  6.1 0.1 broadcast_add_fusion
  6.2 0.7 multiply_reduce_fusion
  7.0 0.8 and_reduce_fusion
  7.7 1.2 fusion.10
  9.0 2.0 fusion.12
  11.0 23.7 %scatter_custom_fusion = bf16[1280,2048]{1,0:T(8,128)(2,1)} fusion(s32[1024]{0:T(1024)S(1)} %get-tuple-element.9, bf16[128,2048]{1,0:T(8,128)(2,1)} %fusion.12, s32[1024]{0:T(1024)S(1)} %get-tuple-element.8, bf16[]{:T(256)} %constant.30.clone.1), kind=kCustom, calls=%fused_computation.6 | custom fusion | bytes 5243392
  34.7 0.0 copy-start.2
  34.7 121.6 %all_to_all.10 = bf16[16,80,2048]{2,1,0:T(8,128)(2,1)S(1)} all-to-all(bf16[16,80,2048]{2,1,0:T(8,128)(2,1)} %bitcast.46), channel_id=1, replica_groups=mesh['group'=2,'ep'=16] {'ep'}, dimensions={0} | all-to-all | bytes 10485760 | tf_op jit(solution)/shard_map/all_to_all | solution.py:25
  156.3 0.0 copy-done.2
  156.3 0.0 copy-start.3
  156.4 4.3 %fusion.7 = f32[1280,768]{1,0:T(8,128)S(1)} fusion(bf16[1280,2048]{1,0:T(8,128)(2,1)S(1)} %bitcast.48, bf16[1,2048,768]{2,1,0:T(8,128)(2,1)S(1)} %copy-done.2), kind=kOutput, calls=%fused_computation.12 | convolution fusion | flops 4026531840 | bytes 12320768 | tf_op jit(solution)/shard_map/dot_general | solution.py:27
  160.7 0.0 copy-done.3
  160.7 4.8 %fusion.4 = bf16[1280,768]{1,0:T(8,128)(2,1)S(1)} fusion(bf16[1280,2048]{1,0:T(8,128)(2,1)S(1)} %bitcast.49, f32[1280,768]{1,0:T(8,128)S(1)} %fusion.7, bf16[1,2048,768]{2,1,0:T(8,128)(2,1)S(1)} %copy-done.3), kind=kOutput, calls=%fused_computation.9 | convolution fusion | flops 4032430080 | bytes 14286848 | tf_op jit(solution)/shard_map/dot_general | solution.py:28
  165.5 0.0 copy-done
  165.5 6.1 %convolution_convert_fusion = bf16[1280,2048]{1,0:T(8,128)(2,1)} fusion(bf16[1280,768]{1,0:T(8,128)(2,1)S(1)} %fusion.4, bf16[1,768,2048]{2,1,0:T(8,128)(2,1)S(1)} %copy-done), kind=kOutput, calls=%fused_computation.3 | convolution fusion | flops 4029153280 | bytes 10354688 | tf_op jit(solution)/shard_map/dot_general | solution.py:30
  171.6 0.0 copy-start.1
  171.6 5.1 %all-to-all-start.1 = ((bf16[16,80,2048]{2,1,0:T(8,128)(2,1)}), bf16[16,80,2048]{2,1,0:T(8,128)(2,1)}, u32[]{:S(2)}, u32[]{:S(2)}) async-start(bf16[16,80,2048]{2,1,0:T(8,128)(2,1)} %bitcast.47), calls=%async_computation.1 | async-start | bytes 10485760 | tf_op jit(solution)/shard_map/all_to_all | solution.py:31
  176.7 0.0 copy-done.1
  176.7 0.1 copy.15
  176.8 115.0 %all-to-all-done.1 = bf16[16,80,2048]{2,1,0:T(8,128)(2,1)} async-done(((bf16[16,80,2048]{2,1,0:T(8,128)(2,1)}), bf16[16,80,2048]{2,1,0:T(8,128)(2,1)}, u32[]{:S(2)}, u32[]{:S(2)}) %all-to-all-start.1) | async-done | bytes 5242912 | tf_op jit(solution)/shard_map/all_to_all | solution.py:31
  291.8 25.6 %gather_fusion = bf16[1024,2048]{1,0:T(8,128)(2,1)} fusion(bf16[16,80,2048]{2,1,0:T(8,128)(2,1)} %all-to-all-done.1, s32[1024]{0:T(1024)S(1)} %bitcast.45), kind=kCustom, calls=%fused_computation.1 | custom fusion | bytes 8396800 | tf_op jit(solution)/shard_map/gather | solution.py:34
  317.4 3.4 %fusion = bf16[128,1,2048]{2,1,0:T(2,128)(2,1)S(1)} fusion(bf16[128,8,1]{1,2,0:T(2,128)(2,1)S(1)} %copy.15, bf16[1024,2048]{1,0:T(8,128)(2,1)} %gather_fusion), kind=kOutput, calls=%fused_computation.4 | convolution fusion | flops 4194304 | bytes 4720640 | tf_op jit(solution)/shard_map/tk,tkd->td/dot_general | solution.py:36
  320.8 1.1 copy.20
  (10 shorter events, 0.1 us)
Async XLA Ops:
  0.0 165.5 %copy-start = (bf16[1,768,2048]{2,1,0:T(8,128)(2,1)S(1)}, bf16[1,768,2048]{2,1,0:T(8,128)(2,1)}, u32[]{:S(2)}) copy-start(bf16[1,768,2048]{2,1,0:T(8,128)(2,1)} %param.13) | copy-start | bytes 9437188
  34.7 121.6 %copy-start.2 = (bf16[1,2048,768]{2,1,0:T(8,128)(2,1)S(1)}, bf16[1,2048,768]{2,1,0:T(8,128)(2,1)}, u32[]{:S(2)}) copy-start(bf16[1,2048,768]{2,1,0:T(8,128)(2,1)} %param.11) | copy-start | bytes 9437188
  156.3 4.3 %copy-start.3 = (bf16[1,2048,768]{2,1,0:T(8,128)(2,1)S(1)}, bf16[1,2048,768]{2,1,0:T(8,128)(2,1)}, u32[]{:S(2)}) copy-start(bf16[1,2048,768]{2,1,0:T(8,128)(2,1)} %param.12) | copy-start | bytes 9437188
  171.6 5.1 %copy-start.1 = (f32[128,8]{0,1:T(8,128)S(1)}, f32[128,8]{0,1:T(8,128)}, u32[]{:S(2)}) copy-start(f32[128,8]{0,1:T(8,128)} %param.10) | copy-start | bytes 12292
  171.6 120.3 %all-to-all-start.1 = ((bf16[16,80,2048]{2,1,0:T(8,128)(2,1)}), bf16[16,80,2048]{2,1,0:T(8,128)(2,1)}, u32[]{:S(2)}, u32[]{:S(2)}) async-start(bf16[16,80,2048]{2,1,0:T(8,128)(2,1)} %bitcast.47), calls=%async_computation.1 | async-start | bytes 10485760 | tf_op jit(solution)/shard_map/all_to_all | solution.py:31
where the time goes:
time: 323 us; the launch traced here: 322 us
  blocking collectives  122 us (38%)
  waiting for transfers between devices  115 us (36%)
  local copies, waits for them, and re-layouts  52.1 us (16%)
  matrix products  18.6 us (6%)
  other arithmetic  9.49 us (3%)
  starting transfers between devices  5.09 us (2%)
    all_to_all x1, blocking collectives, body(): lax.all_to_all(outgoing, 'ep', split_axis=0, concat_axis=0, tiled=True)  122 us
    all_to_all x1, waiting for transfers between devices, body(): lax.all_to_all(result.reshape(arrived.shape), 'ep', split_axis=0, concat_...  115 us
    gather x1, local copies, waits for them, and re-layouts, body(): picked = coming_back[flat, slot]  25.6 us
    unnamed x10, local copies, waits for them, and re-layouts  24.7 us
  transfers between devices with their start and end apart: 1, of which 1 were waited for; matrix products, arithmetic and copies ran while one was open for 0% of the time, Pallas kernels for 0%

commit v1 on v0

--- a/solution.py
+++ b/solution.py
@@ -1,20 +1,28 @@
+import functools
+
 import jax
 import jax.numpy as jnp
 from jax import lax
+from jax.experimental import pallas as pl
+from jax.experimental.pallas import tpu as pltpu
 from jax.sharding import PartitionSpec as P
 
 
-def body(hidden, norm_gain, routes, route_weight, w_gate, w_up, w_down):
+def normalise(hidden, norm_gain):
+    xf = hidden.astype(jnp.float32)
+    return (xf * lax.rsqrt(jnp.mean(xf * xf, axis=-1, keepdims=True) + 1e-06) * norm_gain).astype(
+        jnp.bfloat16
+    )
+
+
+def send_slots(hidden, norm_gain, routes, route_weight, w_gate, w_up, w_down):
     count = lax.axis_size("ep")
     tok = hidden.shape[0]
     width = hidden.shape[1]
     picks = routes.shape[1]
     experts = count * w_gate.shape[0]
     slots = tok * picks * 5 // (4 * experts)
-    xf = hidden.astype(jnp.float32)
-    normed = (xf * lax.rsqrt(jnp.mean(xf * xf, axis=-1, keepdims=True) + 1e-06) * norm_gain).astype(
-        jnp.bfloat16
-    )
+    normed = normalise(hidden, norm_gain)
     share = route_weight / jnp.sum(route_weight, axis=1, keepdims=True)
     flat = routes.reshape(-1)
     onehot = (flat[:, None] == jnp.arange(experts, dtype=jnp.int32)[None, :]).astype(jnp.int32)
@@ -37,6 +45,146 @@
     return mixed.astype(jnp.bfloat16)
 
 
+def experts_kernel(slots, tile, place, *refs):
+    blocks, refs = refs[: 4 * slots], refs[4 * slots :]
+    weights, refs = refs[:6], refs[6:]
+    mine, other, rows, tail, total = refs
+    tok, width = mine.shape[1], mine.shape[2]
+    ff = weights[0].shape[2]
+    f32, bf16 = jnp.float32, jnp.bfloat16
+    for n in range(slots):
+        inner_own, outer_own, inner_other, outer_other = blocks[4 * n : 4 * n + 4]
+
+        def load(own, far):
+            rows[0:tok, :] = own[:, :width]
+            rows[tok:, :] = far[:, :width]
+            tail[0:tok, :] = own[:, width:].astype(f32)
+            tail[tok:, :] = far[:, width:].astype(f32)
+
+        @pl.when(place[1] == 1)
+        def _():
+            load(inner_own, inner_other)
+
+        @pl.when(place[1] == 0)
+        def _():
+            load(outer_own, outer_other)
+
+        x = rows[...]
+        shares = tail[...]
+        half = shares.shape[1] // 2
+        lane = lax.broadcasted_iota(jnp.int32, shares.shape, 1) % half
+        for j in range(2):
+            wg, wu, wd = weights[3 * j : 3 * j + 3]
+            share = jnp.sum(jnp.where(lane == (place[0] ^ j), shares, 0.0), axis=1, keepdims=True)
+            for t in range(ff // tile):
+                cols = slice(t * tile, (t + 1) * tile)
+                gate = jnp.dot(x, wg[0, :, cols], preferred_element_type=f32)
+                upper = jnp.dot(x, wu[0, :, cols], preferred_element_type=f32)
+                units = (gate / (1.0 + jnp.exp(-gate)) * upper * share).astype(bf16)
+                part = jnp.dot(units, wd[0, cols, :], preferred_element_type=f32)
+                if j == 0 and t == 0:
+                    total[...] = part
+                elif j == 0 or t < ff // tile - 1:
+                    total[...] += part
+                else:
+                    done = (total[...] + part).astype(bf16)
+                    mine[n] = done[:tok]
+                    other[n] = done[tok:]
+
+
+def run_experts(place, slots, weights):
+    tok, wide = slots[0][0].shape
+    _, width, ff = weights[0].shape
+    n = len(slots)
+    vmem = pl.BlockSpec(memory_space=pltpu.VMEM)
+    out = jax.ShapeDtypeStruct((n, tok, width), jnp.bfloat16)
+    return pl.pallas_call(
+        functools.partial(experts_kernel, n, ff // 3),
+        in_specs=[pl.BlockSpec(memory_space=pltpu.SMEM)] + [vmem] * (4 * n + 6),
+        out_specs=[vmem] * 2,
+        out_shape=[out, out],
+        scratch_shapes=[
+            pltpu.VMEM((2 * tok, width), jnp.bfloat16),
+            pltpu.VMEM((2 * tok, wide - width), jnp.float32),
+            pltpu.VMEM((2 * tok, width), jnp.float32),
+        ],
+        compiler_params=pltpu.CompilerParams(vmem_limit_bytes=20 * 2**20),
+        cost_estimate=pl.CostEstimate(
+            flops=2 * n * tok * 2 * width * ff * 6,
+            bytes_accessed=12 * width * ff,
+            transcendentals=4 * n * tok * ff,
+        ),
+    )(place, *[block for slot in slots for block in slot], *weights)
+
+
+def gather_rows(hidden, norm_gain, routes, route_weight, w_gate, w_up, w_down):
+    count = lax.axis_size("ep")
+    experts = count * w_gate.shape[0]
+    tok, width = hidden.shape
+    f32, bf16 = jnp.float32, jnp.bfloat16
+    tie = lambda *arrays: lax.optimization_barrier(arrays)
+
+    def line(x, to):
+        moves = [(i, to[i // 4] * 4 + i % 4) for i in range(count) if to[i // 4] is not None]
+        return lax.ppermute(x, "ep", moves)
+
+    def cross(x, lines=(0, 1, 2, 3)):
+        return lax.ppermute(x, "ep", [(i, i ^ 2) for i in range(count) if i // 4 in lines])
+
+    def other_core(x):
+        return lax.ppermute(x, "ep", [(i, i ^ 1) for i in range(count)])
+
+    ends, inner = (0, 3), (1, 2)
+    pairs, middle = [1, 0, 3, 2], [None, 2, 1, None]
+    outward, inward = [None, 0, 3, None], [1, None, None, 2]
+
+    me = lax.axis_index("ep")
+    is_inner = (me // 4 == 1) | (me // 4 == 2)
+    place = jnp.stack([me, is_inner]).astype(jnp.int32)
+
+    normed = normalise(hidden, norm_gain)
+    share = route_weight / jnp.sum(route_weight, axis=1, keepdims=True)
+    names = routes[:, :, None] == jnp.arange(experts, dtype=jnp.int32)[None, None, :]
+    dense = jnp.sum(jnp.where(names, share[:, :, None], 0.0), axis=1)
+    high = dense.astype(bf16)
+    low = (dense - high.astype(f32)).astype(bf16)
+    gap = jnp.zeros((tok, 64 - experts), bf16)
+    own = jnp.concatenate([normed, high, gap, low, gap], axis=1)
+
+    p1, n2, y0 = line(own, pairs), line(own, middle), cross(own)
+    p1, n2 = tie(p1, n2)
+    n4, n3 = line(p1, middle), line(n2, outward)
+    p1, y0 = tie(p1, y0)
+    y1 = cross(p1)
+    others = [other_core(w) for w in (w_gate, w_up, w_down)]
+    n4, n3 = tie(n4, n3)
+    n5 = line(n4, outward)
+    n3, n2, y1 = tie(n3, n2, y1)
+    yn3, yn2 = cross(n3, ends), cross(n2, inner)
+    n4, y1 = tie(n4, y1)
+    yn4 = cross(n4, inner)
+    n5, yn3, yn2 = tie(n5, yn3, yn2)
+    yn5 = cross(n5, ends)
+
+    weights = [
+        pltpu.with_memory_space_constraint(w, pltpu.VMEM) for w in (w_gate, w_up, w_down, *others)
+    ]
+    ma, oa = run_experts(place, [(own, own, y0, y0), (p1, p1, y1, y1)], weights)
+    mb, ob = run_experts(place, [(n2, n3, yn2, yn3)], weights)
+    mc, oc = run_experts(place, [(n4, n5, yn4, yn5)], weights)
+
+    def add(*parts):
+        return sum(p.astype(f32) for p in parts).astype(bf16)
+
+    r4 = add(mc[0], cross(oc[0]))
+    r3 = add(mb[0], cross(ob[0]))
+    r4 = add(r4, line(r4, inward))
+    q4 = line(r4, middle)
+    r1 = add(ma[1], cross(oa[1]), q4)
+    r3 = add(r3, line(r3, inward))
+    return add(ma[0], cross(oa[0]), line(r1, pairs), line(r3, middle))
+
+
 def solution(mesh):
     in_specs = (
         P(("group", "ep"), None),
@@ -48,4 +196,11 @@
         P("ep", None, None),
     )
     out_specs = P(("group", "ep"), None)
+
+    def body(hidden, norm_gain, routes, route_weight, w_gate, w_up, w_down):
+        count, tok, picks = mesh.shape["ep"], hidden.shape[0], routes.shape[1]
+        dense = count == 16 and w_gate.shape[0] == 1 and 2 * picks >= count
+        plan = gather_rows if dense else send_slots
+        return plan(hidden, norm_gain, routes, route_weight, w_gate, w_up, w_down)
+
     return jax.shard_map(body, mesh=mesh, in_specs=in_specs, out_specs=out_specs, check_vma=False)

time: 323 us -> 165 us (0.51)
  blocking collectives: 122 us -> 0 us
  waiting for transfers between devices: 115 us -> 71.3 us
  local copies, waits for them, and re-layouts: 52.1 us -> 9.31 us
  Pallas kernels: 0 us -> 35.4 us
  starting transfers between devices: 5.09 us -> 37.5 us
  matrix products: 18.6 us -> 0 us
    all_to_all x1 -> x0, blocking collectives: 122 us -> none  [body(): lax.all_to_all(outgoing, 'ep', split_axis=0, concat_axis=0, tiled=True)]
    all_to_all x1 -> x0, waiting for transfers between devices: 115 us -> none  [body(): lax.all_to_all(result.reshape(arrived.shape), 'ep', split_axis=0, concat_...]
    ppermute x0 -> x23, waiting for transfers between devices: none -> 71.3 us  [the longest x10 50.7 us: line(): return lax.ppermute(x, 'ep', moves)]
    ppermute x0 -> x23, starting transfers between devices: none -> 37.5 us  [the longest x10 20.8 us: line(): return lax.ppermute(x, 'ep', moves)]
    pallas_call x0 -> x3, Pallas kernels: none -> 35.4 us  [run_experts(): pl.pallas_call(functools.partial(experts_kernel, n, ff // 3), in_specs=[p...]
    gather x1 -> x0, local copies, waits for them, and re-layouts: 25.6 us -> none  [body(): picked = coming_back[flat, slot]]
    dot_general x4 -> x0, matrix products: 18.6 us -> none  [the longest x1 6.05 us: body(): jnp.dot(units, w_down[0], preferred_element_type=jnp.float32)]
    unnamed x10 -> x28, local copies, waits for them, and re-layouts: 24.7 us -> 7.04 us
  transfers between devices with their start and end apart: 1 -> 23, of which waited for: 1 -> 10; matrix products, arithmetic and copies ran while one was open for 0% -> 5% of each run, Pallas kernels for 0% -> 22%
where the time goes in v1:
time: 165 us; the launch traced here: 161 us
  waiting for transfers between devices  71.3 us (43%)
  starting transfers between devices  37.5 us (23%)
  Pallas kernels  35.4 us (21%)
  local copies, waits for them, and re-layouts  9.31 us (6%)
  other arithmetic  7.61 us (5%)
    ppermute x10, waiting for transfers between devices, line(): return lax.ppermute(x, 'ep', moves)  50.7 us
    pallas_call x3, Pallas kernels, run_experts(): pl.pallas_call(functools.partial(experts_kernel, n, ff // 3), in_specs=[p...  35.4 us
    ppermute x10, starting transfers between devices, line(): return lax.ppermute(x, 'ep', moves)  20.8 us
    ppermute x10, waiting for transfers between devices, cross(): lax.ppermute(x, 'ep', [(i, i ^ 2) for i in range(count) if i // 4 in lines])  20.6 us
    ppermute x10, starting transfers between devices, cross(): lax.ppermute(x, 'ep', [(i, i ^ 2) for i in range(count) if i // 4 in lines])  16.2 us
    unnamed x28, local copies, waits for them, and re-layouts  7.04 us
  transfers between devices with their start and end apart: 23, of which 10 were waited for; matrix products, arithmetic and copies ran while one was open for 5% of the time, Pallas kernels for 22%

profile of v1, /device:TPU:18, one launch (start us, length us, event | category | flops | bytes accessed | tf_op | source)
XLA Modules:
  0.0 161.5 jit_solution(3147647883401552852)
XLA Ops:
  0.6 1.5 fusion
  3.5 2.0 %fusion.2 = bf16[128,2048]{1,0:T(8,128)(2,1)} fusion(bf16[128,2048]{1,0:T(8,128)(2,1)} %param.7, f32[2048]{0:T(1024)} %param.8, f32[128]{0:T(128)S(1)} %add_rsqrt_fusion), kind=kLoop, calls=%fused_computation.4 | loop fusion | flops 1048576 | bytes 1057280 | tf_op jit(solution)/shard_map/convert_element_type | solution.py:13
  6.6 1.9 %concatenate.3.refs_0_.refs_1_ = bf16[128,2176]{1,0:T(8,128)(2,1)} concatenate(bf16[128,2048]{1,0:T(8,128)(2,1)} %fusion.2, bf16[128,16]{1,0:T(8,128)(2,1)S(1)} %copy.14, bf16[128,48]{1,0:T(8,128)(2,1)S(1)} %broadcast_in_dim.23, bf16[128,16]{1,0:T(8,128)(2,1)S(1)} %subtract_convert_fusion, bf16[128,48]{1,0:T(8,128)(2,1)S(1)} %broadcast_in_dim.23), dimensions={1} | concatenate | bytes 1114112 | tf_op jit(solution)/shard_map/concatenate | solution.py:152
  8.5 1.6 collective-permute-start
  10.0 1.9 %collective-permute-start.1 = (bf16[128,2176]{1,0:T(8,128)(2,1)}, bf16[128,2176]{1,0:T(8,128)(2,1)}, u32[]{:S(2)}, u32[]{:S(2)}) collective-permute-start(bf16[128,2176]{1,0:T(8,128)(2,1)} %concatenate.3.refs_0_.refs_1_), channel_id=1, source_target_pairs={{4,8},{5,9},{6,10},{7,11},{8,4},{9,5},{10,6},{11,7},{20,24},{21,25... | collective-permute-start | bytes 1671176 | tf_op jit(solution)/shard_map/ppermute | solution.py:129
  12.0 11.4 %collective-permute-done.refs_4_.refs_5_ = bf16[128,2176]{1,0:T(8,128)(2,1)S(1)} collective-permute-done((bf16[128,2176]{1,0:T(8,128)(2,1)}, bf16[128,2176]{1,0:T(8,128)(2,1)S(1)}, u32[]{:S(2)}, u32[]{:S(2)}) %collective-permute-start) | collective-permute-done | bytes 557088 | tf_op jit(solution)/shard_map/ppermute | solution.py:129
  23.4 1.5 collective-permute-start.2
  24.9 1.8 %collective-permute-done.1.refs_0_ = bf16[128,2176]{1,0:T(8,128)(2,1)} collective-permute-done((bf16[128,2176]{1,0:T(8,128)(2,1)}, bf16[128,2176]{1,0:T(8,128)(2,1)}, u32[]{:S(2)}, u32[]{:S(2)}) %collective-permute-start.1) | collective-permute-done | bytes 557088 | tf_op jit(solution)/shard_map/ppermute | solution.py:129
  26.6 2.2 %collective-permute-start.3 = (bf16[128,2176]{1,0:T(8,128)(2,1)S(1)}, bf16[128,2176]{1,0:T(8,128)(2,1)S(1)}, u32[]{:S(2)}, u32[]{:S(2)}) collective-permute-start(bf16[128,2176]{1,0:T(8,128)(2,1)S(1)} %collective-permute-done.refs_4_.refs_5_), channel_id=1, source_target_pairs={{4,8},{5,9},{6,10},{7,11},{8,4},{9,5},{10,6},{11,7},{20,24},{21,25... | collective-permute-start | bytes 1671176 | tf_op jit(solution)/shard_map/ppermute | solution.py:129
  28.8 8.7 %collective-permute-done.2.refs_2_.refs_3_ = bf16[128,2176]{1,0:T(8,128)(2,1)S(1)} collective-permute-done((bf16[128,2176]{1,0:T(8,128)(2,1)}, bf16[128,2176]{1,0:T(8,128)(2,1)S(1)}, u32[]{:S(2)}, u32[]{:S(2)}) %collective-permute-start.2) | collective-permute-done | bytes 557088 | tf_op jit(solution)/shard_map/ppermute | solution.py:132
  38.4 4.2 %collective-permute-start.4 = (bf16[128,2176]{1,0:T(8,128)(2,1)}, bf16[128,2176]{1,0:T(8,128)(2,1)}, u32[]{:S(2)}, u32[]{:S(2)}) collective-permute-start(bf16[128,2176]{1,0:T(8,128)(2,1)} %collective-permute-done.1.refs_0_), channel_id=1, source_target_pairs={{4,0},{5,1},{6,2},{7,3},{8,12},{9,13},{10,14},{11,15},{20,16},{21,... | collective-permute-start | bytes 1671176 | tf_op jit(solution)/shard_map/ppermute | solution.py:129
  42.6 1.5 collective-permute-start.5
  44.9 7.6 %collective-permute-done.4.refs_1_ = bf16[128,2176]{1,0:T(8,128)(2,1)} collective-permute-done((bf16[128,2176]{1,0:T(8,128)(2,1)}, bf16[128,2176]{1,0:T(8,128)(2,1)}, u32[]{:S(2)}, u32[]{:S(2)}) %collective-permute-start.4) | collective-permute-done | bytes 557088 | tf_op jit(solution)/shard_map/ppermute | solution.py:129
  52.5 4.4 %collective-permute-start.11 = (bf16[128,2176]{1,0:T(8,128)(2,1)S(1)}, bf16[128,2176]{1,0:T(8,128)(2,1)S(1)}, u32[]{:S(2)}, u32[]{:S(2)}) collective-permute-start(bf16[128,2176]{1,0:T(8,128)(2,1)S(1)} %collective-permute-done.3.refs_0_), channel_id=1, source_target_pairs={{4,0},{5,1},{6,2},{7,3},{8,12},{9,13},{10,14},{11,15},{20,16},{21,... | collective-permute-start | bytes 1671176 | tf_op jit(solution)/shard_map/ppermute | solution.py:129
  57.7 1.5 collective-permute-start.12
  59.2 7.2 %collective-permute-done.11.refs_1_ = bf16[128,2176]{1,0:T(8,128)(2,1)S(1)} collective-permute-done((bf16[128,2176]{1,0:T(8,128)(2,1)S(1)}, bf16[128,2176]{1,0:T(8,128)(2,1)S(1)}, u32[]{:S(2)}, u32[]{:S(2)}) %collective-permute-start.11) | collective-permute-done | bytes 557088 | tf_op jit(solution)/shard_map/ppermute | solution.py:129
  67.2 3.4 %collective-permute-start.13 = (bf16[128,2176]{1,0:T(8,128)(2,1)}, bf16[128,2176]{1,0:T(8,128)(2,1)}, u32[]{:S(2)}, u32[]{:S(2)}) collective-permute-start(bf16[128,2176]{1,0:T(8,128)(2,1)} %collective-permute-done.1.refs_0_), channel_id=1, source_target_pairs={{4,6},{5,7},{6,4},{7,5},{8,10},{9,11},{10,8},{11,9},{20,22},{21,23... | collective-permute-start | bytes 1671176 | tf_op jit(solution)/shard_map/ppermute | solution.py:132
  70.7 2.4 %collective-permute-start.14 = (bf16[128,2176]{1,0:T(8,128)(2,1)}, bf16[128,2176]{1,0:T(8,128)(2,1)S(1)}, u32[]{:S(2)}, u32[]{:S(2)}) collective-permute-start(bf16[128,2176]{1,0:T(8,128)(2,1)} %copy-done.3), channel_id=1, source_target_pairs={{4,6},{5,7},{6,4},{7,5},{8,10},{9,11},{10,8},{11,9},{20,22},{21,23... | collective-permute-start | bytes 1671176 | tf_op jit(solution)/shard_map/ppermute | solution.py:132
  73.1 11.9 %collective-permute-done.13.refs_2_ = bf16[128,2176]{1,0:T(8,128)(2,1)} collective-permute-done((bf16[128,2176]{1,0:T(8,128)(2,1)}, bf16[128,2176]{1,0:T(8,128)(2,1)}, u32[]{:S(2)}, u32[]{:S(2)}) %collective-permute-start.13) | collective-permute-done | bytes 557088 | tf_op jit(solution)/shard_map/ppermute | solution.py:132
  85.8 1.9 %copy-done.1 = bf16[1,2048,768]{2,1,0:T(8,128)(2,1)S(1)} copy-done((bf16[1,2048,768]{2,1,0:T(8,128)(2,1)S(1)}, bf16[1,2048,768]{2,1,0:T(8,128)(2,1)}, u32[]{:S(2)}) %copy-start.1) | copy-done | bytes 3145752
  87.6 1.9 %copy-done.2 = bf16[1,768,2048]{2,1,0:T(8,128)(2,1)S(1)} copy-done((bf16[1,768,2048]{2,1,0:T(8,128)(2,1)S(1)}, bf16[1,768,2048]{2,1,0:T(8,128)(2,1)}, u32[]{:S(2)}) %copy-start.2) | copy-done | bytes 3145752
  89.5 10.3 %shard_map.75 = (bf16[1,128,2048]{2,1,0:T(8,128)(2,1)S(1)}, bf16[1,128,2048]{2,1,0:T(8,128)(2,1)S(1)}) custom-call(s32[2]{0:T(128)S(1)} %pad_add_fusion.place, bf16[128,2176]{1,0:T(8,128)(2,1)} %collective-permute-done.1.refs_0_, bf16[128,2176]{1,0:T(8,128)(2,1)} %collective-permute-done.4.refs_1_, bf16[128,2176]{1,0:T(8,128)(2,1)} %collective-permute-done.13.refs_2_, ...), custom_call_target="tpu_custom_call" | custom-call | flops 4831838208 | bytes 18874368 | tf_op jit(solution)/shard_map/pallas_call | solution.py:101
  99.9 1.6 collective-permute-start.20
  101.5 9.6 %shard_map.74 = (bf16[1,128,2048]{2,1,0:T(8,128)(2,1)S(1)}, bf16[1,128,2048]{2,1,0:T(8,128)(2,1)S(1)}) custom-call(s32[2]{0:T(128)S(1)} %pad_add_fusion.place, bf16[128,2176]{1,0:T(8,128)(2,1)S(1)} %copy-done.4, bf16[128,2176]{1,0:T(8,128)(2,1)S(1)} %copy-done.6, bf16[128,2176]{1,0:T(8,128)(2,1)S(1)} %collective-permute-done.14.refs_2_, ...), custom_call_target="tpu_custom_call" | custom-call | flops 4831838208 | bytes 18874368 | tf_op jit(solution)/shard_map/pallas_call | solution.py:101
  111.7 15.5 %shard_map.73 = (bf16[2,128,2048]{2,1,0:T(8,128)(2,1)S(1)}, bf16[2,128,2048]{2,1,0:T(8,128)(2,1)S(1)}) custom-call(s32[2]{0:T(128)S(1)} %pad_add_fusion.place, bf16[128,2176]{1,0:T(8,128)(2,1)S(1)} %copy-done.7, bf16[128,2176]{1,0:T(8,128)(2,1)S(1)} %copy-done.7, bf16[128,2176]{1,0:T(8,128)(2,1)S(1)} %copy-done.11, bf16[128,2176]{1,0:T(8,128)(2,1)S(1)} %copy-done.11, ...), custom_call_target="tpu_custom_call" | custom-call | flops 9663676416 | bytes 18874368 | tf_op jit(solution)/shard_map/pallas_call | solution.py:101
  130.2 1.6 collective-permute-start.10
  131.7 7.7 %collective-permute-done.17 = bf16[128,2048]{1,0:T(8,128)(2,1)S(1)} collective-permute-done((bf16[128,2048]{1,0:T(8,128)(2,1)S(1)}, bf16[128,2048]{1,0:T(8,128)(2,1)S(1)}, u32[]{:S(2)}, u32[]{:S(2)}) %collective-permute-start.17) | collective-permute-done | bytes 524320 | tf_op jit(solution)/shard_map/ppermute | solution.py:129
  139.6 1.9 %collective-permute-start.18 = (bf16[128,2048]{1,0:T(8,128)(2,1)S(1)}, bf16[128,2048]{1,0:T(8,128)(2,1)S(1)}, u32[]{:S(2)}, u32[]{:S(2)}) collective-permute-start(bf16[128,2048]{1,0:T(8,128)(2,1)S(1)} %add_convert_fusion.1), channel_id=1, source_target_pairs={{4,8},{5,9},{6,10},{7,11},{8,4},{9,5},{10,6},{11,7},{20,24},{21,25... | collective-permute-start | bytes 1572872 | tf_op jit(solution)/shard_map/ppermute | solution.py:129
  141.5 1.4 collective-permute-start.9
  142.9 5.8 %collective-permute-done.21 = bf16[128,2048]{1,0:T(8,128)(2,1)S(1)} collective-permute-done((bf16[128,2048]{1,0:T(8,128)(2,1)S(1)}, bf16[128,2048]{1,0:T(8,128)(2,1)S(1)}, u32[]{:S(2)}, u32[]{:S(2)}) %collective-permute-start.21) | collective-permute-done | bytes 524320 | tf_op jit(solution)/shard_map/ppermute | solution.py:129
  148.9 1.9 %collective-permute-start.22 = (bf16[128,2048]{1,0:T(8,128)(2,1)S(1)}, bf16[128,2048]{1,0:T(8,128)(2,1)S(1)}, u32[]{:S(2)}, u32[]{:S(2)}) collective-permute-start(bf16[128,2048]{1,0:T(8,128)(2,1)S(1)} %add_convert_fusion), channel_id=1, source_target_pairs={{4,8},{5,9},{6,10},{7,11},{8,4},{9,5},{10,6},{11,7},{20,24},{21,25... | collective-permute-start | bytes 1572872 | tf_op jit(solution)/shard_map/ppermute | solution.py:129
  151.2 8.8 %collective-permute-done.22 = bf16[128,2048]{1,0:T(8,128)(2,1)S(1)} collective-permute-done((bf16[128,2048]{1,0:T(8,128)(2,1)S(1)}, bf16[128,2048]{1,0:T(8,128)(2,1)S(1)}, u32[]{:S(2)}, u32[]{:S(2)}) %collective-permute-start.22) | collective-permute-done | bytes 524320 | tf_op jit(solution)/shard_map/ppermute | solution.py:129
  (66 shorter events, 12.7 us)
Async XLA Ops:
  0.0 85.7 %copy-start = (bf16[1,2048,768]{2,1,0:T(8,128)(2,1)S(1)}, bf16[1,2048,768]{2,1,0:T(8,128)(2,1)}, u32[]{:S(2)}) copy-start(bf16[1,2048,768]{2,1,0:T(8,128)(2,1)} %refs_4_.3) | copy-start | bytes 9437188
  0.0 85.7 %collective-permute-start.6 = (bf16[1,2048,768]{2,1,0:T(8,128)(2,1)}, bf16[1,2048,768]{2,1,0:T(8,128)(2,1)}, u32[]{:S(2)}, u32[]{:S(2)}) collective-permute-start(bf16[1,2048,768]{2,1,0:T(8,128)(2,1)} %refs_4_.3), channel_id=1, source_target_pairs={{0,1},{1,0},{2,3},{3,2},{4,5},{5,4},{6,7},{7,6},{8,9},{9,8},{10,11... | collective-permute-start | bytes 9437192 | tf_op jit(solution)/shard_map/ppermute | solution.py:135
  0.0 85.7 %collective-permute-start.7 = (bf16[1,2048,768]{2,1,0:T(8,128)(2,1)}, bf16[1,2048,768]{2,1,0:T(8,128)(2,1)}, u32[]{:S(2)}, u32[]{:S(2)}) collective-permute-start(bf16[1,2048,768]{2,1,0:T(8,128)(2,1)} %refs_5_.3), channel_id=1, source_target_pairs={{0,1},{1,0},{2,3},{3,2},{4,5},{5,4},{6,7},{7,6},{8,9},{9,8},{10,11... | collective-permute-start | bytes 9437192 | tf_op jit(solution)/shard_map/ppermute | solution.py:135
  0.5 85.2 %collective-permute-start.8 = (bf16[1,768,2048]{2,1,0:T(8,128)(2,1)}, bf16[1,768,2048]{2,1,0:T(8,128)(2,1)}, u32[]{:S(2)}, u32[]{:S(2)}) collective-permute-start(bf16[1,768,2048]{2,1,0:T(8,128)(2,1)} %refs_6_.3), channel_id=1, source_target_pairs={{0,1},{1,0},{2,3},{3,2},{4,5},{5,4},{6,7},{7,6},{8,9},{9,8},{10,11... | collective-permute-start | bytes 9437192 | tf_op jit(solution)/shard_map/ppermute | solution.py:135
  8.5 14.9 %collective-permute-start = (bf16[128,2176]{1,0:T(8,128)(2,1)}, bf16[128,2176]{1,0:T(8,128)(2,1)S(1)}, u32[]{:S(2)}, u32[]{:S(2)}) collective-permute-start(bf16[128,2176]{1,0:T(8,128)(2,1)} %concatenate.3.refs_0_.refs_1_), channel_id=1, source_target_pairs={{0,4},{1,5},{2,6},{3,7},{4,0},{5,1},{6,2},{7,3},{8,12},{9,13},{10,... | collective-permute-start | bytes 1671176 | tf_op jit(solution)/shard_map/ppermute | solution.py:129
  10.0 16.6 %collective-permute-start.1 = (bf16[128,2176]{1,0:T(8,128)(2,1)}, bf16[128,2176]{1,0:T(8,128)(2,1)}, u32[]{:S(2)}, u32[]{:S(2)}) collective-permute-start(bf16[128,2176]{1,0:T(8,128)(2,1)} %concatenate.3.refs_0_.refs_1_), channel_id=1, source_target_pairs={{4,8},{5,9},{6,10},{7,11},{8,4},{9,5},{10,6},{11,7},{20,24},{21,25... | collective-permute-start | bytes 1671176 | tf_op jit(solution)/shard_map/ppermute | solution.py:129
  23.4 14.2 %collective-permute-start.2 = (bf16[128,2176]{1,0:T(8,128)(2,1)}, bf16[128,2176]{1,0:T(8,128)(2,1)S(1)}, u32[]{:S(2)}, u32[]{:S(2)}) collective-permute-start(bf16[128,2176]{1,0:T(8,128)(2,1)} %concatenate.3.refs_0_.refs_1_), channel_id=1, source_target_pairs={{0,2},{1,3},{2,0},{3,1},{4,6},{5,7},{6,4},{7,5},{8,10},{9,11},{10,... | collective-permute-start | bytes 1671176 | tf_op jit(solution)/shard_map/ppermute | solution.py:132
  26.6 15.9 %collective-permute-start.3 = (bf16[128,2176]{1,0:T(8,128)(2,1)S(1)}, bf16[128,2176]{1,0:T(8,128)(2,1)S(1)}, u32[]{:S(2)}, u32[]{:S(2)}) collective-permute-start(bf16[128,2176]{1,0:T(8,128)(2,1)S(1)} %collective-permute-done.refs_4_.refs_5_), channel_id=1, source_target_pairs={{4,8},{5,9},{6,10},{7,11},{8,4},{9,5},{10,6},{11,7},{20,24},{21,25... | collective-permute-start | bytes 1671176 | tf_op jit(solution)/shard_map/ppermute | solution.py:129
  38.4 14.1 %collective-permute-start.4 = (bf16[128,2176]{1,0:T(8,128)(2,1)}, bf16[128,2176]{1,0:T(8,128)(2,1)}, u32[]{:S(2)}, u32[]{:S(2)}) collective-permute-start(bf16[128,2176]{1,0:T(8,128)(2,1)} %collective-permute-done.1.refs_0_), channel_id=1, source_target_pairs={{4,0},{5,1},{6,2},{7,3},{8,12},{9,13},{10,14},{11,15},{20,16},{21,... | collective-permute-start | bytes 1671176 | tf_op jit(solution)/shard_map/ppermute | solution.py:129
  42.6 9.9 %copy-start.3 = (bf16[128,2176]{1,0:T(8,128)(2,1)}, bf16[128,2176]{1,0:T(8,128)(2,1)S(1)}, u32[]{:S(2)}) copy-start(bf16[128,2176]{1,0:T(8,128)(2,1)S(1)} %collective-permute-done.3.refs_0_) | copy-start | bytes 1671172
  42.6 14.3 %collective-permute-start.5 = (bf16[128,2176]{1,0:T(8,128)(2,1)S(1)}, bf16[128,2176]{1,0:T(8,128)(2,1)S(1)}, u32[]{:S(2)}, u32[]{:S(2)}) collective-permute-start(bf16[128,2176]{1,0:T(8,128)(2,1)S(1)} %collective-permute-done.refs_4_.refs_5_), channel_id=1, source_target_pairs={{0,2},{1,3},{2,0},{3,1},{4,6},{5,7},{6,4},{7,5},{8,10},{9,11},{10,... | collective-permute-start | bytes 1671176 | tf_op jit(solution)/shard_map/ppermute | solution.py:132
  52.5 13.9 %collective-permute-start.11 = (bf16[128,2176]{1,0:T(8,128)(2,1)S(1)}, bf16[128,2176]{1,0:T(8,128)(2,1)S(1)}, u32[]{:S(2)}, u32[]{:S(2)}) collective-permute-start(bf16[128,2176]{1,0:T(8,128)(2,1)S(1)} %collective-permute-done.3.refs_0_), channel_id=1, source_target_pairs={{4,0},{5,1},{6,2},{7,3},{8,12},{9,13},{10,14},{11,15},{20,16},{21,... | collective-permute-start | bytes 1671176 | tf_op jit(solution)/shard_map/ppermute | solution.py:129
  57.7 12.9 %collective-permute-start.12 = (bf16[128,2176]{1,0:T(8,128)(2,1)}, bf16[128,2176]{1,0:T(8,128)(2,1)}, u32[]{:S(2)}, u32[]{:S(2)}) collective-permute-start(bf16[128,2176]{1,0:T(8,128)(2,1)} %collective-permute-done.4.refs_1_), channel_id=1, source_target_pairs={{0,2},{1,3},{2,0},{3,1},{12,14},{13,15},{14,12},{15,13},{16,18},{1... | collective-permute-start | bytes 1671176 | tf_op jit(solution)/shard_map/ppermute | solution.py:132
  67.2 17.8 %collective-permute-start.13 = (bf16[128,2176]{1,0:T(8,128)(2,1)}, bf16[128,2176]{1,0:T(8,128)(2,1)}, u32[]{:S(2)}, u32[]{:S(2)}) collective-permute-start(bf16[128,2176]{1,0:T(8,128)(2,1)} %collective-permute-done.1.refs_0_), channel_id=1, source_target_pairs={{4,6},{5,7},{6,4},{7,5},{8,10},{9,11},{10,8},{11,9},{20,22},{21,23... | collective-permute-start | bytes 1671176 | tf_op jit(solution)/shard_map/ppermute | solution.py:132
  70.7 30.8 %collective-permute-start.14 = (bf16[128,2176]{1,0:T(8,128)(2,1)}, bf16[128,2176]{1,0:T(8,128)(2,1)S(1)}, u32[]{:S(2)}, u32[]{:S(2)}) collective-permute-start(bf16[128,2176]{1,0:T(8,128)(2,1)} %copy-done.3), channel_id=1, source_target_pairs={{4,6},{5,7},{6,4},{7,5},{8,10},{9,11},{10,8},{11,9},{20,22},{21,23... | collective-permute-start | bytes 1671176 | tf_op jit(solution)/shard_map/ppermute | solution.py:132
  85.0 16.5 %collective-permute-start.15 = (bf16[128,2176]{1,0:T(8,128)(2,1)}, bf16[128,2176]{1,0:T(8,128)(2,1)S(1)}, u32[]{:S(2)}, u32[]{:S(2)}) collective-permute-start(bf16[128,2176]{1,0:T(8,128)(2,1)} %copy-done.5), channel_id=1, source_target_pairs={{0,2},{1,3},{2,0},{3,1},{12,14},{13,15},{14,12},{15,13},{16,18},{1... | collective-permute-start | bytes 1671176 | tf_op jit(solution)/shard_map/ppermute | solution.py:132
  85.8 1.9 %copy-start.1 = (bf16[1,2048,768]{2,1,0:T(8,128)(2,1)S(1)}, bf16[1,2048,768]{2,1,0:T(8,128)(2,1)}, u32[]{:S(2)}) copy-start(bf16[1,2048,768]{2,1,0:T(8,128)(2,1)} %refs_5_.3) | copy-start | bytes 9437188
  89.5 11.9 %copy-start.4 = (bf16[128,2176]{1,0:T(8,128)(2,1)S(1)}, bf16[128,2176]{1,0:T(8,128)(2,1)}, u32[]{:S(2)}) copy-start(bf16[128,2176]{1,0:T(8,128)(2,1)} %copy-done.3) | copy-start | bytes 1671172
  89.5 11.9 %copy-start.6 = (bf16[128,2176]{1,0:T(8,128)(2,1)S(1)}, bf16[128,2176]{1,0:T(8,128)(2,1)}, u32[]{:S(2)}) copy-start(bf16[128,2176]{1,0:T(8,128)(2,1)} %copy-done.5) | copy-start | bytes 1671172
  99.8 11.8 %copy-start.7 = (bf16[128,2176]{1,0:T(8,128)(2,1)S(1)}, bf16[128,2176]{1,0:T(8,128)(2,1)}, u32[]{:S(2)}) copy-start(bf16[128,2176]{1,0:T(8,128)(2,1)} %concatenate.3.refs_0_.refs_1_) | copy-start | bytes 1671172
  99.8 11.8 %copy-start.9 = (bf16[128,2176]{1,0:T(8,128)(2,1)S(1)}, bf16[128,2176]{1,0:T(8,128)(2,1)}, u32[]{:S(2)}) copy-start(bf16[128,2176]{1,0:T(8,128)(2,1)} %copy-done.8) | copy-start | bytes 1671172
  99.9 11.8 %copy-start.11 = (bf16[128,2176]{1,0:T(8,128)(2,1)S(1)}, bf16[128,2176]{1,0:T(8,128)(2,1)}, u32[]{:S(2)}) copy-start(bf16[128,2176]{1,0:T(8,128)(2,1)} %copy-done.10) | copy-start | bytes 1671172
  99.9 11.8 %copy-start.13 = (bf16[128,2176]{1,0:T(8,128)(2,1)S(1)}, bf16[128,2176]{1,0:T(8,128)(2,1)}, u32[]{:S(2)}) copy-start(bf16[128,2176]{1,0:T(8,128)(2,1)} %copy-done.12) | copy-start | bytes 1671172
  99.9 28.8 %collective-permute-start.20 = (bf16[128,2048]{1,0:T(8,128)(2,1)S(1)}, bf16[128,2048]{1,0:T(8,128)(2,1)S(1)}, u32[]{:S(2)}, u32[]{:S(2)}) collective-permute-start(bf16[128,2048]{1,0:T(8,128)(2,1)S(1)} %bitcast.20), channel_id=1, source_target_pairs={{0,2},{1,3},{2,0},{3,1},{4,6},{5,7},{6,4},{7,5},{8,10},{9,11},{10,... | collective-permute-start | bytes 1572872 | tf_op jit(solution)/shard_map/ppermute | solution.py:132
  111.1 16.1 %collective-permute-start.16 = (bf16[128,2048]{1,0:T(8,128)(2,1)S(1)}, bf16[128,2048]{1,0:T(8,128)(2,1)S(1)}, u32[]{:S(2)}, u32[]{:S(2)}) collective-permute-start(bf16[128,2048]{1,0:T(8,128)(2,1)S(1)} %bitcast.21), channel_id=1, source_target_pairs={{0,2},{1,3},{2,0},{3,1},{4,6},{5,7},{6,4},{7,5},{8,10},{9,11},{10,... | collective-permute-start | bytes 1572872 | tf_op jit(solution)/shard_map/ppermute | solution.py:132
  127.3 12.1 %collective-permute-start.17 = (bf16[128,2048]{1,0:T(8,128)(2,1)S(1)}, bf16[128,2048]{1,0:T(8,128)(2,1)S(1)}, u32[]{:S(2)}, u32[]{:S(2)}) collective-permute-start(bf16[128,2048]{1,0:T(8,128)(2,1)S(1)} %fusion.4), channel_id=1, source_target_pairs={{0,4},{1,5},{2,6},{3,7},{12,8},{13,9},{14,10},{15,11},{16,20},{17,... | collective-permute-start | bytes 1572872 | tf_op jit(solution)/shard_map/ppermute | solution.py:129
  128.9 19.9 %collective-permute-start.21 = (bf16[128,2048]{1,0:T(8,128)(2,1)S(1)}, bf16[128,2048]{1,0:T(8,128)(2,1)S(1)}, u32[]{:S(2)}, u32[]{:S(2)}) collective-permute-start(bf16[128,2048]{1,0:T(8,128)(2,1)S(1)} %fusion.3), channel_id=1, source_target_pairs={{0,4},{1,5},{2,6},{3,7},{12,8},{13,9},{14,10},{15,11},{16,20},{17,... | collective-permute-start | bytes 1572872 | tf_op jit(solution)/shard_map/ppermute | solution.py:129
  130.2 20.7 %collective-permute-start.10 = (bf16[128,2048]{1,0:T(8,128)(2,1)S(1)}, bf16[128,2048]{1,0:T(8,128)(2,1)S(1)}, u32[]{:S(2)}, u32[]{:S(2)}) collective-permute-start(bf16[128,2048]{1,0:T(8,128)(2,1)S(1)} %get-tuple-element.46), channel_id=1, source_target_pairs={{0,2},{1,3},{2,0},{3,1},{4,6},{5,7},{6,4},{7,5},{8,10},{9,11},{10,... | collective-permute-start | bytes 1572872 | tf_op jit(solution)/shard_map/ppermute | solution.py:132
  139.6 11.3 %collective-permute-start.18 = (bf16[128,2048]{1,0:T(8,128)(2,1)S(1)}, bf16[128,2048]{1,0:T(8,128)(2,1)S(1)}, u32[]{:S(2)}, u32[]{:S(2)}) collective-permute-start(bf16[128,2048]{1,0:T(8,128)(2,1)S(1)} %add_convert_fusion.1), channel_id=1, source_target_pairs={{4,8},{5,9},{6,10},{7,11},{8,4},{9,5},{10,6},{11,7},{20,24},{21,25... | collective-permute-start | bytes 1572872 | tf_op jit(solution)/shard_map/ppermute | solution.py:129
  141.5 9.7 %collective-permute-start.9 = (bf16[128,2048]{1,0:T(8,128)(2,1)S(1)}, bf16[128,2048]{1,0:T(8,128)(2,1)S(1)}, u32[]{:S(2)}, u32[]{:S(2)}) collective-permute-start(bf16[128,2048]{1,0:T(8,128)(2,1)S(1)} %get-tuple-element.45), channel_id=1, source_target_pairs={{0,2},{1,3},{2,0},{3,1},{4,6},{5,7},{6,4},{7,5},{8,10},{9,11},{10,... | collective-permute-start | bytes 1572872 | tf_op jit(solution)/shard_map/ppermute | solution.py:132
  148.9 11.1 %collective-permute-start.22 = (bf16[128,2048]{1,0:T(8,128)(2,1)S(1)}, bf16[128,2048]{1,0:T(8,128)(2,1)S(1)}, u32[]{:S(2)}, u32[]{:S(2)}) collective-permute-start(bf16[128,2048]{1,0:T(8,128)(2,1)S(1)} %add_convert_fusion), channel_id=1, source_target_pairs={{4,8},{5,9},{6,10},{7,11},{8,4},{9,5},{10,6},{11,7},{20,24},{21,25... | collective-permute-start | bytes 1572872 | tf_op jit(solution)/shard_map/ppermute | solution.py:129
  151.1 9.2 %collective-permute-start.19 = (bf16[128,2048]{1,0:T(8,128)(2,1)S(1)}, bf16[128,2048]{1,0:T(8,128)(2,1)S(1)}, u32[]{:S(2)}, u32[]{:S(2)}) collective-permute-start(bf16[128,2048]{1,0:T(8,128)(2,1)S(1)} %fusion.6), channel_id=1, source_target_pairs={{0,4},{1,5},{2,6},{3,7},{4,0},{5,1},{6,2},{7,3},{8,12},{9,13},{10,... | collective-permute-start | bytes 1572872 | tf_op jit(solution)/shard_map/ppermute | solution.py:129
  (5 other events, 5.1 us)

commit v2 on v0

--- a/solution.py
+++ b/solution.py
@@ -1,20 +1,31 @@
+import functools
+
 import jax
 import jax.numpy as jnp
 from jax import lax
+from jax.experimental import pallas as pl
+from jax.experimental.pallas import tpu as pltpu
 from jax.sharding import PartitionSpec as P
 
 
-def body(hidden, norm_gain, routes, route_weight, w_gate, w_up, w_down):
+SMALL = pl.CostEstimate(flops=1, bytes_accessed=1, transcendentals=0)
+
+
+def normalise(hidden, norm_gain):
+    xf = hidden.astype(jnp.float32)
+    return (xf * lax.rsqrt(jnp.mean(xf * xf, axis=-1, keepdims=True) + 1e-06) * norm_gain).astype(
+        jnp.bfloat16
+    )
+
+
+def send_slots(hidden, norm_gain, routes, route_weight, w_gate, w_up, w_down):
     count = lax.axis_size("ep")
     tok = hidden.shape[0]
     width = hidden.shape[1]
     picks = routes.shape[1]
     experts = count * w_gate.shape[0]
     slots = tok * picks * 5 // (4 * experts)
-    xf = hidden.astype(jnp.float32)
-    normed = (xf * lax.rsqrt(jnp.mean(xf * xf, axis=-1, keepdims=True) + 1e-06) * norm_gain).astype(
-        jnp.bfloat16
-    )
+    normed = normalise(hidden, norm_gain)
     share = route_weight / jnp.sum(route_weight, axis=1, keepdims=True)
     flat = routes.reshape(-1)
     onehot = (flat[:, None] == jnp.arange(experts, dtype=jnp.int32)[None, :]).astype(jnp.int32)
@@ -37,6 +48,244 @@
     return mixed.astype(jnp.bfloat16)
 
 
+def prepare_kernel(*refs):
+    out, sems = refs[4], refs[9]
+    hidden, gain, routes, scores = refs[5:9]
+    copies = [pltpu.make_async_copy(refs[n], refs[5 + n], sems.at[n]) for n in range(4)]
+    for copy in copies:
+        copy.start()
+    for copy in copies:
+        copy.wait()
+    f32, bf16 = jnp.float32, jnp.bfloat16
+    tok, width = hidden.shape
+    x = hidden[...].astype(f32)
+    mean = jnp.mean(x * x, axis=-1, keepdims=True)
+    out[:, :width] = (x * lax.rsqrt(mean + 1e-06) * gain[...]).astype(bf16)
+    score = scores[...].T
+    share = score / jnp.sum(score, axis=1, keepdims=True)
+    names = routes[...].T
+    pad = out.shape[1] - width
+    lane = lax.broadcasted_iota(jnp.int32, (tok, pad), 1)
+    expert = lane % (pad // 2)
+    dense = jnp.zeros((tok, pad), f32)
+    for k in range(names.shape[1]):
+        dense += jnp.where(expert == names[:, k : k + 1], share[:, k : k + 1], 0.0)
+    high = dense.astype(bf16).astype(f32)
+    out[:, width:] = jnp.where(lane < pad // 2, high, dense - high).astype(bf16)
+
+
+def prepare(hidden, norm_gain, routes, route_weight):
+    tok, width = hidden.shape
+    arrays = (hidden, norm_gain.reshape(1, width), routes.T, route_weight.T)
+    return pl.pallas_call(
+        prepare_kernel,
+        in_specs=[pl.BlockSpec(memory_space=pltpu.HBM)] * 4,
+        out_specs=pl.BlockSpec(memory_space=pltpu.VMEM),
+        out_shape=jax.ShapeDtypeStruct((tok, width + 128), jnp.bfloat16),
+        scratch_shapes=[pltpu.VMEM(array.shape, array.dtype) for array in arrays]
+        + [pltpu.SemaphoreType.DMA((4,))],
+        compiler_params=pltpu.CompilerParams(vmem_limit_bytes=62 * 2**20),
+    )(*arrays)
+
+
+def hold_kernel(count, *refs):
+    token, sems = refs[-2:]
+    copies = [pltpu.make_async_copy(refs[n], refs[count + n], sems.at[n]) for n in range(count)]
+    for copy in copies:
+        copy.start()
+    token[...] = jnp.zeros(token.shape, token.dtype)
+    for copy in copies:
+        copy.wait()
+
+
+def hold(*arrays):
+    count = len(arrays)
+    *held, token = pl.pallas_call(
+        functools.partial(hold_kernel, count),
+        in_specs=[pl.BlockSpec(memory_space=pl.ANY)] * count,
+        out_specs=[pl.BlockSpec(memory_space=pltpu.VMEM)] * (count + 1),
+        out_shape=[pltpu.VMEM(array.shape, array.dtype) for array in arrays]
+        + [jax.ShapeDtypeStruct((8, 128), jnp.float32)],
+        scratch_shapes=[pltpu.SemaphoreType.DMA((count,))],
+        compiler_params=pltpu.CompilerParams(vmem_limit_bytes=2 * 2**20),
+        cost_estimate=SMALL,
+    )(*[pltpu.with_memory_space_constraint(array, pltpu.HBM) for array in arrays])
+    return held, token
+
+
+def again_kernel(array, after, out, sem):
+    del after
+    copy = pltpu.make_async_copy(array, out, sem)
+    copy.start()
+    copy.wait()
+
+
+def again(array, after):
+    anywhere = pl.BlockSpec(memory_space=pl.ANY)
+    return pl.pallas_call(
+        again_kernel,
+        in_specs=[anywhere] * 2,
+        out_specs=anywhere,
+        out_shape=jax.ShapeDtypeStruct(array.shape, array.dtype),
+        scratch_shapes=[pltpu.SemaphoreType.DMA],
+        compiler_params=pltpu.CompilerParams(vmem_limit_bytes=2**20),
+        cost_estimate=SMALL,
+    )(pltpu.with_memory_space_constraint(array, pltpu.HBM), after)
+
+
+def gate_kernel(*refs):
+    del refs
+
+
+def gate(through, after):
+    count = len(through)
+    anywhere = pl.BlockSpec(memory_space=pl.ANY)
+    return pl.pallas_call(
+        gate_kernel,
+        in_specs=[anywhere] * (count + len(after)),
+        out_specs=[anywhere] * count,
+        out_shape=[jax.ShapeDtypeStruct(array.shape, array.dtype) for array in through],
+        input_output_aliases={n: n for n in range(count)},
+        compiler_params=pltpu.CompilerParams(vmem_limit_bytes=2**20),
+        cost_estimate=SMALL,
+    )(*through, *after)
+
+
+def experts_kernel(pieces, tile, *refs):
+    me = lax.axis_index("ep")
+    line = me // 4
+    is_inner = (line == 1) | (line == 2)
+    blocks = []
+    for count in pieces:
+        blocks.append(refs[:count])
+        refs = refs[count:]
+    weights, refs = refs[:6], refs[6:]
+    outs, refs = refs[: len(pieces)], refs[len(pieces) :]
+    rows, total, sems = refs
+    width = outs[0].shape[1]
+    ff = weights[0].shape[2]
+    f32, bf16 = jnp.float32, jnp.bfloat16
+
+    def each_block(act):
+        at = 0
+        for p, block in enumerate(blocks):
+            size = block[0].shape[0]
+            for n, ref in enumerate(block):
+                copy = pltpu.make_async_copy(ref, rows.at[pl.ds(at, size)], sems.at[p, n])
+                if len(block) == 1:
+                    act(copy)
+                else:
+                    pl.when(is_inner if n == 0 else ~is_inner)(functools.partial(act, copy))
+            at += size
+
+    each_block(lambda copy: copy.start())
+    each_block(lambda copy: copy.wait())
+
+    shares = rows[:, width:].astype(f32)
+    half = shares.shape[1] // 2
+    lane = lax.broadcasted_iota(jnp.int32, shares.shape, 1) % half
+    x = rows[:, :width]
+    steps = ff // tile
+    for j in range(2):
+        wg, wu, wd = weights[3 * j : 3 * j + 3]
+        share = jnp.sum(jnp.where(lane == (me ^ j), shares, 0.0), axis=1, keepdims=True)
+        for t in range(steps):
+            some = pl.ds(t * tile, tile)
+            gate = jnp.dot(x, wg[0, :, some], preferred_element_type=f32)
+            upper = jnp.dot(x, wu[0, :, some], preferred_element_type=f32)
+            units = (gate / (1.0 + jnp.exp(-gate)) * upper * share).astype(bf16)
+            part = jnp.dot(units, wd[0, some, :], preferred_element_type=f32)
+            if j == 0 and t == 0:
+                total[...] = part
+            elif j == 0 or t < steps - 1:
+                total[...] += part
+            else:
+                done = (total[...] + part).astype(bf16)
+                at = 0
+                for out in outs:
+                    out[...] = done[at : at + out.shape[0]]
+                    at += out.shape[0]
+
+
+def run_experts(pieces, weights):
+    sizes = [piece[0].shape[0] for piece in pieces]
+    wide = pieces[0][0].shape[1]
+    _, width, ff = weights[0].shape
+    whole = sum(sizes)
+    blocks = [block for piece in pieces for block in piece]
+    vmem, anywhere = pl.BlockSpec(memory_space=pltpu.VMEM), pl.BlockSpec(memory_space=pl.ANY)
+    return pl.pallas_call(
+        functools.partial(experts_kernel, [len(piece) for piece in pieces], ff // 3),
+        in_specs=[anywhere] * len(blocks) + [vmem] * 6,
+        out_specs=[vmem] * len(pieces),
+        out_shape=[jax.ShapeDtypeStruct((size, width), jnp.bfloat16) for size in sizes],
+        scratch_shapes=[
+            pltpu.VMEM((whole, wide), jnp.bfloat16),
+            pltpu.VMEM((whole, width), jnp.float32),
+            pltpu.SemaphoreType.DMA((len(pieces), 2)),
+        ],
+        compiler_params=pltpu.CompilerParams(vmem_limit_bytes=20 * 2**20),
+        cost_estimate=SMALL,
+    )(*blocks, *weights)
+
+
+def gather_rows(hidden, norm_gain, routes, route_weight, w_gate, w_up, w_down):
+    count = lax.axis_size("ep")
+    f32, bf16 = jnp.float32, jnp.bfloat16
+    tie = lambda *arrays: lax.optimization_barrier(arrays)
+
+    def line(x, to):
+        moves = [(i, to[i // 4] * 4 + i % 4) for i in range(count) if to[i // 4] is not None]
+        return lax.ppermute(x, "ep", moves)
+
+    def cross(x, lines=(0, 1, 2, 3)):
+        return lax.ppermute(x, "ep", [(i, i ^ 2) for i in range(count) if i // 4 in lines])
+
+    def other_core(x):
+        return lax.ppermute(x, "ep", [(i, i ^ 1) for i in range(count)])
+
+    ends, inner = (0, 3), (1, 2)
+    pairs, middle = [1, 0, 3, 2], [None, 2, 1, None]
+    outward, inward = [None, 0, 3, None], [1, None, None, 2]
+
+    far_gate, far_up = other_core(w_gate), other_core(w_up)
+    own = prepare(hidden, norm_gain, routes, route_weight)
+
+    p1, n2, y0 = line(own, pairs), line(own, middle), cross(own)
+    weights, token = hold(w_gate, w_up, w_down)
+    p1, n2, y0, far_gate, far_up = gate([p1, n2, y0, far_gate, far_up], [token])
+
+    n4, n3, yn2 = line(p1, middle), line(n2, outward), cross(n2, inner)
+    far_down = other_core(again(w_down, p1))
+    held, token = hold(far_gate, far_up)
+    weights += held
+    n4, n3, yn2, far_down = gate([n4, n3, yn2, far_down], [token])
+
+    n5, yn3, yn4 = line(n4, outward), cross(n3, ends), cross(n4, inner)
+    held, token = hold(far_down)
+    weights += held
+    m0, o0 = run_experts([(own,), (y0,)], weights)
+    n5, yn3, yn4 = gate([n5, yn3, yn4], [o0])
+
+    yn5, y1 = cross(n5, ends), line(y0, pairs)
+    m3, o3 = run_experts([(n2, n3), (yn2, yn3)], weights)
+    yn5, y1 = gate([yn5, y1], [o3])
+    m4, o4 = run_experts([(n4, n5), (yn4, yn5)], weights)
+
+    def add(*parts):
+        return sum(p.astype(f32) for p in parts).astype(bf16)
+
+    o4 = cross(o4)
+    m1, o1 = run_experts([(p1,), (y1,)], weights)
+    o4, o3 = gate([o4, o3], [o1])
+    r4 = add(m4, o4)
+    r3 = add(m3, cross(o3))
+    r4 = add(r4, line(r4, inward))
+    r1 = add(m1, cross(o1), line(r4, middle))
+    r3 = add(r3, line(r3, inward))
+    return add(m0, cross(o0), line(r1, pairs), line(r3, middle))
+
+
 def solution(mesh):
     in_specs = (
         P(("group", "ep"), None),
@@ -48,4 +297,11 @@
         P("ep", None, None),
     )
     out_specs = P(("group", "ep"), None)
+
+    def body(hidden, norm_gain, routes, route_weight, w_gate, w_up, w_down):
+        count, tok, picks = mesh.shape["ep"], hidden.shape[0], routes.shape[1]
+        dense = count == 16 and w_gate.shape[0] == 1 and 2 * picks >= count
+        plan = gather_rows if dense else send_slots
+        return plan(hidden, norm_gain, routes, route_weight, w_gate, w_up, w_down)
+
     return jax.shard_map(body, mesh=mesh, in_specs=in_specs, out_specs=out_specs, check_vma=False)

time: 323 us -> 138 us (0.43)
  blocking collectives: 122 us -> 0 us
  waiting for transfers between devices: 115 us -> 59.3 us
  local copies, waits for them, and re-layouts: 52.1 us -> 1.64 us
  Pallas kernels: 0 us -> 37.2 us
  starting transfers between devices: 5.09 us -> 37 us
  matrix products: 18.6 us -> 0 us
  other arithmetic: 9.49 us -> 1.87 us
    all_to_all x1 -> x0, blocking collectives: 122 us -> none  [body(): lax.all_to_all(outgoing, 'ep', split_axis=0, concat_axis=0, tiled=True)]
    all_to_all x1 -> x0, waiting for transfers between devices: 115 us -> none  [body(): lax.all_to_all(result.reshape(arrived.shape), 'ep', split_axis=0, concat_...]
    ppermute x0 -> x23, waiting for transfers between devices: none -> 59.3 us  [the longest x11 38.1 us: line(): return lax.ppermute(x, 'ep', moves)]
    pallas_call x0 -> x14, Pallas kernels: none -> 37.2 us  [the longest x4 23.7 us: run_experts(): pl.pallas_call(functools.partial(experts_kernel, [len(piece) for piece in...]
    ppermute x0 -> x23, starting transfers between devices: none -> 37 us  [the longest x11 21.6 us: line(): return lax.ppermute(x, 'ep', moves)]
    gather x1 -> x0, local copies, waits for them, and re-layouts: 25.6 us -> none  [body(): picked = coming_back[flat, slot]]
    unnamed x10 -> x4, local copies, waits for them, and re-layouts: 24.7 us -> 1.64 us
    dot_general x4 -> x0, matrix products: 18.6 us -> none  [the longest x1 6.05 us: body(): jnp.dot(units, w_down[0], preferred_element_type=jnp.float32)]
  transfers between devices with their start and end apart: 1 -> 23, of which waited for: 1 -> 15; matrix products, arithmetic and copies ran while one was open for 0% -> 0% of each run, Pallas kernels for 0% -> 21%
where the time goes in v2:
time: 138 us; the launch traced here: 137 us
  waiting for transfers between devices  59.3 us (43%)
  Pallas kernels  37.2 us (27%)
  starting transfers between devices  37 us (27%)
  other arithmetic  1.87 us (1%)
  local copies, waits for them, and re-layouts  1.64 us (1%)
    ppermute x11, waiting for transfers between devices, line(): return lax.ppermute(x, 'ep', moves)  38.1 us
    pallas_call x4, Pallas kernels, run_experts(): pl.pallas_call(functools.partial(experts_kernel, [len(piece) for piece in...  23.7 us
    ppermute x11, starting transfers between devices, line(): return lax.ppermute(x, 'ep', moves)  21.6 us
    ppermute x9, waiting for transfers between devices, cross(): lax.ppermute(x, 'ep', [(i, i ^ 2) for i in range(count) if i // 4 in lines])  21.2 us
    ppermute x9, starting transfers between devices, cross(): lax.ppermute(x, 'ep', [(i, i ^ 2) for i in range(count) if i // 4 in lines])  14.8 us
    pallas_call x3, Pallas kernels, hold(): pl.pallas_call(functools.partial(hold_kernel, count), in_specs=[pl.BlockS...  9.14 us
  transfers between devices with their start and end apart: 23, of which 15 were waited for; matrix products, arithmetic and copies ran while one was open for 0% of the time, Pallas kernels for 21%

profile of v2, /device:TPU:18, one launch (start us, length us, event | category | flops | bytes accessed | tf_op | source)
XLA Modules:
  0.0 137.2 jit_solution(9509840784962135962)
XLA Ops:
  0.5 2.5 %shard_map.73.refs_0_ = bf16[128,2176]{1,0:T(8,128)(2,1)} custom-call(bf16[128,2048]{1,0:T(8,128)(2,1)} %refs_0_.2, f32[1,2048]{1,0:T(1,128)} %bitcast.3, s32[8,128]{1,0:T(8,128)} %bitcast.4, f32[8,128]{1,0:T(8,128)} %bitcast.5), custom_call_target="tpu_custom_call" | custom-call | tf_op jit(solution)/shard_map/pallas_call | solution.py:80
  3.0 1.6 %collective-permute-start = (bf16[128,2176]{1,0:T(8,128)(2,1)}, bf16[128,2176]{1,0:T(8,128)(2,1)S(1)}, u32[]{:S(2)}, u32[]{:S(2)}) collective-permute-start(bf16[128,2176]{1,0:T(8,128)(2,1)} %shard_map.73.refs_0_), channel_id=1, source_target_pairs={{0,4},{1,5},{2,6},{3,7},{4,0},{5,1},{6,2},{7,3},{8,12},{9,13},{10,... | collective-permute-start | bytes 1671176 | tf_op jit(solution)/shard_map/ppermute | solution.py:239
  4.6 1.9 %collective-permute-start.1 = (bf16[128,2176]{1,0:T(8,128)(2,1)}, bf16[128,2176]{1,0:T(8,128)(2,1)S(1)}, u32[]{:S(2)}, u32[]{:S(2)}) collective-permute-start(bf16[128,2176]{1,0:T(8,128)(2,1)} %shard_map.73.refs_0_), channel_id=1, source_target_pairs={{4,8},{5,9},{6,10},{7,11},{8,4},{9,5},{10,6},{11,7},{20,24},{21,25... | collective-permute-start | bytes 1671176 | tf_op jit(solution)/shard_map/ppermute | solution.py:239
  6.6 1.6 %collective-permute-start.2 = (bf16[128,2176]{1,0:T(8,128)(2,1)}, bf16[128,2176]{1,0:T(8,128)(2,1)S(1)}, u32[]{:S(2)}, u32[]{:S(2)}) collective-permute-start(bf16[128,2176]{1,0:T(8,128)(2,1)} %shard_map.73.refs_0_), channel_id=1, source_target_pairs={{0,2},{1,3},{2,0},{3,1},{4,6},{5,7},{6,4},{7,5},{8,10},{9,11},{10,... | collective-permute-start | bytes 1671176 | tf_op jit(solution)/shard_map/ppermute | solution.py:242
  8.1 3.8 %shard_map.74 = (bf16[1,2048,768]{2,1,0:T(8,128)(2,1)S(1)}, bf16[1,2048,768]{2,1,0:T(8,128)(2,1)S(1)}, bf16[1,768,2048]{2,1,0:T(8,128)(2,1)S(1)}, f32[8,128]{1,0:T(8,128)S(1)}) custom-call(bf16[1,2048,768]{2,1,0:T(8,128)(2,1)} %refs_0_.3, bf16[1,2048,768]{2,1,0:T(8,128)(2,1)} %refs_1_.1, bf16[1,768,2048]{2,1,0:T(8,128)(2,1)} %array.1), custom_call_target="tpu_custom_call" | custom-call | flops 1 | bytes 1 | tf_op jit(solution)/shard_map/pallas_call | solution.py:103
  11.9 5.9 %collective-permute-done.refs_0_ = bf16[128,2176]{1,0:T(8,128)(2,1)S(1)} collective-permute-done((bf16[128,2176]{1,0:T(8,128)(2,1)}, bf16[128,2176]{1,0:T(8,128)(2,1)S(1)}, u32[]{:S(2)}, u32[]{:S(2)}) %collective-permute-start) | collective-permute-done | bytes 557088 | tf_op jit(solution)/shard_map/ppermute | solution.py:239
  17.8 3.2 %collective-permute-done.1.refs_1_ = bf16[128,2176]{1,0:T(8,128)(2,1)S(1)} collective-permute-done((bf16[128,2176]{1,0:T(8,128)(2,1)}, bf16[128,2176]{1,0:T(8,128)(2,1)S(1)}, u32[]{:S(2)}, u32[]{:S(2)}) %collective-permute-start.1) | collective-permute-done | bytes 557088 | tf_op jit(solution)/shard_map/ppermute | solution.py:239
  21.1 1.9 %shard_map.77 = bf16[1,768,2048]{2,1,0:T(8,128)(2,1)S(1)} custom-call(bf16[1,768,2048]{2,1,0:T(8,128)(2,1)} %array.1, bf16[128,2176]{1,0:T(8,128)(2,1)S(1)} %get-tuple-element.46.after.refs_0_), custom_call_target="tpu_custom_call" | custom-call | flops 1 | bytes 1 | tf_op jit(solution)/shard_map/pallas_call | solution.py:125
  23.1 3.6 %collective-permute-start.5 = (bf16[128,2176]{1,0:T(8,128)(2,1)S(1)}, bf16[128,2176]{1,0:T(8,128)(2,1)S(1)}, u32[]{:S(2)}, u32[]{:S(2)}) collective-permute-start(bf16[128,2176]{1,0:T(8,128)(2,1)S(1)} %get-tuple-element.46.after.refs_0_), channel_id=1, source_target_pairs={{4,8},{5,9},{6,10},{7,11},{8,4},{9,5},{10,6},{11,7},{20,24},{21,25... | collective-permute-start | bytes 1671176 | tf_op jit(solution)/shard_map/ppermute | solution.py:239
  28.1 3.4 %collective-permute-start.7 = (bf16[128,2176]{1,0:T(8,128)(2,1)S(1)}, bf16[128,2176]{1,0:T(8,128)(2,1)S(1)}, u32[]{:S(2)}, u32[]{:S(2)}) collective-permute-start(bf16[128,2176]{1,0:T(8,128)(2,1)S(1)} %get-tuple-element.47.refs_0_), channel_id=1, source_target_pairs={{4,6},{5,7},{6,4},{7,5},{8,10},{9,11},{10,8},{11,9},{20,22},{21,23... | collective-permute-start | bytes 1671176 | tf_op jit(solution)/shard_map/ppermute | solution.py:242
  31.5 2.9 %shard_map.76 = (bf16[1,2048,768]{2,1,0:T(8,128)(2,1)S(1)}, bf16[1,2048,768]{2,1,0:T(8,128)(2,1)S(1)}, f32[8,128]{1,0:T(8,128)S(1)}) custom-call(bf16[1,2048,768]{2,1,0:T(8,128)(2,1)} %get-tuple-element.42.refs_0_, bf16[1,2048,768]{2,1,0:T(8,128)(2,1)} %get-tuple-element.43.refs_1_), custom_call_target="tpu_custom_call" | custom-call | flops 1 | bytes 1 | tf_op jit(solution)/shard_map/pallas_call | solution.py:103
  34.4 5.6 %collective-permute-done.5.refs_0_ = bf16[128,2176]{1,0:T(8,128)(2,1)S(1)} collective-permute-done((bf16[128,2176]{1,0:T(8,128)(2,1)S(1)}, bf16[128,2176]{1,0:T(8,128)(2,1)S(1)}, u32[]{:S(2)}, u32[]{:S(2)}) %collective-permute-start.5) | collective-permute-done | bytes 557088 | tf_op jit(solution)/shard_map/ppermute | solution.py:239
  40.6 4.1 %collective-permute-done.7.refs_2_ = bf16[128,2176]{1,0:T(8,128)(2,1)S(1)} collective-permute-done((bf16[128,2176]{1,0:T(8,128)(2,1)S(1)}, bf16[128,2176]{1,0:T(8,128)(2,1)S(1)}, u32[]{:S(2)}, u32[]{:S(2)}) %collective-permute-start.7) | collective-permute-done | bytes 557088 | tf_op jit(solution)/shard_map/ppermute | solution.py:242
  44.7 1.6 %copy-done = bf16[1,768,2048]{2,1,0:T(8,128)(2,1)} copy-done((bf16[1,768,2048]{2,1,0:T(8,128)(2,1)}, bf16[1,768,2048]{2,1,0:T(8,128)(2,1)S(1)}, u32[]{:S(2)}) %copy-start) | copy-done | bytes 3145752
  48.4 3.4 %collective-permute-start.12 = (bf16[128,2176]{1,0:T(8,128)(2,1)S(1)}, bf16[128,2176]{1,0:T(8,128)(2,1)S(1)}, u32[]{:S(2)}, u32[]{:S(2)}) collective-permute-start(bf16[128,2176]{1,0:T(8,128)(2,1)S(1)} %get-tuple-element.53.refs_0_), channel_id=1, source_target_pairs={{4,6},{5,7},{6,4},{7,5},{8,10},{9,11},{10,8},{11,9},{20,22},{21,23... | collective-permute-start | bytes 1671176 | tf_op jit(solution)/shard_map/ppermute | solution.py:242
  51.9 2.5 %shard_map.79 = (bf16[1,768,2048]{2,1,0:T(8,128)(2,1)S(1)}, f32[8,128]{1,0:T(8,128)}) custom-call(bf16[1,768,2048]{2,1,0:T(8,128)(2,1)} %copy-done), custom_call_target="tpu_custom_call" | custom-call | flops 1 | bytes 1 | tf_op jit(solution)/shard_map/pallas_call | solution.py:103
  54.4 5.9 %shard_map.80 = (bf16[128,2048]{1,0:T(8,128)(2,1)S(1)}, bf16[128,2048]{1,0:T(8,128)(2,1)S(1)}) custom-call(bf16[128,2176]{1,0:T(8,128)(2,1)S(1)} %copy-done.1, bf16[128,2176]{1,0:T(8,128)(2,1)S(1)} %get-tuple-element.38.refs_1_, bf16[1,2048,768]{2,1,0:T(8,128)(2,1)S(1)} %get-tuple-element.39.refs_2_.refs_4_, ...), custom_call_target="tpu_custom_call" | custom-call | flops 1 | bytes 1 | tf_op jit(solution)/shard_map/pallas_call | solution.py:217
  60.7 3.5 %collective-permute-done.12.refs_2_ = bf16[128,2176]{1,0:T(8,128)(2,1)S(1)} collective-permute-done((bf16[128,2176]{1,0:T(8,128)(2,1)S(1)}, bf16[128,2176]{1,0:T(8,128)(2,1)S(1)}, u32[]{:S(2)}, u32[]{:S(2)}) %collective-permute-start.12) | collective-permute-done | bytes 557088 | tf_op jit(solution)/shard_map/ppermute | solution.py:242
  64.9 5.9 %shard_map.82 = (bf16[128,2048]{1,0:T(8,128)(2,1)S(1)}, bf16[128,2048]{1,0:T(8,128)(2,1)S(1)}) custom-call(bf16[128,2176]{1,0:T(8,128)(2,1)S(1)} %get-tuple-element.47.refs_0_, bf16[128,2176]{1,0:T(8,128)(2,1)S(1)} %get-tuple-element.54.refs_1_, bf16[128,2176]{1,0:T(8,128)(2,1)S(1)} %get-tuple-element.56.refs_2_, ...), custom_call_target="tpu_custom_call" | custom-call | flops 1 | bytes 1 | tf_op jit(solution)/shard_map/pallas_call | solution.py:217
  71.3 6.0 %shard_map.85 = (bf16[128,2048]{1,0:T(8,128)(2,1)S(1)}, bf16[128,2048]{1,0:T(8,128)(2,1)S(1)}) custom-call(bf16[128,2176]{1,0:T(8,128)(2,1)S(1)} %get-tuple-element.53.refs_0_, bf16[128,2176]{1,0:T(8,128)(2,1)S(1)} %get-tuple-element.55.refs_1_, bf16[128,2176]{1,0:T(8,128)(2,1)S(1)} %get-tuple-element.62.refs_2_, ...), custom_call_target="tpu_custom_call" | custom-call | flops 1 | bytes 1 | tf_op jit(solution)/shard_map/pallas_call | solution.py:217
  77.3 1.6 %collective-permute-start.16 = (bf16[128,2048]{1,0:T(8,128)(2,1)S(1)}, bf16[128,2048]{1,0:T(8,128)(2,1)S(1)}, u32[]{:S(2)}, u32[]{:S(2)}) collective-permute-start(bf16[128,2048]{1,0:T(8,128)(2,1)S(1)} %get-tuple-element.65), channel_id=1, source_target_pairs={{0,2},{1,3},{2,0},{3,1},{4,6},{5,7},{6,4},{7,5},{8,10},{9,11},{10,... | collective-permute-start | bytes 1572872 | tf_op jit(solution)/shard_map/ppermute | solution.py:242
  78.9 5.9 %shard_map.84 = (bf16[128,2048]{1,0:T(8,128)(2,1)S(1)}, bf16[128,2048]{1,0:T(8,128)(2,1)S(1)}) custom-call(bf16[128,2176]{1,0:T(8,128)(2,1)S(1)} %get-tuple-element.46.after.refs_0_, bf16[128,2176]{1,0:T(8,128)(2,1)S(1)} %get-tuple-element.59.refs_1_, bf16[1,2048,768]{2,1,0:T(8,128)(2,1)S(1)} %get-tuple-element.39.refs_2_.refs_4_, ...), custom_call_target="tpu_custom_call" | custom-call | flops 1 | bytes 1 | tf_op jit(solution)/shard_map/pallas_call | solution.py:217
  84.8 5.2 %collective-permute-done.16.refs_0_ = bf16[128,2048]{1,0:T(8,128)(2,1)S(1)} collective-permute-done((bf16[128,2048]{1,0:T(8,128)(2,1)S(1)}, bf16[128,2048]{1,0:T(8,128)(2,1)S(1)}, u32[]{:S(2)}, u32[]{:S(2)}) %collective-permute-start.16) | collective-permute-done | bytes 524320 | tf_op jit(solution)/shard_map/ppermute | solution.py:242
  91.4 1.6 %collective-permute-start.20 = (bf16[128,2048]{1,0:T(8,128)(2,1)S(1)}, bf16[128,2048]{1,0:T(8,128)(2,1)S(1)}, u32[]{:S(2)}, u32[]{:S(2)}) collective-permute-start(bf16[128,2048]{1,0:T(8,128)(2,1)S(1)} %get-tuple-element.68), channel_id=1, source_target_pairs={{0,2},{1,3},{2,0},{3,1},{4,6},{5,7},{6,4},{7,5},{8,10},{9,11},{10,... | collective-permute-start | bytes 1572872 | tf_op jit(solution)/shard_map/ppermute | solution.py:242
  93.5 10.8 %collective-permute-done.17 = bf16[128,2048]{1,0:T(8,128)(2,1)S(1)} collective-permute-done((bf16[128,2048]{1,0:T(8,128)(2,1)S(1)}, bf16[128,2048]{1,0:T(8,128)(2,1)S(1)}, u32[]{:S(2)}, u32[]{:S(2)}) %collective-permute-start.17) | collective-permute-done | bytes 524320 | tf_op jit(solution)/shard_map/ppermute | solution.py:239
  104.4 2.2 %collective-permute-start.18 = (bf16[128,2048]{1,0:T(8,128)(2,1)S(1)}, bf16[128,2048]{1,0:T(8,128)(2,1)S(1)}, u32[]{:S(2)}, u32[]{:S(2)}) collective-permute-start(bf16[128,2048]{1,0:T(8,128)(2,1)S(1)} %add_convert_fusion.4), channel_id=1, source_target_pairs={{4,8},{5,9},{6,10},{7,11},{8,4},{9,5},{10,6},{11,7},{20,24},{21,25... | collective-permute-start | bytes 1572872 | tf_op jit(solution)/shard_map/ppermute | solution.py:239
  109.4 8.2 %collective-permute-done.15 = bf16[128,2048]{1,0:T(8,128)(2,1)S(1)} collective-permute-done((bf16[128,2048]{1,0:T(8,128)(2,1)S(1)}, bf16[128,2048]{1,0:T(8,128)(2,1)S(1)}, u32[]{:S(2)}, u32[]{:S(2)}) %collective-permute-start.15) | collective-permute-done | bytes 524320 | tf_op jit(solution)/shard_map/ppermute | solution.py:242
  117.8 4.7 %collective-permute-start.19 = (bf16[128,2048]{1,0:T(8,128)(2,1)S(1)}, bf16[128,2048]{1,0:T(8,128)(2,1)S(1)}, u32[]{:S(2)}, u32[]{:S(2)}) collective-permute-start(bf16[128,2048]{1,0:T(8,128)(2,1)S(1)} %add_convert_fusion.3), channel_id=1, source_target_pairs={{0,4},{1,5},{2,6},{3,7},{4,0},{5,1},{6,2},{7,3},{8,12},{9,13},{10,... | collective-permute-start | bytes 1572872 | tf_op jit(solution)/shard_map/ppermute | solution.py:239
  122.5 2.4 %collective-permute-done.21 = bf16[128,2048]{1,0:T(8,128)(2,1)S(1)} collective-permute-done((bf16[128,2048]{1,0:T(8,128)(2,1)S(1)}, bf16[128,2048]{1,0:T(8,128)(2,1)S(1)}, u32[]{:S(2)}, u32[]{:S(2)}) %collective-permute-start.21) | collective-permute-done | bytes 524320 | tf_op jit(solution)/shard_map/ppermute | solution.py:239
  125.0 2.2 %collective-permute-start.22 = (bf16[128,2048]{1,0:T(8,128)(2,1)S(1)}, bf16[128,2048]{1,0:T(8,128)(2,1)S(1)}, u32[]{:S(2)}, u32[]{:S(2)}) collective-permute-start(bf16[128,2048]{1,0:T(8,128)(2,1)S(1)} %add_convert_fusion.1), channel_id=1, source_target_pairs={{4,8},{5,9},{6,10},{7,11},{8,4},{9,5},{10,6},{11,7},{20,24},{21,25... | collective-permute-start | bytes 1572872 | tf_op jit(solution)/shard_map/ppermute | solution.py:239
  127.3 3.5 %collective-permute-done.19 = bf16[128,2048]{1,0:T(8,128)(2,1)S(1)} collective-permute-done((bf16[128,2048]{1,0:T(8,128)(2,1)S(1)}, bf16[128,2048]{1,0:T(8,128)(2,1)S(1)}, u32[]{:S(2)}, u32[]{:S(2)}) %collective-permute-start.19) | collective-permute-done | bytes 524320 | tf_op jit(solution)/shard_map/ppermute | solution.py:239
  130.8 5.3 %collective-permute-done.22 = bf16[128,2048]{1,0:T(8,128)(2,1)S(1)} collective-permute-done((bf16[128,2048]{1,0:T(8,128)(2,1)S(1)}, bf16[128,2048]{1,0:T(8,128)(2,1)S(1)}, u32[]{:S(2)}, u32[]{:S(2)}) %collective-permute-start.22) | collective-permute-done | bytes 524320 | tf_op jit(solution)/shard_map/ppermute | solution.py:239
  (38 shorter events, 12.5 us)
Async XLA Ops:
  0.0 21.1 %collective-permute-start.3 = (bf16[1,2048,768]{2,1,0:T(8,128)(2,1)}, bf16[1,2048,768]{2,1,0:T(8,128)(2,1)}, u32[]{:S(2)}, u32[]{:S(2)}) collective-permute-start(bf16[1,2048,768]{2,1,0:T(8,128)(2,1)} %refs_0_.3), channel_id=1, source_target_pairs={{0,1},{1,0},{2,3},{3,2},{4,5},{5,4},{6,7},{7,6},{8,9},{9,8},{10,11... | collective-permute-start | bytes 9437192 | tf_op jit(solution)/shard_map/ppermute | solution.py:245
  0.0 21.1 %collective-permute-start.4 = (bf16[1,2048,768]{2,1,0:T(8,128)(2,1)}, bf16[1,2048,768]{2,1,0:T(8,128)(2,1)}, u32[]{:S(2)}, u32[]{:S(2)}) collective-permute-start(bf16[1,2048,768]{2,1,0:T(8,128)(2,1)} %refs_1_.1), channel_id=1, source_target_pairs={{0,1},{1,0},{2,3},{3,2},{4,5},{5,4},{6,7},{7,6},{8,9},{9,8},{10,11... | collective-permute-start | bytes 9437192 | tf_op jit(solution)/shard_map/ppermute | solution.py:245
  3.0 14.8 %collective-permute-start = (bf16[128,2176]{1,0:T(8,128)(2,1)}, bf16[128,2176]{1,0:T(8,128)(2,1)S(1)}, u32[]{:S(2)}, u32[]{:S(2)}) collective-permute-start(bf16[128,2176]{1,0:T(8,128)(2,1)} %shard_map.73.refs_0_), channel_id=1, source_target_pairs={{0,4},{1,5},{2,6},{3,7},{4,0},{5,1},{6,2},{7,3},{8,12},{9,13},{10,... | collective-permute-start | bytes 1671176 | tf_op jit(solution)/shard_map/ppermute | solution.py:239
  4.6 16.3 %collective-permute-start.1 = (bf16[128,2176]{1,0:T(8,128)(2,1)}, bf16[128,2176]{1,0:T(8,128)(2,1)S(1)}, u32[]{:S(2)}, u32[]{:S(2)}) collective-permute-start(bf16[128,2176]{1,0:T(8,128)(2,1)} %shard_map.73.refs_0_), channel_id=1, source_target_pairs={{4,8},{5,9},{6,10},{7,11},{8,4},{9,5},{10,6},{11,7},{20,24},{21,25... | collective-permute-start | bytes 1671176 | tf_op jit(solution)/shard_map/ppermute | solution.py:239
  6.6 14.5 %collective-permute-start.2 = (bf16[128,2176]{1,0:T(8,128)(2,1)}, bf16[128,2176]{1,0:T(8,128)(2,1)S(1)}, u32[]{:S(2)}, u32[]{:S(2)}) collective-permute-start(bf16[128,2176]{1,0:T(8,128)(2,1)} %shard_map.73.refs_0_), channel_id=1, source_target_pairs={{0,2},{1,3},{2,0},{3,1},{4,6},{5,7},{6,4},{7,5},{8,10},{9,11},{10,... | collective-permute-start | bytes 1671176 | tf_op jit(solution)/shard_map/ppermute | solution.py:242
  23.0 21.7 %collective-permute-start.8 = (bf16[1,768,2048]{2,1,0:T(8,128)(2,1)S(1)}, bf16[1,768,2048]{2,1,0:T(8,128)(2,1)S(1)}, u32[]{:S(2)}, u32[]{:S(2)}) collective-permute-start(bf16[1,768,2048]{2,1,0:T(8,128)(2,1)S(1)} %shard_map.77), channel_id=1, source_target_pairs={{0,1},{1,0},{2,3},{3,2},{4,5},{5,4},{6,7},{7,6},{8,9},{9,8},{10,11... | collective-permute-start | bytes 9437192 | tf_op jit(solution)/shard_map/ppermute | solution.py:245
  23.1 16.9 %collective-permute-start.5 = (bf16[128,2176]{1,0:T(8,128)(2,1)S(1)}, bf16[128,2176]{1,0:T(8,128)(2,1)S(1)}, u32[]{:S(2)}, u32[]{:S(2)}) collective-permute-start(bf16[128,2176]{1,0:T(8,128)(2,1)S(1)} %get-tuple-element.46.after.refs_0_), channel_id=1, source_target_pairs={{4,8},{5,9},{6,10},{7,11},{8,4},{9,5},{10,6},{11,7},{20,24},{21,25... | collective-permute-start | bytes 1671176 | tf_op jit(solution)/shard_map/ppermute | solution.py:239
  26.7 13.8 %collective-permute-start.6 = (bf16[128,2176]{1,0:T(8,128)(2,1)S(1)}, bf16[128,2176]{1,0:T(8,128)(2,1)S(1)}, u32[]{:S(2)}, u32[]{:S(2)}) collective-permute-start(bf16[128,2176]{1,0:T(8,128)(2,1)S(1)} %get-tuple-element.47.refs_0_), channel_id=1, source_target_pairs={{4,0},{5,1},{6,2},{7,3},{8,12},{9,13},{10,14},{11,15},{20,16},{21,... | collective-permute-start | bytes 1671176 | tf_op jit(solution)/shard_map/ppermute | solution.py:239
  28.1 16.6 %collective-permute-start.7 = (bf16[128,2176]{1,0:T(8,128)(2,1)S(1)}, bf16[128,2176]{1,0:T(8,128)(2,1)S(1)}, u32[]{:S(2)}, u32[]{:S(2)}) collective-permute-start(bf16[128,2176]{1,0:T(8,128)(2,1)S(1)} %get-tuple-element.47.refs_0_), channel_id=1, source_target_pairs={{4,6},{5,7},{6,4},{7,5},{8,10},{9,11},{10,8},{11,9},{20,22},{21,23... | collective-permute-start | bytes 1671176 | tf_op jit(solution)/shard_map/ppermute | solution.py:242
  44.7 9.7 %copy-start.1 = (bf16[128,2176]{1,0:T(8,128)(2,1)S(1)}, bf16[128,2176]{1,0:T(8,128)(2,1)}, u32[]{:S(2)}) copy-start(bf16[128,2176]{1,0:T(8,128)(2,1)} %shard_map.73.refs_0_) | copy-start | bytes 1671172
  44.7 1.6 %copy-start = (bf16[1,768,2048]{2,1,0:T(8,128)(2,1)}, bf16[1,768,2048]{2,1,0:T(8,128)(2,1)S(1)}, u32[]{:S(2)}) copy-start(bf16[1,768,2048]{2,1,0:T(8,128)(2,1)S(1)} %get-tuple-element.49.refs_0_) | copy-start | bytes 9437188
  46.3 14.3 %collective-permute-start.10 = (bf16[128,2176]{1,0:T(8,128)(2,1)S(1)}, bf16[128,2176]{1,0:T(8,128)(2,1)S(1)}, u32[]{:S(2)}, u32[]{:S(2)}) collective-permute-start(bf16[128,2176]{1,0:T(8,128)(2,1)S(1)} %get-tuple-element.53.refs_0_), channel_id=1, source_target_pairs={{4,0},{5,1},{6,2},{7,3},{8,12},{9,13},{10,14},{11,15},{20,16},{21,... | collective-permute-start | bytes 1671176 | tf_op jit(solution)/shard_map/ppermute | solution.py:239
  47.7 13.0 %collective-permute-start.11 = (bf16[128,2176]{1,0:T(8,128)(2,1)S(1)}, bf16[128,2176]{1,0:T(8,128)(2,1)S(1)}, u32[]{:S(2)}, u32[]{:S(2)}) collective-permute-start(bf16[128,2176]{1,0:T(8,128)(2,1)S(1)} %get-tuple-element.54.refs_1_), channel_id=1, source_target_pairs={{0,2},{1,3},{2,0},{3,1},{12,14},{13,15},{14,12},{15,13},{16,18},{1... | collective-permute-start | bytes 1671176 | tf_op jit(solution)/shard_map/ppermute | solution.py:242
  48.4 15.8 %collective-permute-start.12 = (bf16[128,2176]{1,0:T(8,128)(2,1)S(1)}, bf16[128,2176]{1,0:T(8,128)(2,1)S(1)}, u32[]{:S(2)}, u32[]{:S(2)}) collective-permute-start(bf16[128,2176]{1,0:T(8,128)(2,1)S(1)} %get-tuple-element.53.refs_0_), channel_id=1, source_target_pairs={{4,6},{5,7},{6,4},{7,5},{8,10},{9,11},{10,8},{11,9},{20,22},{21,23... | collective-permute-start | bytes 1671176 | tf_op jit(solution)/shard_map/ppermute | solution.py:242
  51.8 19.5 %collective-permute-start.14 = (bf16[128,2176]{1,0:T(8,128)(2,1)S(1)}, bf16[128,2176]{1,0:T(8,128)(2,1)S(1)}, u32[]{:S(2)}, u32[]{:S(2)}) collective-permute-start(bf16[128,2176]{1,0:T(8,128)(2,1)S(1)} %get-tuple-element.38.refs_1_), channel_id=1, source_target_pairs={{0,4},{1,5},{2,6},{3,7},{4,0},{5,1},{6,2},{7,3},{8,12},{9,13},{10,... | collective-permute-start | bytes 1671176 | tf_op jit(solution)/shard_map/ppermute | solution.py:239
  64.2 7.1 %collective-permute-start.13 = (bf16[128,2176]{1,0:T(8,128)(2,1)S(1)}, bf16[128,2176]{1,0:T(8,128)(2,1)S(1)}, u32[]{:S(2)}, u32[]{:S(2)}) collective-permute-start(bf16[128,2176]{1,0:T(8,128)(2,1)S(1)} %get-tuple-element.55.refs_1_), channel_id=1, source_target_pairs={{0,2},{1,3},{2,0},{3,1},{12,14},{13,15},{14,12},{15,13},{16,18},{1... | collective-permute-start | bytes 1671176 | tf_op jit(solution)/shard_map/ppermute | solution.py:242
  77.3 12.7 %collective-permute-start.16 = (bf16[128,2048]{1,0:T(8,128)(2,1)S(1)}, bf16[128,2048]{1,0:T(8,128)(2,1)S(1)}, u32[]{:S(2)}, u32[]{:S(2)}) collective-permute-start(bf16[128,2048]{1,0:T(8,128)(2,1)S(1)} %get-tuple-element.65), channel_id=1, source_target_pairs={{0,2},{1,3},{2,0},{3,1},{4,6},{5,7},{6,4},{7,5},{8,10},{9,11},{10,... | collective-permute-start | bytes 1572872 | tf_op jit(solution)/shard_map/ppermute | solution.py:242
  90.1 14.1 %collective-permute-start.17 = (bf16[128,2048]{1,0:T(8,128)(2,1)S(1)}, bf16[128,2048]{1,0:T(8,128)(2,1)S(1)}, u32[]{:S(2)}, u32[]{:S(2)}) collective-permute-start(bf16[128,2048]{1,0:T(8,128)(2,1)S(1)} %add_convert_fusion.5), channel_id=1, source_target_pairs={{0,4},{1,5},{2,6},{3,7},{12,8},{13,9},{14,10},{15,11},{16,20},{17,... | collective-permute-start | bytes 1572872 | tf_op jit(solution)/shard_map/ppermute | solution.py:239
  91.4 15.2 %collective-permute-start.20 = (bf16[128,2048]{1,0:T(8,128)(2,1)S(1)}, bf16[128,2048]{1,0:T(8,128)(2,1)S(1)}, u32[]{:S(2)}, u32[]{:S(2)}) collective-permute-start(bf16[128,2048]{1,0:T(8,128)(2,1)S(1)} %get-tuple-element.68), channel_id=1, source_target_pairs={{0,2},{1,3},{2,0},{3,1},{4,6},{5,7},{6,4},{7,5},{8,10},{9,11},{10,... | collective-permute-start | bytes 1572872 | tf_op jit(solution)/shard_map/ppermute | solution.py:242
  93.0 24.6 %collective-permute-start.15 = (bf16[128,2048]{1,0:T(8,128)(2,1)S(1)}, bf16[128,2048]{1,0:T(8,128)(2,1)S(1)}, u32[]{:S(2)}, u32[]{:S(2)}) collective-permute-start(bf16[128,2048]{1,0:T(8,128)(2,1)S(1)} %get-tuple-element.61.refs_2_), channel_id=1, source_target_pairs={{0,2},{1,3},{2,0},{3,1},{4,6},{5,7},{6,4},{7,5},{8,10},{9,11},{10,... | collective-permute-start | bytes 1572872 | tf_op jit(solution)/shard_map/ppermute | solution.py:242
  104.4 13.2 %collective-permute-start.18 = (bf16[128,2048]{1,0:T(8,128)(2,1)S(1)}, bf16[128,2048]{1,0:T(8,128)(2,1)S(1)}, u32[]{:S(2)}, u32[]{:S(2)}) collective-permute-start(bf16[128,2048]{1,0:T(8,128)(2,1)S(1)} %add_convert_fusion.4), channel_id=1, source_target_pairs={{4,8},{5,9},{6,10},{7,11},{8,4},{9,5},{10,6},{11,7},{20,24},{21,25... | collective-permute-start | bytes 1572872 | tf_op jit(solution)/shard_map/ppermute | solution.py:239
  106.7 18.2 %collective-permute-start.21 = (bf16[128,2048]{1,0:T(8,128)(2,1)S(1)}, bf16[128,2048]{1,0:T(8,128)(2,1)S(1)}, u32[]{:S(2)}, u32[]{:S(2)}) collective-permute-start(bf16[128,2048]{1,0:T(8,128)(2,1)S(1)} %add_convert_fusion.2), channel_id=1, source_target_pairs={{0,4},{1,5},{2,6},{3,7},{12,8},{13,9},{14,10},{15,11},{16,20},{17,... | collective-permute-start | bytes 1572872 | tf_op jit(solution)/shard_map/ppermute | solution.py:239
  108.0 19.2 %collective-permute-start.9 = (bf16[128,2048]{1,0:T(8,128)(2,1)S(1)}, bf16[128,2048]{1,0:T(8,128)(2,1)S(1)}, u32[]{:S(2)}, u32[]{:S(2)}) collective-permute-start(bf16[128,2048]{1,0:T(8,128)(2,1)S(1)} %get-tuple-element.52.refs_3_), channel_id=1, source_target_pairs={{0,2},{1,3},{2,0},{3,1},{4,6},{5,7},{6,4},{7,5},{8,10},{9,11},{10,... | collective-permute-start | bytes 1572872 | tf_op jit(solution)/shard_map/ppermute | solution.py:242
  117.8 13.0 %collective-permute-start.19 = (bf16[128,2048]{1,0:T(8,128)(2,1)S(1)}, bf16[128,2048]{1,0:T(8,128)(2,1)S(1)}, u32[]{:S(2)}, u32[]{:S(2)}) collective-permute-start(bf16[128,2048]{1,0:T(8,128)(2,1)S(1)} %add_convert_fusion.3), channel_id=1, source_target_pairs={{0,4},{1,5},{2,6},{3,7},{4,0},{5,1},{6,2},{7,3},{8,12},{9,13},{10,... | collective-permute-start | bytes 1572872 | tf_op jit(solution)/shard_map/ppermute | solution.py:239
  125.0 11.1 %collective-permute-start.22 = (bf16[128,2048]{1,0:T(8,128)(2,1)S(1)}, bf16[128,2048]{1,0:T(8,128)(2,1)S(1)}, u32[]{:S(2)}, u32[]{:S(2)}) collective-permute-start(bf16[128,2048]{1,0:T(8,128)(2,1)S(1)} %add_convert_fusion.1), channel_id=1, source_target_pairs={{4,8},{5,9},{6,10},{7,11},{8,4},{9,5},{10,6},{11,7},{20,24},{21,25... | collective-permute-start | bytes 1572872 | tf_op jit(solution)/shard_map/ppermute | solution.py:239

commit v3 on v2

--- a/solution.py
+++ b/solution.py
@@ -151,35 +151,23 @@
     )(*through, *after)
 
 
-def experts_kernel(pieces, tile, *refs):
+def experts_kernel(count, tile, *refs):
     me = lax.axis_index("ep")
-    line = me // 4
-    is_inner = (line == 1) | (line == 2)
-    blocks = []
-    for count in pieces:
-        blocks.append(refs[:count])
-        refs = refs[count:]
-    weights, refs = refs[:6], refs[6:]
-    outs, refs = refs[: len(pieces)], refs[len(pieces) :]
-    rows, total, sems = refs
+    blocks, weights, outs = refs[:count], refs[count : count + 6], refs[count + 6 : 2 * count + 6]
+    rows, total, sems = refs[2 * count + 6 :]
     width = outs[0].shape[1]
     ff = weights[0].shape[2]
     f32, bf16 = jnp.float32, jnp.bfloat16
 
-    def each_block(act):
-        at = 0
-        for p, block in enumerate(blocks):
-            size = block[0].shape[0]
-            for n, ref in enumerate(block):
-                copy = pltpu.make_async_copy(ref, rows.at[pl.ds(at, size)], sems.at[p, n])
-                if len(block) == 1:
-                    act(copy)
-                else:
-                    pl.when(is_inner if n == 0 else ~is_inner)(functools.partial(act, copy))
-            at += size
-
-    each_block(lambda copy: copy.start())
-    each_block(lambda copy: copy.wait())
+    copies, at = [], 0
+    for n, block in enumerate(blocks):
+        size = block.shape[0]
+        copies.append(pltpu.make_async_copy(block, rows.at[pl.ds(at, size)], sems.at[n]))
+        at += size
+    for copy in copies:
+        copy.start()
+    for copy in copies:
+        copy.wait()
 
     shares = rows[:, width:].astype(f32)
     half = shares.shape[1] // 2
@@ -207,26 +195,52 @@
                     at += out.shape[0]
 
 
-def run_experts(pieces, weights):
-    sizes = [piece[0].shape[0] for piece in pieces]
-    wide = pieces[0][0].shape[1]
+def run_experts(blocks, weights):
+    count = len(blocks)
+    sizes = [block.shape[0] for block in blocks]
+    wide = blocks[0].shape[1]
     _, width, ff = weights[0].shape
     whole = sum(sizes)
-    blocks = [block for piece in pieces for block in piece]
     vmem, anywhere = pl.BlockSpec(memory_space=pltpu.VMEM), pl.BlockSpec(memory_space=pl.ANY)
     return pl.pallas_call(
-        functools.partial(experts_kernel, [len(piece) for piece in pieces], ff // 3),
-        in_specs=[anywhere] * len(blocks) + [vmem] * 6,
-        out_specs=[vmem] * len(pieces),
+        functools.partial(experts_kernel, count, ff // 3),
+        in_specs=[anywhere] * count + [vmem] * 6,
+        out_specs=[vmem] * count,
         out_shape=[jax.ShapeDtypeStruct((size, width), jnp.bfloat16) for size in sizes],
         scratch_shapes=[
             pltpu.VMEM((whole, wide), jnp.bfloat16),
             pltpu.VMEM((whole, width), jnp.float32),
-            pltpu.SemaphoreType.DMA((len(pieces), 2)),
+            pltpu.SemaphoreType.DMA((count,)),
         ],
         compiler_params=pltpu.CompilerParams(vmem_limit_bytes=20 * 2**20),
         cost_estimate=SMALL,
     )(*blocks, *weights)
+
+
+def choose_kernel(inner, outer, out, sem):
+    line = lax.axis_index("ep") // 4
+    is_inner = (line == 1) | (line == 2)
+
+    def take(array):
+        copy = pltpu.make_async_copy(array, out, sem)
+        copy.start()
+        copy.wait()
+
+    pl.when(is_inner)(functools.partial(take, inner))
+    pl.when(~is_inner)(functools.partial(take, outer))
+
+
+def choose(inner, outer):
+    anywhere = pl.BlockSpec(memory_space=pl.ANY)
+    return pl.pallas_call(
+        choose_kernel,
+        in_specs=[anywhere] * 2,
+        out_specs=anywhere,
+        out_shape=jax.ShapeDtypeStruct(inner.shape, inner.dtype),
+        scratch_shapes=[pltpu.SemaphoreType.DMA],
+        compiler_params=pltpu.CompilerParams(vmem_limit_bytes=2**20),
+        cost_estimate=SMALL,
+    )(inner, outer)
 
 
 def gather_rows(hidden, norm_gain, routes, route_weight, w_gate, w_up, w_down):
@@ -238,52 +252,56 @@
         moves = [(i, to[i // 4] * 4 + i % 4) for i in range(count) if to[i // 4] is not None]
         return lax.ppermute(x, "ep", moves)
 
-    def cross(x, lines=(0, 1, 2, 3)):
-        return lax.ppermute(x, "ep", [(i, i ^ 2) for i in range(count) if i // 4 in lines])
+    def cross(x):
+        return lax.ppermute(x, "ep", [(i, i ^ 2) for i in range(count)])
 
     def other_core(x):
         return lax.ppermute(x, "ep", [(i, i ^ 1) for i in range(count)])
 
-    ends, inner = (0, 3), (1, 2)
+    def add(*parts):
+        return sum(p.astype(f32) for p in parts).astype(bf16)
+
+    far, back = [2, 0, 3, 1], [1, 3, 0, 2]
     pairs, middle = [1, 0, 3, 2], [None, 2, 1, None]
     outward, inward = [None, 0, 3, None], [1, None, None, 2]
 
     far_gate, far_up = other_core(w_gate), other_core(w_up)
     own = prepare(hidden, norm_gain, routes, route_weight)
 
-    p1, n2, y0 = line(own, pairs), line(own, middle), cross(own)
+    a, y0 = line(own, far), cross(own)
     weights, token = hold(w_gate, w_up, w_down)
-    p1, n2, y0, far_gate, far_up = gate([p1, n2, y0, far_gate, far_up], [token])
-
-    n4, n3, yn2 = line(p1, middle), line(n2, outward), cross(n2, inner)
-    far_down = other_core(again(w_down, p1))
+    a, y0, far_gate, far_up = gate([a, y0, far_gate, far_up], [token])
+
+    b, n, ya = line(choose(a, own), pairs), line(own, middle), cross(a)
+    far_down = other_core(w_down)
     held, token = hold(far_gate, far_up)
     weights += held
-    n4, n3, yn2, far_down = gate([n4, n3, yn2, far_down], [token])
-
-    n5, yn3, yn4 = line(n4, outward), cross(n3, ends), cross(n4, inner)
+    b, n, ya = gate([b, n, ya], [token])
+
+    c, yb = line(n, outward), cross(b)
     held, token = hold(far_down)
     weights += held
-    m0, o0 = run_experts([(own,), (y0,)], weights)
-    n5, yn3, yn4 = gate([n5, yn3, yn4], [o0])
-
-    yn5, y1 = cross(n5, ends), line(y0, pairs)
-    m3, o3 = run_experts([(n2, n3), (yn2, yn3)], weights)
-    yn5, y1 = gate([yn5, y1], [o3])
-    m4, o4 = run_experts([(n4, n5), (yn4, yn5)], weights)
-
-    def add(*parts):
-        return sum(p.astype(f32) for p in parts).astype(bf16)
-
-    o4 = cross(o4)
-    m1, o1 = run_experts([(p1,), (y1,)], weights)
-    o4, o3 = gate([o4, o3], [o1])
-    r4 = add(m4, o4)
-    r3 = add(m3, cross(o3))
-    r4 = add(r4, line(r4, inward))
-    r1 = add(m1, cross(o1), line(r4, middle))
-    r3 = add(r3, line(r3, inward))
-    return add(m0, cross(o0), line(r1, pairs), line(r3, middle))
+    m0, o0 = run_experts([own, y0], weights)
+    c, yb = gate([c, yb], [o0])
+
+    c = choose(n, c)
+    yc = cross(c)
+    ma, oa = run_experts([a, ya], weights)
+    (yc,) = gate([yc], [oa])
+    mc, oc = run_experts([c, yc], weights)
+
+    oc = cross(oc)
+    mb, ob = run_experts([b, yb], weights)
+    oc, ob = gate([oc, ob], [])
+    rc = add(mc, oc)
+    rb = add(mb, cross(ob))
+    rc = add(rc, line(rc, inward))
+    p = line(rb, pairs)
+    place = lax.axis_index("ep") // 4
+    is_inner = (place == 1) | (place == 2)
+    zero = jnp.zeros_like(p)
+    ra = add(ma, cross(oa), jnp.where(is_inner, p, zero))
+    return add(m0, cross(o0), line(ra, back), line(rc, middle), jnp.where(is_inner, zero, p))
 
 
 def solution(mesh):

time: 138 us -> 128 us (0.928)
  the two profiles are of different devices: /device:TPU:18 before, /device:TPU:0 now
where the time goes in v3:
time: 128 us
  waiting for transfers between devices  59.3 us (46%)
  Pallas kernels  35.4 us (28%)
  starting transfers between devices  28.3 us (22%)
  other arithmetic  4.74 us (4%)
    ppermute x8, waiting for transfers between devices, line(): return lax.ppermute(x, 'ep', moves)  33.5 us
    ppermute x8, waiting for transfers between devices, cross(): return lax.ppermute(x, 'ep', [(i, i ^ 2) for i in range(count)])  25.8 us
    pallas_call x4, Pallas kernels, run_experts(): pl.pallas_call(functools.partial(experts_kernel, count, ff // 3), in_spec...  23.4 us
    ppermute x8, starting transfers between devices, line(): return lax.ppermute(x, 'ep', moves)  16 us
    ppermute x8, starting transfers between devices, cross(): return lax.ppermute(x, 'ep', [(i, i ^ 2) for i in range(count)])  11.3 us
    pallas_call x3, Pallas kernels, hold(): pl.pallas_call(functools.partial(hold_kernel, count), in_specs=[pl.BlockS...  9.13 us
    convert_element_type x5, other arithmetic, add(): return sum((p.astype(f32) for p in parts)).astype(bf16)  4.74 us
  transfers between devices with their start and end apart: 19, of which 11 were waited for; matrix products, arithmetic and copies ran while one was open for 3% of the time, Pallas kernels for 23%

profile of v3, /device:TPU:0, one launch (start us, length us, event | category | flops | bytes accessed | tf_op | source)
XLA Modules:
  0.0 127.9 jit_solution(1059735554887780442)
XLA Ops:
  1.0 2.5 %shard_map.73.refs_0_.outer = bf16[128,2176]{1,0:T(8,128)(2,1)} custom-call(bf16[128,2048]{1,0:T(8,128)(2,1)} %refs_0_.2, f32[1,2048]{1,0:T(1,128)} %bitcast.3, s32[8,128]{1,0:T(8,128)} %bitcast.4, f32[8,128]{1,0:T(8,128)} %bitcast.5), custom_call_target="tpu_custom_call" | custom-call | tf_op jit(solution)/shard_map/pallas_call | solution.py:80
  3.4 3.6 %collective-permute-start = (bf16[128,2176]{1,0:T(8,128)(2,1)}, bf16[128,2176]{1,0:T(8,128)(2,1)S(1)}, u32[]{:S(2)}, u32[]{:S(2)}) collective-permute-start(bf16[128,2176]{1,0:T(8,128)(2,1)} %shard_map.73.refs_0_.outer), channel_id=1, source_target_pairs={{0,8},{1,9},{2,10},{3,11},{4,0},{5,1},{6,2},{7,3},{8,12},{9,13},{1... | collective-permute-start | bytes 1671176 | tf_op jit(solution)/shard_map/ppermute | solution.py:253
  7.1 1.5 %collective-permute-start.1 = (bf16[128,2176]{1,0:T(8,128)(2,1)}, bf16[128,2176]{1,0:T(8,128)(2,1)S(1)}, u32[]{:S(2)}, u32[]{:S(2)}) collective-permute-start(bf16[128,2176]{1,0:T(8,128)(2,1)} %shard_map.73.refs_0_.outer), channel_id=1, source_target_pairs={{0,2},{1,3},{2,0},{3,1},{4,6},{5,7},{6,4},{7,5},{8,10},{9,11},{10,... | collective-permute-start | bytes 1671176 | tf_op jit(solution)/shard_map/ppermute | solution.py:256
  8.6 3.8 %shard_map.74 = (bf16[1,2048,768]{2,1,0:T(8,128)(2,1)S(1)}, bf16[1,2048,768]{2,1,0:T(8,128)(2,1)S(1)}, bf16[1,768,2048]{2,1,0:T(8,128)(2,1)S(1)}, f32[8,128]{1,0:T(8,128)S(1)}) custom-call(bf16[1,2048,768]{2,1,0:T(8,128)(2,1)} %refs_0_.3, bf16[1,2048,768]{2,1,0:T(8,128)(2,1)} %refs_1_.1, bf16[1,768,2048]{2,1,0:T(8,128)(2,1)} %refs_2_.1), custom_call_target="tpu_custom_call" | custom-call | flops 1 | bytes 1 | tf_op jit(solution)/shard_map/pallas_call | solution.py:103
  12.4 7.6 %collective-permute-done.refs_0_ = bf16[128,2176]{1,0:T(8,128)(2,1)S(1)} collective-permute-done((bf16[128,2176]{1,0:T(8,128)(2,1)}, bf16[128,2176]{1,0:T(8,128)(2,1)S(1)}, u32[]{:S(2)}, u32[]{:S(2)}) %collective-permute-start) | collective-permute-done | bytes 557088 | tf_op jit(solution)/shard_map/ppermute | solution.py:253
  20.7 1.4 %collective-permute-done.1.refs_1_ = bf16[128,2176]{1,0:T(8,128)(2,1)S(1)} collective-permute-done((bf16[128,2176]{1,0:T(8,128)(2,1)}, bf16[128,2176]{1,0:T(8,128)(2,1)S(1)}, u32[]{:S(2)}, u32[]{:S(2)}) %collective-permute-start.1) | collective-permute-done | bytes 557088 | tf_op jit(solution)/shard_map/ppermute | solution.py:256
  22.2 3.8 %collective-permute-start.6 = (bf16[128,2176]{1,0:T(8,128)(2,1)S(1)}, bf16[128,2176]{1,0:T(8,128)(2,1)S(1)}, u32[]{:S(2)}, u32[]{:S(2)}) collective-permute-start(bf16[128,2176]{1,0:T(8,128)(2,1)S(1)} %shard_map.79), channel_id=1, source_target_pairs={{0,4},{1,5},{2,6},{3,7},{4,0},{5,1},{6,2},{7,3},{8,12},{9,13},{10,... | collective-permute-start | bytes 1671176 | tf_op jit(solution)/shard_map/ppermute | solution.py:253
  25.9 1.5 %collective-permute-start.8 = (bf16[128,2176]{1,0:T(8,128)(2,1)S(1)}, bf16[128,2176]{1,0:T(8,128)(2,1)S(1)}, u32[]{:S(2)}, u32[]{:S(2)}) collective-permute-start(bf16[128,2176]{1,0:T(8,128)(2,1)S(1)} %get-tuple-element.44.inner.refs_0_), channel_id=1, source_target_pairs={{0,2},{1,3},{2,0},{3,1},{4,6},{5,7},{6,4},{7,5},{8,10},{9,11},{10,... | collective-permute-start | bytes 1671176 | tf_op jit(solution)/shard_map/ppermute | solution.py:256
  27.4 2.9 %shard_map.76 = (bf16[1,2048,768]{2,1,0:T(8,128)(2,1)S(1)}, bf16[1,2048,768]{2,1,0:T(8,128)(2,1)S(1)}, f32[8,128]{1,0:T(8,128)S(1)}) custom-call(bf16[1,2048,768]{2,1,0:T(8,128)(2,1)} %get-tuple-element.37.refs_0_, bf16[1,2048,768]{2,1,0:T(8,128)(2,1)} %get-tuple-element.38.refs_1_), custom_call_target="tpu_custom_call" | custom-call | flops 1 | bytes 1 | tf_op jit(solution)/shard_map/pallas_call | solution.py:103
  30.3 7.8 %collective-permute-done.6.refs_0_ = bf16[128,2176]{1,0:T(8,128)(2,1)S(1)} collective-permute-done((bf16[128,2176]{1,0:T(8,128)(2,1)S(1)}, bf16[128,2176]{1,0:T(8,128)(2,1)S(1)}, u32[]{:S(2)}, u32[]{:S(2)}) %collective-permute-start.6) | collective-permute-done | bytes 557088 | tf_op jit(solution)/shard_map/ppermute | solution.py:253
  38.2 1.5 %collective-permute-done.8.refs_2_ = bf16[128,2176]{1,0:T(8,128)(2,1)S(1)} collective-permute-done((bf16[128,2176]{1,0:T(8,128)(2,1)S(1)}, bf16[128,2176]{1,0:T(8,128)(2,1)S(1)}, u32[]{:S(2)}, u32[]{:S(2)}) %collective-permute-start.8) | collective-permute-done | bytes 557088 | tf_op jit(solution)/shard_map/ppermute | solution.py:256
  39.6 1.3 %collective-permute-start.10 = (bf16[128,2176]{1,0:T(8,128)(2,1)S(1)}, bf16[128,2176]{1,0:T(8,128)(2,1)S(1)}, u32[]{:S(2)}, u32[]{:S(2)}) collective-permute-start(bf16[128,2176]{1,0:T(8,128)(2,1)S(1)} %get-tuple-element.50.inner), channel_id=1, source_target_pairs={{4,0},{5,1},{6,2},{7,3},{8,12},{9,13},{10,14},{11,15},{20,16},{21,... | collective-permute-start | bytes 1671176 | tf_op jit(solution)/shard_map/ppermute | solution.py:253
  40.9 1.6 %collective-permute-start.11 = (bf16[128,2176]{1,0:T(8,128)(2,1)S(1)}, bf16[128,2176]{1,0:T(8,128)(2,1)S(1)}, u32[]{:S(2)}, u32[]{:S(2)}) collective-permute-start(bf16[128,2176]{1,0:T(8,128)(2,1)S(1)} %get-tuple-element.49.refs_0_), channel_id=1, source_target_pairs={{0,2},{1,3},{2,0},{3,1},{4,6},{5,7},{6,4},{7,5},{8,10},{9,11},{10,... | collective-permute-start | bytes 1671176 | tf_op jit(solution)/shard_map/ppermute | solution.py:256
  42.5 2.5 %shard_map.77 = (bf16[1,768,2048]{2,1,0:T(8,128)(2,1)S(1)}, f32[8,128]{1,0:T(8,128)}) custom-call(bf16[1,768,2048]{2,1,0:T(8,128)(2,1)} %collective-permute-done.4.refs_0_), custom_call_target="tpu_custom_call" | custom-call | flops 1 | bytes 1 | tf_op jit(solution)/shard_map/pallas_call | solution.py:103
  45.0 5.9 %shard_map.78 = (bf16[128,2048]{1,0:T(8,128)(2,1)S(1)}, bf16[128,2048]{1,0:T(8,128)(2,1)S(1)}) custom-call(bf16[128,2176]{1,0:T(8,128)(2,1)S(1)} %copy-done, bf16[128,2176]{1,0:T(8,128)(2,1)S(1)} %get-tuple-element.33.refs_1_, bf16[1,2048,768]{2,1,0:T(8,128)(2,1)S(1)} %get-tuple-element.34.refs_2_, bf16[1,2048,768]{2,1,0:T(8,128)(2,1)S(1)} %get-tuple-element.35.refs_3_, ...), custom_call_target="tpu_custom_call" | custom-call | flops 1 | bytes 1 | tf_op jit(solution)/shard_map/pallas_call | solution.py:205
  50.9 3.4 %collective-permute-done.10.refs_0_ = bf16[128,2176]{1,0:T(8,128)(2,1)S(1)} collective-permute-done((bf16[128,2176]{1,0:T(8,128)(2,1)S(1)}, bf16[128,2176]{1,0:T(8,128)(2,1)S(1)}, u32[]{:S(2)}, u32[]{:S(2)}) %collective-permute-start.10) | collective-permute-done | bytes 557088 | tf_op jit(solution)/shard_map/ppermute | solution.py:253
  54.6 1.6 %collective-permute-start.12 = (bf16[128,2176]{1,0:T(8,128)(2,1)S(1)}, bf16[128,2176]{1,0:T(8,128)(2,1)S(1)}, u32[]{:S(2)}, u32[]{:S(2)}) collective-permute-start(bf16[128,2176]{1,0:T(8,128)(2,1)S(1)} %shard_map.84.refs_0_), channel_id=1, source_target_pairs={{0,2},{1,3},{2,0},{3,1},{4,6},{5,7},{6,4},{7,5},{8,10},{9,11},{10,... | collective-permute-start | bytes 1671176 | tf_op jit(solution)/shard_map/ppermute | solution.py:256
  56.1 5.8 %shard_map.81 = (bf16[128,2048]{1,0:T(8,128)(2,1)S(1)}, bf16[128,2048]{1,0:T(8,128)(2,1)S(1)}) custom-call(bf16[128,2176]{1,0:T(8,128)(2,1)S(1)} %get-tuple-element.44.inner.refs_0_, bf16[128,2176]{1,0:T(8,128)(2,1)S(1)} %get-tuple-element.46.refs_1_, bf16[1,2048,768]{2,1,0:T(8,128)(2,1)S(1)} %get-tuple-element.34.refs_2_, ...), custom_call_target="tpu_custom_call" | custom-call | flops 1 | bytes 1 | tf_op jit(solution)/shard_map/pallas_call | solution.py:205
  62.0 4.5 %collective-permute-done.12.refs_0_ = bf16[128,2176]{1,0:T(8,128)(2,1)S(1)} collective-permute-done((bf16[128,2176]{1,0:T(8,128)(2,1)S(1)}, bf16[128,2176]{1,0:T(8,128)(2,1)S(1)}, u32[]{:S(2)}, u32[]{:S(2)}) %collective-permute-start.12) | collective-permute-done | bytes 557088 | tf_op jit(solution)/shard_map/ppermute | solution.py:256
  66.5 5.8 %shard_map.86 = (bf16[128,2048]{1,0:T(8,128)(2,1)S(1)}, bf16[128,2048]{1,0:T(8,128)(2,1)S(1)}) custom-call(bf16[128,2176]{1,0:T(8,128)(2,1)S(1)} %shard_map.84.refs_0_, bf16[128,2176]{1,0:T(8,128)(2,1)S(1)} %shard_map.85.refs_1_, bf16[1,2048,768]{2,1,0:T(8,128)(2,1)S(1)} %get-tuple-element.34.refs_2_, bf16[1,2048,768]{2,1,0:T(8,128)(2,1)S(1)} %get-tuple-element.35.refs_3_, ...), custom_call_target="tpu_custom_call" | custom-call | flops 1 | bytes 1 | tf_op jit(solution)/shard_map/pallas_call | solution.py:205
  72.3 1.6 %collective-permute-start.13 = (bf16[128,2048]{1,0:T(8,128)(2,1)S(1)}, bf16[128,2048]{1,0:T(8,128)(2,1)S(1)}, u32[]{:S(2)}, u32[]{:S(2)}) collective-permute-start(bf16[128,2048]{1,0:T(8,128)(2,1)S(1)} %get-tuple-element.54), channel_id=1, source_target_pairs={{0,2},{1,3},{2,0},{3,1},{4,6},{5,7},{6,4},{7,5},{8,10},{9,11},{10,... | collective-permute-start | bytes 1572872 | tf_op jit(solution)/shard_map/ppermute | solution.py:256
  73.9 5.8 %shard_map.83 = (bf16[128,2048]{1,0:T(8,128)(2,1)S(1)}, bf16[128,2048]{1,0:T(8,128)(2,1)S(1)}) custom-call(bf16[128,2176]{1,0:T(8,128)(2,1)S(1)} %get-tuple-element.49.refs_0_, bf16[128,2176]{1,0:T(8,128)(2,1)S(1)} %get-tuple-element.51.refs_1_, bf16[1,2048,768]{2,1,0:T(8,128)(2,1)S(1)} %get-tuple-element.34.refs_2_, ...), custom_call_target="tpu_custom_call" | custom-call | flops 1 | bytes 1 | tf_op jit(solution)/shard_map/pallas_call | solution.py:205
  79.8 4.7 %collective-permute-done.13.refs_0_ = bf16[128,2048]{1,0:T(8,128)(2,1)S(1)} collective-permute-done((bf16[128,2048]{1,0:T(8,128)(2,1)S(1)}, bf16[128,2048]{1,0:T(8,128)(2,1)S(1)}, u32[]{:S(2)}, u32[]{:S(2)}) %collective-permute-start.13) | collective-permute-done | bytes 524320 | tf_op jit(solution)/shard_map/ppermute | solution.py:256
  84.5 1.5 %collective-permute-start.14 = (bf16[128,2048]{1,0:T(8,128)(2,1)S(1)}, bf16[128,2048]{1,0:T(8,128)(2,1)S(1)}, u32[]{:S(2)}, u32[]{:S(2)}) collective-permute-start(bf16[128,2048]{1,0:T(8,128)(2,1)S(1)} %get-tuple-element.56), channel_id=1, source_target_pairs={{0,2},{1,3},{2,0},{3,1},{4,6},{5,7},{6,4},{7,5},{8,10},{9,11},{10,... | collective-permute-start | bytes 1572872 | tf_op jit(solution)/shard_map/ppermute | solution.py:256
  86.6 4.3 %collective-permute-start.17 = (bf16[128,2048]{1,0:T(8,128)(2,1)S(1)}, bf16[128,2048]{1,0:T(8,128)(2,1)}, u32[]{:S(2)}, u32[]{:S(2)}) collective-permute-start(bf16[128,2048]{1,0:T(8,128)(2,1)S(1)} %add_convert_fusion.2), channel_id=1, source_target_pairs={{0,4},{1,5},{2,6},{3,7},{12,8},{13,9},{14,10},{15,11},{16,20},{17,... | collective-permute-start | bytes 1572872 | tf_op jit(solution)/shard_map/ppermute | solution.py:253
  91.0 8.4 %collective-permute-done.14 = bf16[128,2048]{1,0:T(8,128)(2,1)S(1)} collective-permute-done((bf16[128,2048]{1,0:T(8,128)(2,1)S(1)}, bf16[128,2048]{1,0:T(8,128)(2,1)S(1)}, u32[]{:S(2)}, u32[]{:S(2)}) %collective-permute-start.14) | collective-permute-done | bytes 524320 | tf_op jit(solution)/shard_map/ppermute | solution.py:256
  100.3 1.6 %collective-permute-start.15 = (bf16[128,2048]{1,0:T(8,128)(2,1)}, bf16[128,2048]{1,0:T(8,128)(2,1)S(1)}, u32[]{:S(2)}, u32[]{:S(2)}) collective-permute-start(bf16[128,2048]{1,0:T(8,128)(2,1)} %add_convert_fusion.4), channel_id=1, source_target_pairs={{0,4},{1,5},{2,6},{3,7},{4,0},{5,1},{6,2},{7,3},{8,12},{9,13},{10,... | collective-permute-start | bytes 1572872 | tf_op jit(solution)/shard_map/ppermute | solution.py:253
  101.9 1.5 %collective-permute-start.5 = (bf16[128,2048]{1,0:T(8,128)(2,1)S(1)}, bf16[128,2048]{1,0:T(8,128)(2,1)S(1)}, u32[]{:S(2)}, u32[]{:S(2)}) collective-permute-start(bf16[128,2048]{1,0:T(8,128)(2,1)S(1)} %get-tuple-element.43.refs_2_), channel_id=1, source_target_pairs={{0,2},{1,3},{2,0},{3,1},{4,6},{5,7},{6,4},{7,5},{8,10},{9,11},{10,... | collective-permute-start | bytes 1572872 | tf_op jit(solution)/shard_map/ppermute | solution.py:256
  105.3 5.4 %collective-permute-done.9 = bf16[128,2048]{1,0:T(8,128)(2,1)} collective-permute-done((bf16[128,2048]{1,0:T(8,128)(2,1)S(1)}, bf16[128,2048]{1,0:T(8,128)(2,1)}, u32[]{:S(2)}, u32[]{:S(2)}) %collective-permute-start.9) | collective-permute-done | bytes 524320 | tf_op jit(solution)/shard_map/ppermute | solution.py:256
  110.7 4.6 %collective-permute-done.15 = bf16[128,2048]{1,0:T(8,128)(2,1)S(1)} collective-permute-done((bf16[128,2048]{1,0:T(8,128)(2,1)}, bf16[128,2048]{1,0:T(8,128)(2,1)S(1)}, u32[]{:S(2)}, u32[]{:S(2)}) %collective-permute-start.15) | collective-permute-done | bytes 524320 | tf_op jit(solution)/shard_map/ppermute | solution.py:253
  115.3 1.3 %add_convert_fusion.3 = bf16[128,2048]{1,0:T(8,128)(2,1)S(1)} fusion(bf16[128,2048]{1,0:T(8,128)(2,1)} %collective-permute-done.9, bf16[128,2048]{1,0:T(8,128)(2,1)S(1)} %get-tuple-element.47, bf16[128,2048]{1,0:T(8,128)(2,1)S(1)} %collective-permute-done.15, pred[]{:T(512)S(6)} %or.3), kind=kLoop, calls=%fused_computation.3 | loop fusion | flops 1835008 | bytes 2097153 | tf_op jit(solution)/shard_map/convert_element_type | solution.py:262
  116.7 10.0 %collective-permute-done.16 = bf16[128,2048]{1,0:T(8,128)(2,1)S(1)} collective-permute-done((bf16[128,2048]{1,0:T(8,128)(2,1)S(1)}, bf16[128,2048]{1,0:T(8,128)(2,1)S(1)}, u32[]{:S(2)}, u32[]{:S(2)}) %collective-permute-start.16) | collective-permute-done | bytes 524320 | tf_op jit(solution)/shard_map/ppermute | solution.py:253
  (28 shorter events, 6.8 us)
Async XLA Ops:
  0.0 22.1 %collective-permute-start.2 = (bf16[1,2048,768]{2,1,0:T(8,128)(2,1)}, bf16[1,2048,768]{2,1,0:T(8,128)(2,1)}, u32[]{:S(2)}, u32[]{:S(2)}) collective-permute-start(bf16[1,2048,768]{2,1,0:T(8,128)(2,1)} %refs_0_.3), channel_id=1, source_target_pairs={{0,1},{1,0},{2,3},{3,2},{4,5},{5,4},{6,7},{7,6},{8,9},{9,8},{10,11... | collective-permute-start | bytes 9437192 | tf_op jit(solution)/shard_map/ppermute | solution.py:259
  0.5 21.6 %collective-permute-start.3 = (bf16[1,2048,768]{2,1,0:T(8,128)(2,1)}, bf16[1,2048,768]{2,1,0:T(8,128)(2,1)}, u32[]{:S(2)}, u32[]{:S(2)}) collective-permute-start(bf16[1,2048,768]{2,1,0:T(8,128)(2,1)} %refs_1_.1), channel_id=1, source_target_pairs={{0,1},{1,0},{2,3},{3,2},{4,5},{5,4},{6,7},{7,6},{8,9},{9,8},{10,11... | collective-permute-start | bytes 9437192 | tf_op jit(solution)/shard_map/ppermute | solution.py:259
  0.5 42.0 %collective-permute-start.4 = (bf16[1,768,2048]{2,1,0:T(8,128)(2,1)}, bf16[1,768,2048]{2,1,0:T(8,128)(2,1)}, u32[]{:S(2)}, u32[]{:S(2)}) collective-permute-start(bf16[1,768,2048]{2,1,0:T(8,128)(2,1)} %refs_2_.1), channel_id=1, source_target_pairs={{0,1},{1,0},{2,3},{3,2},{4,5},{5,4},{6,7},{7,6},{8,9},{9,8},{10,11... | collective-permute-start | bytes 9437192 | tf_op jit(solution)/shard_map/ppermute | solution.py:259
  3.4 16.5 %copy-start = (bf16[128,2176]{1,0:T(8,128)(2,1)S(1)}, bf16[128,2176]{1,0:T(8,128)(2,1)}, u32[]{:S(2)}) copy-start(bf16[128,2176]{1,0:T(8,128)(2,1)} %shard_map.73.refs_0_.outer) | copy-start | bytes 1671172
  3.4 16.5 %collective-permute-start = (bf16[128,2176]{1,0:T(8,128)(2,1)}, bf16[128,2176]{1,0:T(8,128)(2,1)S(1)}, u32[]{:S(2)}, u32[]{:S(2)}) collective-permute-start(bf16[128,2176]{1,0:T(8,128)(2,1)} %shard_map.73.refs_0_.outer), channel_id=1, source_target_pairs={{0,8},{1,9},{2,10},{3,11},{4,0},{5,1},{6,2},{7,3},{8,12},{9,13},{1... | collective-permute-start | bytes 1671176 | tf_op jit(solution)/shard_map/ppermute | solution.py:253
  7.1 15.0 %collective-permute-start.1 = (bf16[128,2176]{1,0:T(8,128)(2,1)}, bf16[128,2176]{1,0:T(8,128)(2,1)S(1)}, u32[]{:S(2)}, u32[]{:S(2)}) collective-permute-start(bf16[128,2176]{1,0:T(8,128)(2,1)} %shard_map.73.refs_0_.outer), channel_id=1, source_target_pairs={{0,2},{1,3},{2,0},{3,1},{4,6},{5,7},{6,4},{7,5},{8,10},{9,11},{10,... | collective-permute-start | bytes 1671176 | tf_op jit(solution)/shard_map/ppermute | solution.py:256
  20.0 10.4 %collective-permute-start.7 = (bf16[128,2176]{1,0:T(8,128)(2,1)S(1)}, bf16[128,2176]{1,0:T(8,128)(2,1)S(1)}, u32[]{:S(2)}, u32[]{:S(2)}) collective-permute-start(bf16[128,2176]{1,0:T(8,128)(2,1)S(1)} %copy-done), channel_id=1, source_target_pairs={{4,8},{5,9},{6,10},{7,11},{8,4},{9,5},{10,6},{11,7},{20,24},{21,25... | collective-permute-start | bytes 1671176 | tf_op jit(solution)/shard_map/ppermute | solution.py:253
  22.2 16.0 %collective-permute-start.6 = (bf16[128,2176]{1,0:T(8,128)(2,1)S(1)}, bf16[128,2176]{1,0:T(8,128)(2,1)S(1)}, u32[]{:S(2)}, u32[]{:S(2)}) collective-permute-start(bf16[128,2176]{1,0:T(8,128)(2,1)S(1)} %shard_map.79), channel_id=1, source_target_pairs={{0,4},{1,5},{2,6},{3,7},{4,0},{5,1},{6,2},{7,3},{8,12},{9,13},{10,... | collective-permute-start | bytes 1671176 | tf_op jit(solution)/shard_map/ppermute | solution.py:253
  25.9 13.7 %collective-permute-start.8 = (bf16[128,2176]{1,0:T(8,128)(2,1)S(1)}, bf16[128,2176]{1,0:T(8,128)(2,1)S(1)}, u32[]{:S(2)}, u32[]{:S(2)}) collective-permute-start(bf16[128,2176]{1,0:T(8,128)(2,1)S(1)} %get-tuple-element.44.inner.refs_0_), channel_id=1, source_target_pairs={{0,2},{1,3},{2,0},{3,1},{4,6},{5,7},{6,4},{7,5},{8,10},{9,11},{10,... | collective-permute-start | bytes 1671176 | tf_op jit(solution)/shard_map/ppermute | solution.py:256
  39.6 14.7 %collective-permute-start.10 = (bf16[128,2176]{1,0:T(8,128)(2,1)S(1)}, bf16[128,2176]{1,0:T(8,128)(2,1)S(1)}, u32[]{:S(2)}, u32[]{:S(2)}) collective-permute-start(bf16[128,2176]{1,0:T(8,128)(2,1)S(1)} %get-tuple-element.50.inner), channel_id=1, source_target_pairs={{4,0},{5,1},{6,2},{7,3},{8,12},{9,13},{10,14},{11,15},{20,16},{21,... | collective-permute-start | bytes 1671176 | tf_op jit(solution)/shard_map/ppermute | solution.py:253
  40.9 13.4 %collective-permute-start.11 = (bf16[128,2176]{1,0:T(8,128)(2,1)S(1)}, bf16[128,2176]{1,0:T(8,128)(2,1)S(1)}, u32[]{:S(2)}, u32[]{:S(2)}) collective-permute-start(bf16[128,2176]{1,0:T(8,128)(2,1)S(1)} %get-tuple-element.49.refs_0_), channel_id=1, source_target_pairs={{0,2},{1,3},{2,0},{3,1},{4,6},{5,7},{6,4},{7,5},{8,10},{9,11},{10,... | collective-permute-start | bytes 1671176 | tf_op jit(solution)/shard_map/ppermute | solution.py:256
  54.6 11.9 %collective-permute-start.12 = (bf16[128,2176]{1,0:T(8,128)(2,1)S(1)}, bf16[128,2176]{1,0:T(8,128)(2,1)S(1)}, u32[]{:S(2)}, u32[]{:S(2)}) collective-permute-start(bf16[128,2176]{1,0:T(8,128)(2,1)S(1)} %shard_map.84.refs_0_), channel_id=1, source_target_pairs={{0,2},{1,3},{2,0},{3,1},{4,6},{5,7},{6,4},{7,5},{8,10},{9,11},{10,... | collective-permute-start | bytes 1671176 | tf_op jit(solution)/shard_map/ppermute | solution.py:256
  72.3 12.1 %collective-permute-start.13 = (bf16[128,2048]{1,0:T(8,128)(2,1)S(1)}, bf16[128,2048]{1,0:T(8,128)(2,1)S(1)}, u32[]{:S(2)}, u32[]{:S(2)}) collective-permute-start(bf16[128,2048]{1,0:T(8,128)(2,1)S(1)} %get-tuple-element.54), channel_id=1, source_target_pairs={{0,2},{1,3},{2,0},{3,1},{4,6},{5,7},{6,4},{7,5},{8,10},{9,11},{10,... | collective-permute-start | bytes 1572872 | tf_op jit(solution)/shard_map/ppermute | solution.py:256
  84.5 14.9 %collective-permute-start.14 = (bf16[128,2048]{1,0:T(8,128)(2,1)S(1)}, bf16[128,2048]{1,0:T(8,128)(2,1)S(1)}, u32[]{:S(2)}, u32[]{:S(2)}) collective-permute-start(bf16[128,2048]{1,0:T(8,128)(2,1)S(1)} %get-tuple-element.56), channel_id=1, source_target_pairs={{0,2},{1,3},{2,0},{3,1},{4,6},{5,7},{6,4},{7,5},{8,10},{9,11},{10,... | collective-permute-start | bytes 1572872 | tf_op jit(solution)/shard_map/ppermute | solution.py:256
  86.0 24.7 %collective-permute-start.9 = (bf16[128,2048]{1,0:T(8,128)(2,1)S(1)}, bf16[128,2048]{1,0:T(8,128)(2,1)}, u32[]{:S(2)}, u32[]{:S(2)}) collective-permute-start(bf16[128,2048]{1,0:T(8,128)(2,1)S(1)} %get-tuple-element.48.refs_1_), channel_id=1, source_target_pairs={{0,2},{1,3},{2,0},{3,1},{4,6},{5,7},{6,4},{7,5},{8,10},{9,11},{10,... | collective-permute-start | bytes 1572872 | tf_op jit(solution)/shard_map/ppermute | solution.py:256
  86.6 16.8 %collective-permute-start.17 = (bf16[128,2048]{1,0:T(8,128)(2,1)S(1)}, bf16[128,2048]{1,0:T(8,128)(2,1)}, u32[]{:S(2)}, u32[]{:S(2)}) collective-permute-start(bf16[128,2048]{1,0:T(8,128)(2,1)S(1)} %add_convert_fusion.2), channel_id=1, source_target_pairs={{0,4},{1,5},{2,6},{3,7},{12,8},{13,9},{14,10},{15,11},{16,20},{17,... | collective-permute-start | bytes 1572872 | tf_op jit(solution)/shard_map/ppermute | solution.py:253
  100.3 15.0 %collective-permute-start.15 = (bf16[128,2048]{1,0:T(8,128)(2,1)}, bf16[128,2048]{1,0:T(8,128)(2,1)S(1)}, u32[]{:S(2)}, u32[]{:S(2)}) collective-permute-start(bf16[128,2048]{1,0:T(8,128)(2,1)} %add_convert_fusion.4), channel_id=1, source_target_pairs={{0,4},{1,5},{2,6},{3,7},{4,0},{5,1},{6,2},{7,3},{8,12},{9,13},{10,... | collective-permute-start | bytes 1572872 | tf_op jit(solution)/shard_map/ppermute | solution.py:253
  101.9 14.8 %collective-permute-start.5 = (bf16[128,2048]{1,0:T(8,128)(2,1)S(1)}, bf16[128,2048]{1,0:T(8,128)(2,1)S(1)}, u32[]{:S(2)}, u32[]{:S(2)}) collective-permute-start(bf16[128,2048]{1,0:T(8,128)(2,1)S(1)} %get-tuple-element.43.refs_2_), channel_id=1, source_target_pairs={{0,2},{1,3},{2,0},{3,1},{4,6},{5,7},{6,4},{7,5},{8,10},{9,11},{10,... | collective-permute-start | bytes 1572872 | tf_op jit(solution)/shard_map/ppermute | solution.py:256
  104.6 12.1 %collective-permute-start.18 = (bf16[128,2048]{1,0:T(8,128)(2,1)S(1)}, bf16[128,2048]{1,0:T(8,128)(2,1)S(1)}, u32[]{:S(2)}, u32[]{:S(2)}) collective-permute-start(bf16[128,2048]{1,0:T(8,128)(2,1)S(1)} %add_convert_fusion.1), channel_id=1, source_target_pairs={{4,8},{5,9},{6,10},{7,11},{8,4},{9,5},{10,6},{11,7},{20,24},{21,25... | collective-permute-start | bytes 1572872 | tf_op jit(solution)/shard_map/ppermute | solution.py:253
  116.6 10.1 %collective-permute-start.16 = (bf16[128,2048]{1,0:T(8,128)(2,1)S(1)}, bf16[128,2048]{1,0:T(8,128)(2,1)S(1)}, u32[]{:S(2)}, u32[]{:S(2)}) collective-permute-start(bf16[128,2048]{1,0:T(8,128)(2,1)S(1)} %add_convert_fusion.3), channel_id=1, source_target_pairs={{0,4},{1,5},{2,6},{3,7},{4,12},{5,13},{6,14},{7,15},{8,0},{9,1},{1... | collective-permute-start | bytes 1572872 | tf_op jit(solution)/shard_map/ppermute | solution.py:253

commit v4 on v3

--- a/solution.py
+++ b/solution.py
@@ -264,6 +264,7 @@
     far, back = [2, 0, 3, 1], [1, 3, 0, 2]
     pairs, middle = [1, 0, 3, 2], [None, 2, 1, None]
     outward, inward = [None, 0, 3, None], [1, None, None, 2]
+    far_ends = [None, 3, 0, None]
 
     far_gate, far_up = other_core(w_gate), other_core(w_up)
     own = prepare(hidden, norm_gain, routes, route_weight)
@@ -287,21 +288,28 @@
     c = choose(n, c)
     yc = cross(c)
     ma, oa = run_experts([a, ya], weights)
-    (yc,) = gate([yc], [oa])
-    mc, oc = run_experts([c, yc], weights)
-
-    oc = cross(oc)
     mb, ob = run_experts([b, yb], weights)
-    oc, ob = gate([oc, ob], [])
-    rc = add(mc, oc)
-    rb = add(mb, cross(ob))
-    rc = add(rc, line(rc, inward))
-    p = line(rb, pairs)
+    yc, ob = gate([yc, ob], [oa])
+
     place = lax.axis_index("ep") // 4
     is_inner = (place == 1) | (place == 2)
-    zero = jnp.zeros_like(p)
-    ra = add(ma, cross(oa), jnp.where(is_inner, p, zero))
-    return add(m0, cross(o0), line(ra, back), line(rc, middle), jnp.where(is_inner, zero, p))
+
+    yob, xo = cross(ob), line(oa, back)
+    mc, oc = run_experts([c, yc], weights)
+    yob, xo, oc = gate([yob, xo, oc], [])
+
+    yoc, p = cross(oc), line(add(mb, yob), pairs)
+    o0 = add(o0, xo)
+    yoc, p, o0 = gate([yoc, p, o0], [])
+
+    yo0 = cross(o0)
+    rc = add(mc, yoc)
+    q, xm = line(rc, inward), line(add(ma, p), far_ends)
+    m0 = add(m0, jnp.where(is_inner, jnp.zeros_like(p), p))
+    yo0, q, xm, ma, m0 = gate([yo0, q, xm, ma, m0], [])
+
+    xe, xn = line(ma, inward), line(add(rc, q), middle)
+    return add(m0, yo0, xm, xe, xn)
 
 
 def solution(mesh):

time: 128 us -> 120 us (0.938)
  the two profiles are of different devices: /device:TPU:0 before, /device:TPU:18 now
where the time goes in v4:
time: 120 us; the launch traced here: 119 us
  waiting for transfers between devices  53.4 us (44%)
  Pallas kernels  36 us (30%)
  starting transfers between devices  26.9 us (22%)
  other arithmetic  2.81 us (2%)
    ppermute x10, waiting for transfers between devices, line(): return lax.ppermute(x, 'ep', moves)  46.7 us
    pallas_call x4, Pallas kernels, run_experts(): pl.pallas_call(functools.partial(experts_kernel, count, ff // 3), in_spec...  24.2 us
    ppermute x10, starting transfers between devices, line(): return lax.ppermute(x, 'ep', moves)  18.5 us
    pallas_call x3, Pallas kernels, hold(): pl.pallas_call(functools.partial(hold_kernel, count), in_specs=[pl.BlockS...  9.13 us
    ppermute x7, starting transfers between devices, cross(): return lax.ppermute(x, 'ep', [(i, i ^ 2) for i in range(count)])  7.92 us
    ppermute x7, waiting for transfers between devices, cross(): return lax.ppermute(x, 'ep', [(i, i ^ 2) for i in range(count)])  6.74 us
    convert_element_type x6, other arithmetic, add(): return sum((p.astype(f32) for p in parts)).astype(bf16)  2.81 us
    pallas_call x1, Pallas kernels, prepare(): pl.pallas_call(prepare_kernel, in_specs=[pl.BlockSpec(memory_space=pltpu....  2.46 us
  transfers between devices with their start and end apart: 20, of which 13 were waited for; matrix products, arithmetic and copies ran while one was open for 0% of the time, Pallas kernels for 30%

profile of v4, /device:TPU:18, one launch (start us, length us, event | category | flops | bytes accessed | tf_op | source)
XLA Modules:
  0.0 119.4 jit_solution(2636074478916608170)
XLA Ops:
  0.5 2.5 %shard_map.73.outer.refs_0_ = bf16[128,2176]{1,0:T(8,128)(2,1)} custom-call(bf16[128,2048]{1,0:T(8,128)(2,1)} %refs_0_.2, f32[1,2048]{1,0:T(1,128)} %bitcast.3, s32[8,128]{1,0:T(8,128)} %bitcast.4, f32[8,128]{1,0:T(8,128)} %bitcast.5), custom_call_target="tpu_custom_call" | custom-call | tf_op jit(solution)/shard_map/pallas_call | solution.py:80
  3.0 1.6 %collective-permute-start = (bf16[128,2176]{1,0:T(8,128)(2,1)}, bf16[128,2176]{1,0:T(8,128)(2,1)S(1)}, u32[]{:S(2)}, u32[]{:S(2)}) collective-permute-start(bf16[128,2176]{1,0:T(8,128)(2,1)} %shard_map.73.outer.refs_0_), channel_id=1, source_target_pairs={{0,8},{1,9},{2,10},{3,11},{4,0},{5,1},{6,2},{7,3},{8,12},{9,13},{1... | collective-permute-start | bytes 1671176 | tf_op jit(solution)/shard_map/ppermute | solution.py:253
  4.6 1.5 %collective-permute-start.1 = (bf16[128,2176]{1,0:T(8,128)(2,1)}, bf16[128,2176]{1,0:T(8,128)(2,1)S(1)}, u32[]{:S(2)}, u32[]{:S(2)}) collective-permute-start(bf16[128,2176]{1,0:T(8,128)(2,1)} %shard_map.73.outer.refs_0_), channel_id=1, source_target_pairs={{0,2},{1,3},{2,0},{3,1},{4,6},{5,7},{6,4},{7,5},{8,10},{9,11},{10,... | collective-permute-start | bytes 1671176 | tf_op jit(solution)/shard_map/ppermute | solution.py:256
  6.1 3.8 %shard_map.74 = (bf16[1,2048,768]{2,1,0:T(8,128)(2,1)S(1)}, bf16[1,2048,768]{2,1,0:T(8,128)(2,1)S(1)}, bf16[1,768,2048]{2,1,0:T(8,128)(2,1)S(1)}, f32[8,128]{1,0:T(8,128)S(1)}) custom-call(bf16[1,2048,768]{2,1,0:T(8,128)(2,1)} %refs_0_.3, bf16[1,2048,768]{2,1,0:T(8,128)(2,1)} %refs_1_.1, bf16[1,768,2048]{2,1,0:T(8,128)(2,1)} %refs_2_.1), custom_call_target="tpu_custom_call" | custom-call | flops 1 | bytes 1 | tf_op jit(solution)/shard_map/pallas_call | solution.py:103
  9.9 9.3 %collective-permute-done.refs_0_ = bf16[128,2176]{1,0:T(8,128)(2,1)S(1)} collective-permute-done((bf16[128,2176]{1,0:T(8,128)(2,1)}, bf16[128,2176]{1,0:T(8,128)(2,1)S(1)}, u32[]{:S(2)}, u32[]{:S(2)}) %collective-permute-start) | collective-permute-done | bytes 557088 | tf_op jit(solution)/shard_map/ppermute | solution.py:253
  19.2 2.3 %collective-permute-start.5 = (bf16[128,2176]{1,0:T(8,128)(2,1)S(1)}, bf16[128,2176]{1,0:T(8,128)(2,1)S(1)}, u32[]{:S(2)}, u32[]{:S(2)}) collective-permute-start(bf16[128,2176]{1,0:T(8,128)(2,1)S(1)} %copy-done), channel_id=1, source_target_pairs={{4,8},{5,9},{6,10},{7,11},{8,4},{9,5},{10,6},{11,7},{20,24},{21,25... | collective-permute-start | bytes 1671176 | tf_op jit(solution)/shard_map/ppermute | solution.py:253
  21.8 1.6 %collective-permute-start.6 = (bf16[128,2176]{1,0:T(8,128)(2,1)S(1)}, bf16[128,2176]{1,0:T(8,128)(2,1)S(1)}, u32[]{:S(2)}, u32[]{:S(2)}) collective-permute-start(bf16[128,2176]{1,0:T(8,128)(2,1)S(1)} %get-tuple-element.44.inner.refs_0_), channel_id=1, source_target_pairs={{0,2},{1,3},{2,0},{3,1},{4,6},{5,7},{6,4},{7,5},{8,10},{9,11},{10,... | collective-permute-start | bytes 1671176 | tf_op jit(solution)/shard_map/ppermute | solution.py:256
  23.4 2.9 %shard_map.77 = (bf16[1,2048,768]{2,1,0:T(8,128)(2,1)S(1)}, bf16[1,2048,768]{2,1,0:T(8,128)(2,1)S(1)}, f32[8,128]{1,0:T(8,128)S(1)}) custom-call(bf16[1,2048,768]{2,1,0:T(8,128)(2,1)} %get-tuple-element.45.refs_0_, bf16[1,2048,768]{2,1,0:T(8,128)(2,1)} %get-tuple-element.46.refs_1_), custom_call_target="tpu_custom_call" | custom-call | flops 1 | bytes 1 | tf_op jit(solution)/shard_map/pallas_call | solution.py:103
  26.2 9.1 %collective-permute-done.5.refs_1_ = bf16[128,2176]{1,0:T(8,128)(2,1)S(1)} collective-permute-done((bf16[128,2176]{1,0:T(8,128)(2,1)S(1)}, bf16[128,2176]{1,0:T(8,128)(2,1)S(1)}, u32[]{:S(2)}, u32[]{:S(2)}) %collective-permute-start.5) | collective-permute-done | bytes 557088 | tf_op jit(solution)/shard_map/ppermute | solution.py:253
  35.8 3.6 %collective-permute-start.7 = (bf16[128,2176]{1,0:T(8,128)(2,1)S(1)}, bf16[128,2176]{1,0:T(8,128)(2,1)S(1)}, u32[]{:S(2)}, u32[]{:S(2)}) collective-permute-start(bf16[128,2176]{1,0:T(8,128)(2,1)S(1)} %get-tuple-element.48.inner), channel_id=1, source_target_pairs={{4,0},{5,1},{6,2},{7,3},{8,12},{9,13},{10,14},{11,15},{20,16},{21,... | collective-permute-start | bytes 1671176 | tf_op jit(solution)/shard_map/ppermute | solution.py:253
  39.4 1.6 %collective-permute-start.8 = (bf16[128,2176]{1,0:T(8,128)(2,1)S(1)}, bf16[128,2176]{1,0:T(8,128)(2,1)S(1)}, u32[]{:S(2)}, u32[]{:S(2)}) collective-permute-start(bf16[128,2176]{1,0:T(8,128)(2,1)S(1)} %get-tuple-element.49.refs_0_), channel_id=1, source_target_pairs={{0,2},{1,3},{2,0},{3,1},{4,6},{5,7},{6,4},{7,5},{8,10},{9,11},{10,... | collective-permute-start | bytes 1671176 | tf_op jit(solution)/shard_map/ppermute | solution.py:256
  41.0 2.5 %shard_map.79 = (bf16[1,768,2048]{2,1,0:T(8,128)(2,1)S(1)}, f32[8,128]{1,0:T(8,128)}) custom-call(bf16[1,768,2048]{2,1,0:T(8,128)(2,1)} %collective-permute-done.9.refs_0_), custom_call_target="tpu_custom_call" | custom-call | flops 1 | bytes 1 | tf_op jit(solution)/shard_map/pallas_call | solution.py:103
  43.5 5.9 %shard_map.80 = (bf16[128,2048]{1,0:T(8,128)(2,1)S(1)}, bf16[128,2048]{1,0:T(8,128)(2,1)S(1)}) custom-call(bf16[128,2176]{1,0:T(8,128)(2,1)S(1)} %copy-done, bf16[128,2176]{1,0:T(8,128)(2,1)S(1)} %get-tuple-element.50.refs_1_, bf16[1,2048,768]{2,1,0:T(8,128)(2,1)S(1)} %get-tuple-element.51.refs_2_, bf16[1,2048,768]{2,1,0:T(8,128)(2,1)S(1)} %get-tuple-element.52.refs_3_, ...), custom_call_target="tpu_custom_call" | custom-call | flops 1 | bytes 1 | tf_op jit(solution)/shard_map/pallas_call | solution.py:205
  49.7 2.5 %collective-permute-done.8.refs_1_ = bf16[128,2176]{1,0:T(8,128)(2,1)S(1)} collective-permute-done((bf16[128,2176]{1,0:T(8,128)(2,1)S(1)}, bf16[128,2176]{1,0:T(8,128)(2,1)S(1)}, u32[]{:S(2)}, u32[]{:S(2)}) %collective-permute-start.8) | collective-permute-done | bytes 557088 | tf_op jit(solution)/shard_map/ppermute | solution.py:256
  52.2 1.6 %collective-permute-start.10 = (bf16[128,2176]{1,0:T(8,128)(2,1)S(1)}, bf16[128,2176]{1,0:T(8,128)(2,1)S(1)}, u32[]{:S(2)}, u32[]{:S(2)}) collective-permute-start(bf16[128,2176]{1,0:T(8,128)(2,1)S(1)} %shard_map.82.refs_0_), channel_id=1, source_target_pairs={{0,2},{1,3},{2,0},{3,1},{4,6},{5,7},{6,4},{7,5},{8,10},{9,11},{10,... | collective-permute-start | bytes 1671176 | tf_op jit(solution)/shard_map/ppermute | solution.py:256
  53.8 5.8 %shard_map.84 = (bf16[128,2048]{1,0:T(8,128)(2,1)S(1)}, bf16[128,2048]{1,0:T(8,128)(2,1)S(1)}) custom-call(bf16[128,2176]{1,0:T(8,128)(2,1)S(1)} %get-tuple-element.44.inner.refs_0_, bf16[128,2176]{1,0:T(8,128)(2,1)S(1)} %get-tuple-element.61.refs_1_, bf16[1,2048,768]{2,1,0:T(8,128)(2,1)S(1)} %get-tuple-element.51.refs_2_, ...), custom_call_target="tpu_custom_call" | custom-call | flops 1 | bytes 1 | tf_op jit(solution)/shard_map/pallas_call | solution.py:205
  59.7 1.3 %collective-permute-start.12 = (bf16[128,2048]{1,0:T(8,128)(2,1)S(1)}, bf16[128,2048]{1,0:T(8,128)(2,1)S(1)}, u32[]{:S(2)}, u32[]{:S(2)}) collective-permute-start(bf16[128,2048]{1,0:T(8,128)(2,1)S(1)} %get-tuple-element.62.refs_2_), channel_id=1, source_target_pairs={{0,4},{1,5},{2,6},{3,7},{4,12},{5,13},{6,14},{7,15},{8,0},{9,1},{1... | collective-permute-start | bytes 1572872 | tf_op jit(solution)/shard_map/ppermute | solution.py:253
  60.9 5.8 %shard_map.83 = (bf16[128,2048]{1,0:T(8,128)(2,1)S(1)}, bf16[128,2048]{1,0:T(8,128)(2,1)S(1)}) custom-call(bf16[128,2176]{1,0:T(8,128)(2,1)S(1)} %get-tuple-element.49.refs_0_, bf16[128,2176]{1,0:T(8,128)(2,1)S(1)} %get-tuple-element.59.refs_1_, bf16[1,2048,768]{2,1,0:T(8,128)(2,1)S(1)} %get-tuple-element.51.refs_2_, ...), custom_call_target="tpu_custom_call" | custom-call | flops 1 | bytes 1 | tf_op jit(solution)/shard_map/pallas_call | solution.py:205
  66.8 0.6 collective-permute-start.11
  67.4 6.6 %shard_map.86 = (bf16[128,2048]{1,0:T(8,128)(2,1)S(1)}, bf16[128,2048]{1,0:T(8,128)(2,1)}) custom-call(bf16[128,2176]{1,0:T(8,128)(2,1)S(1)} %shard_map.82.refs_0_, bf16[128,2176]{1,0:T(8,128)(2,1)S(1)} %get-tuple-element.64.refs_1_, bf16[1,2048,768]{2,1,0:T(8,128)(2,1)S(1)} %get-tuple-element.51.refs_2_, ...), custom_call_target="tpu_custom_call" | custom-call | flops 1 | bytes 1 | tf_op jit(solution)/shard_map/pallas_call | solution.py:205
  74.1 3.8 %collective-permute-done.11.refs_0_ = bf16[128,2048]{1,0:T(8,128)(2,1)S(1)} collective-permute-done((bf16[128,2048]{1,0:T(8,128)(2,1)S(1)}, bf16[128,2048]{1,0:T(8,128)(2,1)S(1)}, u32[]{:S(2)}, u32[]{:S(2)}) %collective-permute-start.11) | collective-permute-done | bytes 524320 | tf_op jit(solution)/shard_map/ppermute | solution.py:256
  77.8 0.9 add_convert_fusion.6
  79.6 8.7 %collective-permute-done.14.refs_1_ = bf16[128,2048]{1,0:T(8,128)(2,1)S(1)} collective-permute-done((bf16[128,2048]{1,0:T(8,128)(2,1)}, bf16[128,2048]{1,0:T(8,128)(2,1)S(1)}, u32[]{:S(2)}, u32[]{:S(2)}) %collective-permute-start.14) | collective-permute-done | bytes 524320 | tf_op jit(solution)/shard_map/ppermute | solution.py:253
  89.0 3.5 %collective-permute-start.17 = (bf16[128,2048]{1,0:T(8,128)(2,1)S(1)}, bf16[128,2048]{1,0:T(8,128)(2,1)S(1)}, u32[]{:S(2)}, u32[]{:S(2)}) collective-permute-start(bf16[128,2048]{1,0:T(8,128)(2,1)S(1)} %get-tuple-element.82), channel_id=1, source_target_pairs={{4,12},{5,13},{6,14},{7,15},{8,0},{9,1},{10,2},{11,3},{20,28},{21,... | collective-permute-start | bytes 1572872 | tf_op jit(solution)/shard_map/ppermute | solution.py:253
  92.7 1.3 %collective-permute-start.16 = (bf16[128,2048]{1,0:T(8,128)(2,1)S(1)}, bf16[128,2048]{1,0:T(8,128)(2,1)S(1)}, u32[]{:S(2)}, u32[]{:S(2)}) collective-permute-start(bf16[128,2048]{1,0:T(8,128)(2,1)S(1)} %add_convert_fusion.4), channel_id=1, source_target_pairs={{0,4},{1,5},{2,6},{3,7},{12,8},{13,9},{14,10},{15,11},{16,20},{17,... | collective-permute-start | bytes 1572872 | tf_op jit(solution)/shard_map/ppermute | solution.py:253
  94.5 4.6 %collective-permute-done.17.refs_2_ = bf16[128,2048]{1,0:T(8,128)(2,1)S(1)} collective-permute-done((bf16[128,2048]{1,0:T(8,128)(2,1)S(1)}, bf16[128,2048]{1,0:T(8,128)(2,1)S(1)}, u32[]{:S(2)}, u32[]{:S(2)}) %collective-permute-start.17) | collective-permute-done | bytes 524320 | tf_op jit(solution)/shard_map/ppermute | solution.py:253
  99.2 4.6 %collective-permute-done.16.refs_1_ = bf16[128,2048]{1,0:T(8,128)(2,1)S(1)} collective-permute-done((bf16[128,2048]{1,0:T(8,128)(2,1)S(1)}, bf16[128,2048]{1,0:T(8,128)(2,1)S(1)}, u32[]{:S(2)}, u32[]{:S(2)}) %collective-permute-start.16) | collective-permute-done | bytes 524320 | tf_op jit(solution)/shard_map/ppermute | solution.py:253
  103.9 3.3 %collective-permute-start.19 = (bf16[128,2048]{1,0:T(8,128)(2,1)S(1)}, bf16[128,2048]{1,0:T(8,128)(2,1)S(1)}, u32[]{:S(2)}, u32[]{:S(2)}) collective-permute-start(bf16[128,2048]{1,0:T(8,128)(2,1)S(1)} %add_convert_fusion.1), channel_id=1, source_target_pairs={{4,8},{5,9},{6,10},{7,11},{8,4},{9,5},{10,6},{11,7},{20,24},{21,25... | collective-permute-start | bytes 1572872 | tf_op jit(solution)/shard_map/ppermute | solution.py:253
  107.1 1.3 %collective-permute-start.18 = (bf16[128,2048]{1,0:T(8,128)(2,1)S(1)}, bf16[128,2048]{1,0:T(8,128)(2,1)S(1)}, u32[]{:S(2)}, u32[]{:S(2)}) collective-permute-start(bf16[128,2048]{1,0:T(8,128)(2,1)S(1)} %get-tuple-element.79), channel_id=1, source_target_pairs={{0,4},{1,5},{2,6},{3,7},{12,8},{13,9},{14,10},{15,11},{16,20},{17,... | collective-permute-start | bytes 1572872 | tf_op jit(solution)/shard_map/ppermute | solution.py:253
  108.4 6.5 %collective-permute-done.19 = bf16[128,2048]{1,0:T(8,128)(2,1)S(1)} collective-permute-done((bf16[128,2048]{1,0:T(8,128)(2,1)S(1)}, bf16[128,2048]{1,0:T(8,128)(2,1)S(1)}, u32[]{:S(2)}, u32[]{:S(2)}) %collective-permute-start.19) | collective-permute-done | bytes 524320 | tf_op jit(solution)/shard_map/ppermute | solution.py:253
  115.0 3.3 %collective-permute-done.18 = bf16[128,2048]{1,0:T(8,128)(2,1)S(1)} collective-permute-done((bf16[128,2048]{1,0:T(8,128)(2,1)S(1)}, bf16[128,2048]{1,0:T(8,128)(2,1)S(1)}, u32[]{:S(2)}, u32[]{:S(2)}) %collective-permute-start.18) | collective-permute-done | bytes 524320 | tf_op jit(solution)/shard_map/ppermute | solution.py:253
  118.2 1.2 %add_convert_fusion = bf16[128,2048]{1,0:T(8,128)(2,1)} fusion(bf16[128,2048]{1,0:T(8,128)(2,1)S(1)} %collective-permute-done.19, bf16[128,2048]{1,0:T(8,128)(2,1)S(1)} %collective-permute-done.18, bf16[128,2048]{1,0:T(8,128)(2,1)S(1)} %get-tuple-element.78, bf16[128,2048]{1,0:T(8,128)(2,1)S(1)} %get-tuple-element.77, bf16[128,2048]{1,0:T(8,128)(2,1)S(1)} %get-tuple-element.76), kind=kLoop, calls=%fused_computation | loop fusion | flops 2621440 | bytes 3145728 | tf_op jit(solution)/shard_map/convert_element_type | solution.py:262
  (37 shorter events, 4.0 us)
Async XLA Ops:
  0.0 21.6 %collective-permute-start.2 = (bf16[1,2048,768]{2,1,0:T(8,128)(2,1)}, bf16[1,2048,768]{2,1,0:T(8,128)(2,1)}, u32[]{:S(2)}, u32[]{:S(2)}) collective-permute-start(bf16[1,2048,768]{2,1,0:T(8,128)(2,1)} %refs_0_.3), channel_id=1, source_target_pairs={{0,1},{1,0},{2,3},{3,2},{4,5},{5,4},{6,7},{7,6},{8,9},{9,8},{10,11... | collective-permute-start | bytes 9437192 | tf_op jit(solution)/shard_map/ppermute | solution.py:259
  0.0 21.6 %collective-permute-start.3 = (bf16[1,2048,768]{2,1,0:T(8,128)(2,1)}, bf16[1,2048,768]{2,1,0:T(8,128)(2,1)}, u32[]{:S(2)}, u32[]{:S(2)}) collective-permute-start(bf16[1,2048,768]{2,1,0:T(8,128)(2,1)} %refs_1_.1), channel_id=1, source_target_pairs={{0,1},{1,0},{2,3},{3,2},{4,5},{5,4},{6,7},{7,6},{8,9},{9,8},{10,11... | collective-permute-start | bytes 9437192 | tf_op jit(solution)/shard_map/ppermute | solution.py:259
  0.5 40.5 %collective-permute-start.9 = (bf16[1,768,2048]{2,1,0:T(8,128)(2,1)}, bf16[1,768,2048]{2,1,0:T(8,128)(2,1)}, u32[]{:S(2)}, u32[]{:S(2)}) collective-permute-start(bf16[1,768,2048]{2,1,0:T(8,128)(2,1)} %refs_2_.1), channel_id=1, source_target_pairs={{0,1},{1,0},{2,3},{3,2},{4,5},{5,4},{6,7},{7,6},{8,9},{9,8},{10,11... | collective-permute-start | bytes 9437192 | tf_op jit(solution)/shard_map/ppermute | solution.py:259
  3.0 16.2 %copy-start = (bf16[128,2176]{1,0:T(8,128)(2,1)S(1)}, bf16[128,2176]{1,0:T(8,128)(2,1)}, u32[]{:S(2)}) copy-start(bf16[128,2176]{1,0:T(8,128)(2,1)} %shard_map.73.outer.refs_0_) | copy-start | bytes 1671172
  3.0 16.2 %collective-permute-start = (bf16[128,2176]{1,0:T(8,128)(2,1)}, bf16[128,2176]{1,0:T(8,128)(2,1)S(1)}, u32[]{:S(2)}, u32[]{:S(2)}) collective-permute-start(bf16[128,2176]{1,0:T(8,128)(2,1)} %shard_map.73.outer.refs_0_), channel_id=1, source_target_pairs={{0,8},{1,9},{2,10},{3,11},{4,0},{5,1},{6,2},{7,3},{8,12},{9,13},{1... | collective-permute-start | bytes 1671176 | tf_op jit(solution)/shard_map/ppermute | solution.py:253
  4.6 16.9 %collective-permute-start.1 = (bf16[128,2176]{1,0:T(8,128)(2,1)}, bf16[128,2176]{1,0:T(8,128)(2,1)S(1)}, u32[]{:S(2)}, u32[]{:S(2)}) collective-permute-start(bf16[128,2176]{1,0:T(8,128)(2,1)} %shard_map.73.outer.refs_0_), channel_id=1, source_target_pairs={{0,2},{1,3},{2,0},{3,1},{4,6},{5,7},{6,4},{7,5},{8,10},{9,11},{10,... | collective-permute-start | bytes 1671176 | tf_op jit(solution)/shard_map/ppermute | solution.py:256
  19.2 16.1 %collective-permute-start.5 = (bf16[128,2176]{1,0:T(8,128)(2,1)S(1)}, bf16[128,2176]{1,0:T(8,128)(2,1)S(1)}, u32[]{:S(2)}, u32[]{:S(2)}) collective-permute-start(bf16[128,2176]{1,0:T(8,128)(2,1)S(1)} %copy-done), channel_id=1, source_target_pairs={{4,8},{5,9},{6,10},{7,11},{8,4},{9,5},{10,6},{11,7},{20,24},{21,25... | collective-permute-start | bytes 1671176 | tf_op jit(solution)/shard_map/ppermute | solution.py:253
  21.7 14.0 %collective-permute-start.4 = (bf16[128,2176]{1,0:T(8,128)(2,1)S(1)}, bf16[128,2176]{1,0:T(8,128)(2,1)S(1)}, u32[]{:S(2)}, u32[]{:S(2)}) collective-permute-start(bf16[128,2176]{1,0:T(8,128)(2,1)S(1)} %shard_map.76), channel_id=1, source_target_pairs={{0,4},{1,5},{2,6},{3,7},{4,0},{5,1},{6,2},{7,3},{8,12},{9,13},{10,... | collective-permute-start | bytes 1671176 | tf_op jit(solution)/shard_map/ppermute | solution.py:253
  21.8 14.0 %collective-permute-start.6 = (bf16[128,2176]{1,0:T(8,128)(2,1)S(1)}, bf16[128,2176]{1,0:T(8,128)(2,1)S(1)}, u32[]{:S(2)}, u32[]{:S(2)}) collective-permute-start(bf16[128,2176]{1,0:T(8,128)(2,1)S(1)} %get-tuple-element.44.inner.refs_0_), channel_id=1, source_target_pairs={{0,2},{1,3},{2,0},{3,1},{4,6},{5,7},{6,4},{7,5},{8,10},{9,11},{10,... | collective-permute-start | bytes 1671176 | tf_op jit(solution)/shard_map/ppermute | solution.py:256
  35.8 13.8 %collective-permute-start.7 = (bf16[128,2176]{1,0:T(8,128)(2,1)S(1)}, bf16[128,2176]{1,0:T(8,128)(2,1)S(1)}, u32[]{:S(2)}, u32[]{:S(2)}) collective-permute-start(bf16[128,2176]{1,0:T(8,128)(2,1)S(1)} %get-tuple-element.48.inner), channel_id=1, source_target_pairs={{4,0},{5,1},{6,2},{7,3},{8,12},{9,13},{10,14},{11,15},{20,16},{21,... | collective-permute-start | bytes 1671176 | tf_op jit(solution)/shard_map/ppermute | solution.py:253
  39.4 12.7 %collective-permute-start.8 = (bf16[128,2176]{1,0:T(8,128)(2,1)S(1)}, bf16[128,2176]{1,0:T(8,128)(2,1)S(1)}, u32[]{:S(2)}, u32[]{:S(2)}) collective-permute-start(bf16[128,2176]{1,0:T(8,128)(2,1)S(1)} %get-tuple-element.49.refs_0_), channel_id=1, source_target_pairs={{0,2},{1,3},{2,0},{3,1},{4,6},{5,7},{6,4},{7,5},{8,10},{9,11},{10,... | collective-permute-start | bytes 1671176 | tf_op jit(solution)/shard_map/ppermute | solution.py:256
  49.4 10.3 %copy-start.1 = (bf16[128,2048]{1,0:T(8,128)(2,1)}, bf16[128,2048]{1,0:T(8,128)(2,1)S(1)}, u32[]{:S(2)}) copy-start(bf16[128,2048]{1,0:T(8,128)(2,1)S(1)} %get-tuple-element.75) | copy-start | bytes 1572868
  52.2 14.6 %collective-permute-start.10 = (bf16[128,2176]{1,0:T(8,128)(2,1)S(1)}, bf16[128,2176]{1,0:T(8,128)(2,1)S(1)}, u32[]{:S(2)}, u32[]{:S(2)}) collective-permute-start(bf16[128,2176]{1,0:T(8,128)(2,1)S(1)} %shard_map.82.refs_0_), channel_id=1, source_target_pairs={{0,2},{1,3},{2,0},{3,1},{4,6},{5,7},{6,4},{7,5},{8,10},{9,11},{10,... | collective-permute-start | bytes 1671176 | tf_op jit(solution)/shard_map/ppermute | solution.py:256
  59.7 14.4 %collective-permute-start.12 = (bf16[128,2048]{1,0:T(8,128)(2,1)S(1)}, bf16[128,2048]{1,0:T(8,128)(2,1)S(1)}, u32[]{:S(2)}, u32[]{:S(2)}) collective-permute-start(bf16[128,2048]{1,0:T(8,128)(2,1)S(1)} %get-tuple-element.62.refs_2_), channel_id=1, source_target_pairs={{0,4},{1,5},{2,6},{3,7},{4,12},{5,13},{6,14},{7,15},{8,0},{9,1},{1... | collective-permute-start | bytes 1572872 | tf_op jit(solution)/shard_map/ppermute | solution.py:253
  66.8 11.0 %collective-permute-start.11 = (bf16[128,2048]{1,0:T(8,128)(2,1)S(1)}, bf16[128,2048]{1,0:T(8,128)(2,1)S(1)}, u32[]{:S(2)}, u32[]{:S(2)}) collective-permute-start(bf16[128,2048]{1,0:T(8,128)(2,1)S(1)} %get-tuple-element.63), channel_id=1, source_target_pairs={{0,2},{1,3},{2,0},{3,1},{4,6},{5,7},{6,4},{7,5},{8,10},{9,11},{10,... | collective-permute-start | bytes 1572872 | tf_op jit(solution)/shard_map/ppermute | solution.py:256
  78.8 9.5 %collective-permute-start.14 = (bf16[128,2048]{1,0:T(8,128)(2,1)}, bf16[128,2048]{1,0:T(8,128)(2,1)S(1)}, u32[]{:S(2)}, u32[]{:S(2)}) collective-permute-start(bf16[128,2048]{1,0:T(8,128)(2,1)} %add_convert_fusion.6), channel_id=1, source_target_pairs={{0,4},{1,5},{2,6},{3,7},{4,0},{5,1},{6,2},{7,3},{8,12},{9,13},{10,... | collective-permute-start | bytes 1572872 | tf_op jit(solution)/shard_map/ppermute | solution.py:253
  79.0 9.7 %collective-permute-start.13 = (bf16[128,2048]{1,0:T(8,128)(2,1)}, bf16[128,2048]{1,0:T(8,128)(2,1)S(1)}, u32[]{:S(2)}, u32[]{:S(2)}) collective-permute-start(bf16[128,2048]{1,0:T(8,128)(2,1)} %get-tuple-element.66), channel_id=1, source_target_pairs={{0,2},{1,3},{2,0},{3,1},{4,6},{5,7},{6,4},{7,5},{8,10},{9,11},{10,... | collective-permute-start | bytes 1572872 | tf_op jit(solution)/shard_map/ppermute | solution.py:256
  79.5 9.2 %copy-start.2 = (bf16[128,2048]{1,0:T(8,128)(2,1)S(1)}, bf16[128,2048]{1,0:T(8,128)(2,1)}, u32[]{:S(2)}) copy-start(bf16[128,2048]{1,0:T(8,128)(2,1)} %copy-done.1) | copy-start | bytes 1572868
  89.0 10.2 %collective-permute-start.17 = (bf16[128,2048]{1,0:T(8,128)(2,1)S(1)}, bf16[128,2048]{1,0:T(8,128)(2,1)S(1)}, u32[]{:S(2)}, u32[]{:S(2)}) collective-permute-start(bf16[128,2048]{1,0:T(8,128)(2,1)S(1)} %get-tuple-element.82), channel_id=1, source_target_pairs={{4,12},{5,13},{6,14},{7,15},{8,0},{9,1},{10,2},{11,3},{20,28},{21,... | collective-permute-start | bytes 1572872 | tf_op jit(solution)/shard_map/ppermute | solution.py:253
  92.7 11.1 %collective-permute-start.16 = (bf16[128,2048]{1,0:T(8,128)(2,1)S(1)}, bf16[128,2048]{1,0:T(8,128)(2,1)S(1)}, u32[]{:S(2)}, u32[]{:S(2)}) collective-permute-start(bf16[128,2048]{1,0:T(8,128)(2,1)S(1)} %add_convert_fusion.4), channel_id=1, source_target_pairs={{0,4},{1,5},{2,6},{3,7},{12,8},{13,9},{14,10},{15,11},{16,20},{17,... | collective-permute-start | bytes 1572872 | tf_op jit(solution)/shard_map/ppermute | solution.py:253
  94.0 9.8 %collective-permute-start.15 = (bf16[128,2048]{1,0:T(8,128)(2,1)S(1)}, bf16[128,2048]{1,0:T(8,128)(2,1)S(1)}, u32[]{:S(2)}, u32[]{:S(2)}) collective-permute-start(bf16[128,2048]{1,0:T(8,128)(2,1)S(1)} %get-tuple-element.70), channel_id=1, source_target_pairs={{0,2},{1,3},{2,0},{3,1},{4,6},{5,7},{6,4},{7,5},{8,10},{9,11},{10,... | collective-permute-start | bytes 1572872 | tf_op jit(solution)/shard_map/ppermute | solution.py:256
  103.9 11.1 %collective-permute-start.19 = (bf16[128,2048]{1,0:T(8,128)(2,1)S(1)}, bf16[128,2048]{1,0:T(8,128)(2,1)S(1)}, u32[]{:S(2)}, u32[]{:S(2)}) collective-permute-start(bf16[128,2048]{1,0:T(8,128)(2,1)S(1)} %add_convert_fusion.1), channel_id=1, source_target_pairs={{4,8},{5,9},{6,10},{7,11},{8,4},{9,5},{10,6},{11,7},{20,24},{21,25... | collective-permute-start | bytes 1572872 | tf_op jit(solution)/shard_map/ppermute | solution.py:253
  107.1 11.1 %collective-permute-start.18 = (bf16[128,2048]{1,0:T(8,128)(2,1)S(1)}, bf16[128,2048]{1,0:T(8,128)(2,1)S(1)}, u32[]{:S(2)}, u32[]{:S(2)}) collective-permute-start(bf16[128,2048]{1,0:T(8,128)(2,1)S(1)} %get-tuple-element.79), channel_id=1, source_target_pairs={{0,4},{1,5},{2,6},{3,7},{12,8},{13,9},{14,10},{15,11},{16,20},{17,... | collective-permute-start | bytes 1572872 | tf_op jit(solution)/shard_map/ppermute | solution.py:253

commit v5 on v4

--- a/solution.py
+++ b/solution.py
@@ -275,28 +275,26 @@
 
     b, n, ya = line(choose(a, own), pairs), line(own, middle), cross(a)
     far_down = other_core(w_down)
-    held, token = hold(far_gate, far_up)
+    held, token = hold(far_gate, far_up, far_down)
     weights += held
     b, n, ya = gate([b, n, ya], [token])
 
     c, yb = line(n, outward), cross(b)
-    held, token = hold(far_down)
-    weights += held
     m0, o0 = run_experts([own, y0], weights)
-    c, yb = gate([c, yb], [o0])
+    ma, oa = run_experts([a, ya], weights)
+    c, yb = gate([c, yb], [o0, oa])
 
     c = choose(n, c)
     yc = cross(c)
-    ma, oa = run_experts([a, ya], weights)
     mb, ob = run_experts([b, yb], weights)
-    yc, ob = gate([yc, ob], [oa])
+    yc, ob, oa = gate([yc, ob, oa], [])
 
     place = lax.axis_index("ep") // 4
     is_inner = (place == 1) | (place == 2)
 
     yob, xo = cross(ob), line(oa, back)
     mc, oc = run_experts([c, yc], weights)
-    yob, xo, oc = gate([yob, xo, oc], [])
+    yob, oc = gate([yob, oc], [])
 
     yoc, p = cross(oc), line(add(mb, yob), pairs)
     o0 = add(o0, xo)

time: 120 us -> 121 us (level); the launches traced: 119 us -> 119 us
  Pallas kernels: 36 us -> 34.6 us
    ppermute x7, waiting for transfers between devices: 6.74 us -> 8.92 us  [cross(): return lax.ppermute(x, 'ep', [(i, i ^ 2) for i in range(count)])]
    ppermute x10, waiting for transfers between devices: 46.7 us -> 44.8 us  [line(): return lax.ppermute(x, 'ep', moves)]
    pallas_call x3 -> x2, Pallas kernels: 9.13 us -> 7.56 us  [hold(): pl.pallas_call(functools.partial(hold_kernel, count), in_specs=[pl.BlockS...]
  transfers between devices with their start and end apart: 20 -> 20, of which waited for: 13 -> 12; matrix products, arithmetic and copies ran while one was open for 0% -> 2% of each run, Pallas kernels for 30% -> 29%
where the time goes in v5:
time: 121 us; the launch traced here: 119 us
  waiting for transfers between devices  53.7 us (44%)
  Pallas kernels  34.6 us (29%)
  starting transfers between devices  26.1 us (22%)
  other arithmetic  3.97 us (3%)
    ppermute x10, waiting for transfers between devices, line(): return lax.ppermute(x, 'ep', moves)  44.8 us
    pallas_call x4, Pallas kernels, run_experts(): pl.pallas_call(functools.partial(experts_kernel, count, ff // 3), in_spec...  24.2 us
    ppermute x10, starting transfers between devices, line(): return lax.ppermute(x, 'ep', moves)  18.2 us
    ppermute x7, waiting for transfers between devices, cross(): return lax.ppermute(x, 'ep', [(i, i ^ 2) for i in range(count)])  8.92 us
    pallas_call x2, Pallas kernels, hold(): pl.pallas_call(functools.partial(hold_kernel, count), in_specs=[pl.BlockS...  7.56 us
    ppermute x7, starting transfers between devices, cross(): return lax.ppermute(x, 'ep', [(i, i ^ 2) for i in range(count)])  7.41 us
    convert_element_type x6, other arithmetic, add(): return sum((p.astype(f32) for p in parts)).astype(bf16)  3.97 us
    pallas_call x1, Pallas kernels, prepare(): pl.pallas_call(prepare_kernel, in_specs=[pl.BlockSpec(memory_space=pltpu....  2.46 us
  transfers between devices with their start and end apart: 20, of which 12 were waited for; matrix products, arithmetic and copies ran while one was open for 2% of the time, Pallas kernels for 29%

profile of v5, /device:TPU:18, one launch (start us, length us, event | category | flops | bytes accessed | tf_op | source)
XLA Modules:
  0.0 118.7 jit_solution(16592768813712584196)
XLA Ops:
  0.5 2.5 %shard_map.73.outer.refs_0_ = bf16[128,2176]{1,0:T(8,128)(2,1)} custom-call(bf16[128,2048]{1,0:T(8,128)(2,1)} %refs_0_.2, f32[1,2048]{1,0:T(1,128)} %bitcast.3, s32[8,128]{1,0:T(8,128)} %bitcast.4, f32[8,128]{1,0:T(8,128)} %bitcast.5), custom_call_target="tpu_custom_call" | custom-call | tf_op jit(solution)/shard_map/pallas_call | solution.py:80
  3.0 1.6 %collective-permute-start = (bf16[128,2176]{1,0:T(8,128)(2,1)}, bf16[128,2176]{1,0:T(8,128)(2,1)S(1)}, u32[]{:S(2)}, u32[]{:S(2)}) collective-permute-start(bf16[128,2176]{1,0:T(8,128)(2,1)} %shard_map.73.outer.refs_0_), channel_id=1, source_target_pairs={{0,8},{1,9},{2,10},{3,11},{4,0},{5,1},{6,2},{7,3},{8,12},{9,13},{1... | collective-permute-start | bytes 1671176 | tf_op jit(solution)/shard_map/ppermute | solution.py:253
  4.6 1.5 %collective-permute-start.1 = (bf16[128,2176]{1,0:T(8,128)(2,1)}, bf16[128,2176]{1,0:T(8,128)(2,1)S(1)}, u32[]{:S(2)}, u32[]{:S(2)}) collective-permute-start(bf16[128,2176]{1,0:T(8,128)(2,1)} %shard_map.73.outer.refs_0_), channel_id=1, source_target_pairs={{0,2},{1,3},{2,0},{3,1},{4,6},{5,7},{6,4},{7,5},{8,10},{9,11},{10,... | collective-permute-start | bytes 1671176 | tf_op jit(solution)/shard_map/ppermute | solution.py:256
  6.1 3.8 %shard_map.74 = (bf16[1,2048,768]{2,1,0:T(8,128)(2,1)S(1)}, bf16[1,2048,768]{2,1,0:T(8,128)(2,1)S(1)}, bf16[1,768,2048]{2,1,0:T(8,128)(2,1)S(1)}, f32[8,128]{1,0:T(8,128)S(1)}) custom-call(bf16[1,2048,768]{2,1,0:T(8,128)(2,1)} %refs_0_.3, bf16[1,2048,768]{2,1,0:T(8,128)(2,1)} %refs_1_.1, bf16[1,768,2048]{2,1,0:T(8,128)(2,1)} %refs_2_.1), custom_call_target="tpu_custom_call" | custom-call | flops 1 | bytes 1 | tf_op jit(solution)/shard_map/pallas_call | solution.py:103
  9.9 9.3 %collective-permute-done.refs_0_ = bf16[128,2176]{1,0:T(8,128)(2,1)S(1)} collective-permute-done((bf16[128,2176]{1,0:T(8,128)(2,1)}, bf16[128,2176]{1,0:T(8,128)(2,1)S(1)}, u32[]{:S(2)}, u32[]{:S(2)}) %collective-permute-start) | collective-permute-done | bytes 557088 | tf_op jit(solution)/shard_map/ppermute | solution.py:253
  19.2 2.3 %collective-permute-start.5 = (bf16[128,2176]{1,0:T(8,128)(2,1)S(1)}, bf16[128,2176]{1,0:T(8,128)(2,1)S(1)}, u32[]{:S(2)}, u32[]{:S(2)}) collective-permute-start(bf16[128,2176]{1,0:T(8,128)(2,1)S(1)} %copy-done), channel_id=1, source_target_pairs={{4,8},{5,9},{6,10},{7,11},{8,4},{9,5},{10,6},{11,7},{20,24},{21,25... | collective-permute-start | bytes 1671176 | tf_op jit(solution)/shard_map/ppermute | solution.py:253
  21.8 1.6 %collective-permute-start.6 = (bf16[128,2176]{1,0:T(8,128)(2,1)S(1)}, bf16[128,2176]{1,0:T(8,128)(2,1)S(1)}, u32[]{:S(2)}, u32[]{:S(2)}) collective-permute-start(bf16[128,2176]{1,0:T(8,128)(2,1)S(1)} %get-tuple-element.44.inner.refs_0_), channel_id=1, source_target_pairs={{0,2},{1,3},{2,0},{3,1},{4,6},{5,7},{6,4},{7,5},{8,10},{9,11},{10,... | collective-permute-start | bytes 1671176 | tf_op jit(solution)/shard_map/ppermute | solution.py:256
  23.4 3.8 %shard_map.77 = (bf16[1,2048,768]{2,1,0:T(8,128)(2,1)S(1)}, bf16[1,2048,768]{2,1,0:T(8,128)(2,1)S(1)}, bf16[1,768,2048]{2,1,0:T(8,128)(2,1)S(1)}, f32[8,128]{1,0:T(8,128)S(1)}) custom-call(bf16[1,2048,768]{2,1,0:T(8,128)(2,1)} %get-tuple-element.45.refs_0_, bf16[1,2048,768]{2,1,0:T(8,128)(2,1)} %get-tuple-element.46.refs_1_, ...), custom_call_target="tpu_custom_call" | custom-call | flops 1 | bytes 1 | tf_op jit(solution)/shard_map/pallas_call | solution.py:103
  27.2 8.2 %collective-permute-done.5.refs_1_ = bf16[128,2176]{1,0:T(8,128)(2,1)S(1)} collective-permute-done((bf16[128,2176]{1,0:T(8,128)(2,1)S(1)}, bf16[128,2176]{1,0:T(8,128)(2,1)S(1)}, u32[]{:S(2)}, u32[]{:S(2)}) %collective-permute-start.5) | collective-permute-done | bytes 557088 | tf_op jit(solution)/shard_map/ppermute | solution.py:253
  35.8 3.6 %collective-permute-start.8 = (bf16[128,2176]{1,0:T(8,128)(2,1)S(1)}, bf16[128,2176]{1,0:T(8,128)(2,1)S(1)}, u32[]{:S(2)}, u32[]{:S(2)}) collective-permute-start(bf16[128,2176]{1,0:T(8,128)(2,1)S(1)} %get-tuple-element.48.inner), channel_id=1, source_target_pairs={{4,0},{5,1},{6,2},{7,3},{8,12},{9,13},{10,14},{11,15},{20,16},{21,... | collective-permute-start | bytes 1671176 | tf_op jit(solution)/shard_map/ppermute | solution.py:253
  39.4 1.6 %collective-permute-start.9 = (bf16[128,2176]{1,0:T(8,128)(2,1)S(1)}, bf16[128,2176]{1,0:T(8,128)(2,1)S(1)}, u32[]{:S(2)}, u32[]{:S(2)}) collective-permute-start(bf16[128,2176]{1,0:T(8,128)(2,1)S(1)} %get-tuple-element.49.refs_0_), channel_id=1, source_target_pairs={{0,2},{1,3},{2,0},{3,1},{4,6},{5,7},{6,4},{7,5},{8,10},{9,11},{10,... | collective-permute-start | bytes 1671176 | tf_op jit(solution)/shard_map/ppermute | solution.py:256
  41.0 5.8 %shard_map.79 = (bf16[128,2048]{1,0:T(8,128)(2,1)S(1)}, bf16[128,2048]{1,0:T(8,128)(2,1)S(1)}) custom-call(bf16[128,2176]{1,0:T(8,128)(2,1)S(1)} %copy-done, bf16[128,2176]{1,0:T(8,128)(2,1)S(1)} %get-tuple-element.50.refs_1_, bf16[1,2048,768]{2,1,0:T(8,128)(2,1)S(1)} %get-tuple-element.51.refs_2_, bf16[1,2048,768]{2,1,0:T(8,128)(2,1)S(1)} %get-tuple-element.52.refs_3_, ...), custom_call_target="tpu_custom_call" | custom-call | flops 1 | bytes 1 | tf_op jit(solution)/shard_map/pallas_call | solution.py:205
  46.9 5.9 %shard_map.80 = (bf16[128,2048]{1,0:T(8,128)(2,1)S(1)}, bf16[128,2048]{1,0:T(8,128)(2,1)S(1)}) custom-call(bf16[128,2176]{1,0:T(8,128)(2,1)S(1)} %get-tuple-element.44.inner.refs_0_, bf16[128,2176]{1,0:T(8,128)(2,1)S(1)} %get-tuple-element.58.refs_1_, bf16[1,2048,768]{2,1,0:T(8,128)(2,1)S(1)} %get-tuple-element.51.refs_2_, ...), custom_call_target="tpu_custom_call" | custom-call | flops 1 | bytes 1 | tf_op jit(solution)/shard_map/pallas_call | solution.py:205
  53.1 0.8 collective-permute-start.10
  53.9 5.8 %shard_map.83 = (bf16[128,2048]{1,0:T(8,128)(2,1)S(1)}, bf16[128,2048]{1,0:T(8,128)(2,1)S(1)}) custom-call(bf16[128,2176]{1,0:T(8,128)(2,1)S(1)} %get-tuple-element.49.refs_0_, bf16[128,2176]{1,0:T(8,128)(2,1)S(1)} %get-tuple-element.61.refs_1_, bf16[1,2048,768]{2,1,0:T(8,128)(2,1)S(1)} %get-tuple-element.51.refs_2_, ...), custom_call_target="tpu_custom_call" | custom-call | flops 1 | bytes 1 | tf_op jit(solution)/shard_map/pallas_call | solution.py:205
  59.7 6.2 %collective-permute-done.10.refs_0_ = bf16[128,2176]{1,0:T(8,128)(2,1)S(1)} collective-permute-done((bf16[128,2176]{1,0:T(8,128)(2,1)S(1)}, bf16[128,2176]{1,0:T(8,128)(2,1)S(1)}, u32[]{:S(2)}, u32[]{:S(2)}) %collective-permute-start.10) | collective-permute-done | bytes 557088 | tf_op jit(solution)/shard_map/ppermute | solution.py:256
  65.9 0.7 collective-permute-start.11
  66.6 1.1 collective-permute-start.14
  67.8 6.6 %shard_map.85 = (bf16[128,2048]{1,0:T(8,128)(2,1)S(1)}, bf16[128,2048]{1,0:T(8,128)(2,1)}) custom-call(bf16[128,2176]{1,0:T(8,128)(2,1)S(1)} %shard_map.82.refs_0_, bf16[128,2176]{1,0:T(8,128)(2,1)S(1)} %get-tuple-element.64.refs_1_, bf16[1,2048,768]{2,1,0:T(8,128)(2,1)S(1)} %get-tuple-element.51.refs_2_, ...), custom_call_target="tpu_custom_call" | custom-call | flops 1 | bytes 1 | tf_op jit(solution)/shard_map/pallas_call | solution.py:205
  74.4 2.4 %collective-permute-done.11.refs_0_ = bf16[128,2048]{1,0:T(8,128)(2,1)S(1)} collective-permute-done((bf16[128,2048]{1,0:T(8,128)(2,1)S(1)}, bf16[128,2048]{1,0:T(8,128)(2,1)S(1)}, u32[]{:S(2)}, u32[]{:S(2)}) %collective-permute-start.11) | collective-permute-done | bytes 524320 | tf_op jit(solution)/shard_map/ppermute | solution.py:256
  76.8 0.9 add_convert_fusion.6
  78.4 1.2 %add_convert_fusion.5.refs_2_ = bf16[128,2048]{1,0:T(8,128)(2,1)S(1)} fusion(bf16[128,2048]{1,0:T(8,128)(2,1)} %collective-permute-done.14, bf16[128,2048]{1,0:T(8,128)(2,1)S(1)} %get-tuple-element.57.refs_2_), kind=kLoop, calls=%fused_computation.5 | loop fusion | flops 1048576 | bytes 1572864 | tf_op jit(solution)/shard_map/convert_element_type | solution.py:262
  79.7 7.9 %collective-permute-done.13.refs_1_ = bf16[128,2048]{1,0:T(8,128)(2,1)S(1)} collective-permute-done((bf16[128,2048]{1,0:T(8,128)(2,1)}, bf16[128,2048]{1,0:T(8,128)(2,1)S(1)}, u32[]{:S(2)}, u32[]{:S(2)}) %collective-permute-start.13) | collective-permute-done | bytes 524320 | tf_op jit(solution)/shard_map/ppermute | solution.py:253
  88.1 4.5 %collective-permute-start.17 = (bf16[128,2048]{1,0:T(8,128)(2,1)S(1)}, bf16[128,2048]{1,0:T(8,128)(2,1)S(1)}, u32[]{:S(2)}, u32[]{:S(2)}) collective-permute-start(bf16[128,2048]{1,0:T(8,128)(2,1)S(1)} %get-tuple-element.82), channel_id=1, source_target_pairs={{4,12},{5,13},{6,14},{7,15},{8,0},{9,1},{10,2},{11,3},{20,28},{21,... | collective-permute-start | bytes 1572872 | tf_op jit(solution)/shard_map/ppermute | solution.py:253
  92.7 1.3 %collective-permute-start.16 = (bf16[128,2048]{1,0:T(8,128)(2,1)S(1)}, bf16[128,2048]{1,0:T(8,128)(2,1)S(1)}, u32[]{:S(2)}, u32[]{:S(2)}) collective-permute-start(bf16[128,2048]{1,0:T(8,128)(2,1)S(1)} %add_convert_fusion.4), channel_id=1, source_target_pairs={{0,4},{1,5},{2,6},{3,7},{12,8},{13,9},{14,10},{15,11},{16,20},{17,... | collective-permute-start | bytes 1572872 | tf_op jit(solution)/shard_map/ppermute | solution.py:253
  94.6 4.7 %collective-permute-done.17.refs_2_ = bf16[128,2048]{1,0:T(8,128)(2,1)S(1)} collective-permute-done((bf16[128,2048]{1,0:T(8,128)(2,1)S(1)}, bf16[128,2048]{1,0:T(8,128)(2,1)S(1)}, u32[]{:S(2)}, u32[]{:S(2)}) %collective-permute-start.17) | collective-permute-done | bytes 524320 | tf_op jit(solution)/shard_map/ppermute | solution.py:253
  99.2 4.6 %collective-permute-done.16.refs_1_ = bf16[128,2048]{1,0:T(8,128)(2,1)S(1)} collective-permute-done((bf16[128,2048]{1,0:T(8,128)(2,1)S(1)}, bf16[128,2048]{1,0:T(8,128)(2,1)S(1)}, u32[]{:S(2)}, u32[]{:S(2)}) %collective-permute-start.16) | collective-permute-done | bytes 524320 | tf_op jit(solution)/shard_map/ppermute | solution.py:253
  103.9 2.4 %collective-permute-start.19 = (bf16[128,2048]{1,0:T(8,128)(2,1)S(1)}, bf16[128,2048]{1,0:T(8,128)(2,1)S(1)}, u32[]{:S(2)}, u32[]{:S(2)}) collective-permute-start(bf16[128,2048]{1,0:T(8,128)(2,1)S(1)} %add_convert_fusion.1), channel_id=1, source_target_pairs={{4,8},{5,9},{6,10},{7,11},{8,4},{9,5},{10,6},{11,7},{20,24},{21,25... | collective-permute-start | bytes 1572872 | tf_op jit(solution)/shard_map/ppermute | solution.py:253
  106.3 1.3 %collective-permute-start.18 = (bf16[128,2048]{1,0:T(8,128)(2,1)S(1)}, bf16[128,2048]{1,0:T(8,128)(2,1)S(1)}, u32[]{:S(2)}, u32[]{:S(2)}) collective-permute-start(bf16[128,2048]{1,0:T(8,128)(2,1)S(1)} %get-tuple-element.79), channel_id=1, source_target_pairs={{0,4},{1,5},{2,6},{3,7},{12,8},{13,9},{14,10},{15,11},{16,20},{17,... | collective-permute-start | bytes 1572872 | tf_op jit(solution)/shard_map/ppermute | solution.py:253
  107.6 7.4 %collective-permute-done.19 = bf16[128,2048]{1,0:T(8,128)(2,1)S(1)} collective-permute-done((bf16[128,2048]{1,0:T(8,128)(2,1)S(1)}, bf16[128,2048]{1,0:T(8,128)(2,1)S(1)}, u32[]{:S(2)}, u32[]{:S(2)}) %collective-permute-start.19) | collective-permute-done | bytes 524320 | tf_op jit(solution)/shard_map/ppermute | solution.py:253
  115.0 2.4 %collective-permute-done.18 = bf16[128,2048]{1,0:T(8,128)(2,1)S(1)} collective-permute-done((bf16[128,2048]{1,0:T(8,128)(2,1)S(1)}, bf16[128,2048]{1,0:T(8,128)(2,1)S(1)}, u32[]{:S(2)}, u32[]{:S(2)}) %collective-permute-start.18) | collective-permute-done | bytes 524320 | tf_op jit(solution)/shard_map/ppermute | solution.py:253
  117.4 1.3 %add_convert_fusion = bf16[128,2048]{1,0:T(8,128)(2,1)} fusion(bf16[128,2048]{1,0:T(8,128)(2,1)S(1)} %collective-permute-done.19, bf16[128,2048]{1,0:T(8,128)(2,1)S(1)} %collective-permute-done.18, bf16[128,2048]{1,0:T(8,128)(2,1)S(1)} %get-tuple-element.78, bf16[128,2048]{1,0:T(8,128)(2,1)S(1)} %get-tuple-element.77, bf16[128,2048]{1,0:T(8,128)(2,1)S(1)} %get-tuple-element.76), kind=kLoop, calls=%fused_computation | loop fusion | flops 2621440 | bytes 3145728 | tf_op jit(solution)/shard_map/convert_element_type | solution.py:262
  (36 shorter events, 3.5 us)
Async XLA Ops:
  0.0 21.6 %collective-permute-start.2 = (bf16[1,2048,768]{2,1,0:T(8,128)(2,1)}, bf16[1,2048,768]{2,1,0:T(8,128)(2,1)}, u32[]{:S(2)}, u32[]{:S(2)}) collective-permute-start(bf16[1,2048,768]{2,1,0:T(8,128)(2,1)} %refs_0_.3), channel_id=1, source_target_pairs={{0,1},{1,0},{2,3},{3,2},{4,5},{5,4},{6,7},{7,6},{8,9},{9,8},{10,11... | collective-permute-start | bytes 9437192 | tf_op jit(solution)/shard_map/ppermute | solution.py:259
  0.0 21.6 %collective-permute-start.3 = (bf16[1,2048,768]{2,1,0:T(8,128)(2,1)}, bf16[1,2048,768]{2,1,0:T(8,128)(2,1)}, u32[]{:S(2)}, u32[]{:S(2)}) collective-permute-start(bf16[1,2048,768]{2,1,0:T(8,128)(2,1)} %refs_1_.1), channel_id=1, source_target_pairs={{0,1},{1,0},{2,3},{3,2},{4,5},{5,4},{6,7},{7,6},{8,9},{9,8},{10,11... | collective-permute-start | bytes 9437192 | tf_op jit(solution)/shard_map/ppermute | solution.py:259
  0.5 22.9 %collective-permute-start.7 = (bf16[1,768,2048]{2,1,0:T(8,128)(2,1)}, bf16[1,768,2048]{2,1,0:T(8,128)(2,1)}, u32[]{:S(2)}, u32[]{:S(2)}) collective-permute-start(bf16[1,768,2048]{2,1,0:T(8,128)(2,1)} %refs_2_.1), channel_id=1, source_target_pairs={{0,1},{1,0},{2,3},{3,2},{4,5},{5,4},{6,7},{7,6},{8,9},{9,8},{10,11... | collective-permute-start | bytes 9437192 | tf_op jit(solution)/shard_map/ppermute | solution.py:259
  3.0 16.2 %copy-start = (bf16[128,2176]{1,0:T(8,128)(2,1)S(1)}, bf16[128,2176]{1,0:T(8,128)(2,1)}, u32[]{:S(2)}) copy-start(bf16[128,2176]{1,0:T(8,128)(2,1)} %shard_map.73.outer.refs_0_) | copy-start | bytes 1671172
  3.0 16.2 %collective-permute-start = (bf16[128,2176]{1,0:T(8,128)(2,1)}, bf16[128,2176]{1,0:T(8,128)(2,1)S(1)}, u32[]{:S(2)}, u32[]{:S(2)}) collective-permute-start(bf16[128,2176]{1,0:T(8,128)(2,1)} %shard_map.73.outer.refs_0_), channel_id=1, source_target_pairs={{0,8},{1,9},{2,10},{3,11},{4,0},{5,1},{6,2},{7,3},{8,12},{9,13},{1... | collective-permute-start | bytes 1671176 | tf_op jit(solution)/shard_map/ppermute | solution.py:253
  4.6 16.9 %collective-permute-start.1 = (bf16[128,2176]{1,0:T(8,128)(2,1)}, bf16[128,2176]{1,0:T(8,128)(2,1)S(1)}, u32[]{:S(2)}, u32[]{:S(2)}) collective-permute-start(bf16[128,2176]{1,0:T(8,128)(2,1)} %shard_map.73.outer.refs_0_), channel_id=1, source_target_pairs={{0,2},{1,3},{2,0},{3,1},{4,6},{5,7},{6,4},{7,5},{8,10},{9,11},{10,... | collective-permute-start | bytes 1671176 | tf_op jit(solution)/shard_map/ppermute | solution.py:256
  19.2 16.1 %collective-permute-start.5 = (bf16[128,2176]{1,0:T(8,128)(2,1)S(1)}, bf16[128,2176]{1,0:T(8,128)(2,1)S(1)}, u32[]{:S(2)}, u32[]{:S(2)}) collective-permute-start(bf16[128,2176]{1,0:T(8,128)(2,1)S(1)} %copy-done), channel_id=1, source_target_pairs={{4,8},{5,9},{6,10},{7,11},{8,4},{9,5},{10,6},{11,7},{20,24},{21,25... | collective-permute-start | bytes 1671176 | tf_op jit(solution)/shard_map/ppermute | solution.py:253
  21.7 14.0 %collective-permute-start.4 = (bf16[128,2176]{1,0:T(8,128)(2,1)S(1)}, bf16[128,2176]{1,0:T(8,128)(2,1)S(1)}, u32[]{:S(2)}, u32[]{:S(2)}) collective-permute-start(bf16[128,2176]{1,0:T(8,128)(2,1)S(1)} %shard_map.76), channel_id=1, source_target_pairs={{0,4},{1,5},{2,6},{3,7},{4,0},{5,1},{6,2},{7,3},{8,12},{9,13},{10,... | collective-permute-start | bytes 1671176 | tf_op jit(solution)/shard_map/ppermute | solution.py:253
  21.8 14.0 %collective-permute-start.6 = (bf16[128,2176]{1,0:T(8,128)(2,1)S(1)}, bf16[128,2176]{1,0:T(8,128)(2,1)S(1)}, u32[]{:S(2)}, u32[]{:S(2)}) collective-permute-start(bf16[128,2176]{1,0:T(8,128)(2,1)S(1)} %get-tuple-element.44.inner.refs_0_), channel_id=1, source_target_pairs={{0,2},{1,3},{2,0},{3,1},{4,6},{5,7},{6,4},{7,5},{8,10},{9,11},{10,... | collective-permute-start | bytes 1671176 | tf_op jit(solution)/shard_map/ppermute | solution.py:256
  35.8 16.9 %collective-permute-start.8 = (bf16[128,2176]{1,0:T(8,128)(2,1)S(1)}, bf16[128,2176]{1,0:T(8,128)(2,1)S(1)}, u32[]{:S(2)}, u32[]{:S(2)}) collective-permute-start(bf16[128,2176]{1,0:T(8,128)(2,1)S(1)} %get-tuple-element.48.inner), channel_id=1, source_target_pairs={{4,0},{5,1},{6,2},{7,3},{8,12},{9,13},{10,14},{11,15},{20,16},{21,... | collective-permute-start | bytes 1671176 | tf_op jit(solution)/shard_map/ppermute | solution.py:253
  39.4 13.3 %collective-permute-start.9 = (bf16[128,2176]{1,0:T(8,128)(2,1)S(1)}, bf16[128,2176]{1,0:T(8,128)(2,1)S(1)}, u32[]{:S(2)}, u32[]{:S(2)}) collective-permute-start(bf16[128,2176]{1,0:T(8,128)(2,1)S(1)} %get-tuple-element.49.refs_0_), channel_id=1, source_target_pairs={{0,2},{1,3},{2,0},{3,1},{4,6},{5,7},{6,4},{7,5},{8,10},{9,11},{10,... | collective-permute-start | bytes 1671176 | tf_op jit(solution)/shard_map/ppermute | solution.py:256
  46.9 5.9 %copy-start.1 = (bf16[128,2048]{1,0:T(8,128)(2,1)}, bf16[128,2048]{1,0:T(8,128)(2,1)S(1)}, u32[]{:S(2)}) copy-start(bf16[128,2048]{1,0:T(8,128)(2,1)S(1)} %get-tuple-element.75) | copy-start | bytes 1572868
  53.1 12.9 %collective-permute-start.10 = (bf16[128,2176]{1,0:T(8,128)(2,1)S(1)}, bf16[128,2176]{1,0:T(8,128)(2,1)S(1)}, u32[]{:S(2)}, u32[]{:S(2)}) collective-permute-start(bf16[128,2176]{1,0:T(8,128)(2,1)S(1)} %shard_map.82.refs_0_), channel_id=1, source_target_pairs={{0,2},{1,3},{2,0},{3,1},{4,6},{5,7},{6,4},{7,5},{8,10},{9,11},{10,... | collective-permute-start | bytes 1671176 | tf_op jit(solution)/shard_map/ppermute | solution.py:256
  65.9 10.8 %collective-permute-start.11 = (bf16[128,2048]{1,0:T(8,128)(2,1)S(1)}, bf16[128,2048]{1,0:T(8,128)(2,1)S(1)}, u32[]{:S(2)}, u32[]{:S(2)}) collective-permute-start(bf16[128,2048]{1,0:T(8,128)(2,1)S(1)} %get-tuple-element.63), channel_id=1, source_target_pairs={{0,2},{1,3},{2,0},{3,1},{4,6},{5,7},{6,4},{7,5},{8,10},{9,11},{10,... | collective-permute-start | bytes 1572872 | tf_op jit(solution)/shard_map/ppermute | solution.py:256
  66.6 11.8 %collective-permute-start.14 = (bf16[128,2048]{1,0:T(8,128)(2,1)S(1)}, bf16[128,2048]{1,0:T(8,128)(2,1)}, u32[]{:S(2)}, u32[]{:S(2)}) collective-permute-start(bf16[128,2048]{1,0:T(8,128)(2,1)S(1)} %get-tuple-element.69), channel_id=1, source_target_pairs={{0,4},{1,5},{2,6},{3,7},{4,12},{5,13},{6,14},{7,15},{8,0},{9,1},{1... | collective-permute-start | bytes 1572872 | tf_op jit(solution)/shard_map/ppermute | solution.py:253
  77.7 9.9 %collective-permute-start.13 = (bf16[128,2048]{1,0:T(8,128)(2,1)}, bf16[128,2048]{1,0:T(8,128)(2,1)S(1)}, u32[]{:S(2)}, u32[]{:S(2)}) collective-permute-start(bf16[128,2048]{1,0:T(8,128)(2,1)} %add_convert_fusion.6), channel_id=1, source_target_pairs={{0,4},{1,5},{2,6},{3,7},{4,0},{5,1},{6,2},{7,3},{8,12},{9,13},{10,... | collective-permute-start | bytes 1572872 | tf_op jit(solution)/shard_map/ppermute | solution.py:253
  77.7 10.1 %collective-permute-start.12 = (bf16[128,2048]{1,0:T(8,128)(2,1)}, bf16[128,2048]{1,0:T(8,128)(2,1)S(1)}, u32[]{:S(2)}, u32[]{:S(2)}) collective-permute-start(bf16[128,2048]{1,0:T(8,128)(2,1)} %get-tuple-element.66), channel_id=1, source_target_pairs={{0,2},{1,3},{2,0},{3,1},{4,6},{5,7},{6,4},{7,5},{8,10},{9,11},{10,... | collective-permute-start | bytes 1572872 | tf_op jit(solution)/shard_map/ppermute | solution.py:256
  78.4 9.4 %copy-start.2 = (bf16[128,2048]{1,0:T(8,128)(2,1)S(1)}, bf16[128,2048]{1,0:T(8,128)(2,1)}, u32[]{:S(2)}) copy-start(bf16[128,2048]{1,0:T(8,128)(2,1)} %copy-done.1) | copy-start | bytes 1572868
  88.1 11.1 %collective-permute-start.17 = (bf16[128,2048]{1,0:T(8,128)(2,1)S(1)}, bf16[128,2048]{1,0:T(8,128)(2,1)S(1)}, u32[]{:S(2)}, u32[]{:S(2)}) collective-permute-start(bf16[128,2048]{1,0:T(8,128)(2,1)S(1)} %get-tuple-element.82), channel_id=1, source_target_pairs={{4,12},{5,13},{6,14},{7,15},{8,0},{9,1},{10,2},{11,3},{20,28},{21,... | collective-permute-start | bytes 1572872 | tf_op jit(solution)/shard_map/ppermute | solution.py:253
  92.7 11.1 %collective-permute-start.16 = (bf16[128,2048]{1,0:T(8,128)(2,1)S(1)}, bf16[128,2048]{1,0:T(8,128)(2,1)S(1)}, u32[]{:S(2)}, u32[]{:S(2)}) collective-permute-start(bf16[128,2048]{1,0:T(8,128)(2,1)S(1)} %add_convert_fusion.4), channel_id=1, source_target_pairs={{0,4},{1,5},{2,6},{3,7},{12,8},{13,9},{14,10},{15,11},{16,20},{17,... | collective-permute-start | bytes 1572872 | tf_op jit(solution)/shard_map/ppermute | solution.py:253
  94.0 9.8 %collective-permute-start.15 = (bf16[128,2048]{1,0:T(8,128)(2,1)S(1)}, bf16[128,2048]{1,0:T(8,128)(2,1)S(1)}, u32[]{:S(2)}, u32[]{:S(2)}) collective-permute-start(bf16[128,2048]{1,0:T(8,128)(2,1)S(1)} %get-tuple-element.70), channel_id=1, source_target_pairs={{0,2},{1,3},{2,0},{3,1},{4,6},{5,7},{6,4},{7,5},{8,10},{9,11},{10,... | collective-permute-start | bytes 1572872 | tf_op jit(solution)/shard_map/ppermute | solution.py:256
  103.9 11.1 %collective-permute-start.19 = (bf16[128,2048]{1,0:T(8,128)(2,1)S(1)}, bf16[128,2048]{1,0:T(8,128)(2,1)S(1)}, u32[]{:S(2)}, u32[]{:S(2)}) collective-permute-start(bf16[128,2048]{1,0:T(8,128)(2,1)S(1)} %add_convert_fusion.1), channel_id=1, source_target_pairs={{4,8},{5,9},{6,10},{7,11},{8,4},{9,5},{10,6},{11,7},{20,24},{21,25... | collective-permute-start | bytes 1572872 | tf_op jit(solution)/shard_map/ppermute | solution.py:253
  106.3 11.1 %collective-permute-start.18 = (bf16[128,2048]{1,0:T(8,128)(2,1)S(1)}, bf16[128,2048]{1,0:T(8,128)(2,1)S(1)}, u32[]{:S(2)}, u32[]{:S(2)}) collective-permute-start(bf16[128,2048]{1,0:T(8,128)(2,1)S(1)} %get-tuple-element.79), channel_id=1, source_target_pairs={{0,4},{1,5},{2,6},{3,7},{12,8},{13,9},{14,10},{15,11},{16,20},{17,... | collective-permute-start | bytes 1572872 | tf_op jit(solution)/shard_map/ppermute | solution.py:253
